TPU v7x, 256 devices: a whole 4x4x8 slice. The times are simulated.
256 devices in a mesh: dp: 32 (over z_lo, x, y), seq: 4 (over z_hi), fsdp: 2 (over core).
Axes of the slice: x: 4, y: 4, z: 8 (z_hi: 4, z_lo: 2; z = z_hi * 2 + z_lo), core: 2. Of those that a mesh axis runs over, the one named last changes fastest.
Arguments:
- layer_input: bfloat16 [64, 512, 5120], P(('dp', 'fsdp'), 'seq'), may hold values from -16 to 16
- query: bfloat16 [64, 512, 2560], P(('dp', 'fsdp'), 'seq'), may hold values from -24 to 24
- out_grad: bfloat16 [64, 512, 2560], P(('dp', 'fsdp'), 'seq'), may hold values from -6 to 6
- camera_counts: int32 [64, 1], P(('dp', 'fsdp')), may hold values from 1 to 3
- action_counts: int32 [64, 1], P(('dp', 'fsdp')), may hold values from 20 to 60
- kv_weight: bfloat16 [5120, 1024], P('fsdp'), may hold values from -0.078125 to 0.078125
Outputs:
- input_grad: bfloat16 [64, 512, 5120], P(('dp', 'fsdp'), 'seq')
- weight_grad: float32 [5120, 1024], P(('dp', 'fsdp'), 'seq')
All inputs are finite; a program needn't handle non-finite values.
Results may differ from a plain program's by a relative error of at most 0.011.
Values may be sent and summed in bfloat16 or wider, within the bound.
No kernel may reach another device: no remote copies, remote signals or barrier semaphores. Data moves between devices by JAX's collectives and lax.ppermute only.
A program may use at most 128 MiB of HBM per device.

v0:
```python
import jax
import jax.numpy as jnp
from jax import lax
from jax.sharding import PartitionSpec as P

HD = 128
IMG_TOK = 64
TEXT = 32


rope_base = 1000000.0
neg_fill = -1e30


def token_layout(cameras, actions, length):
    prefix_sizes = cameras * IMG_TOK + TEXT
    sample_sizes = prefix_sizes + actions
    sample_ends = jnp.cumsum(sample_sizes)
    sample_starts = sample_ends - sample_sizes
    places = jnp.arange(length, dtype=jnp.int32)
    segment = jnp.sum((places[:, None] >= sample_ends[None, :]).astype(jnp.int32), axis=1)
    firsts = jnp.concatenate([sample_starts, sample_ends])
    limits = jnp.concatenate([prefix_sizes, jnp.full((1,), length, jnp.int32)])
    labels = jnp.arange(firsts.shape[0], dtype=jnp.int32)
    onehot = segment[:, None] == labels[None, :]
    row_first = jnp.sum(jnp.where(onehot, firsts[None, :], 0), axis=1)
    bounds = jnp.sum(jnp.where(onehot, limits[None, :], 0), axis=1)
    return (segment, places - row_first, bounds)


def rope_tables(position):
    frequency = rope_base ** (-(2.0 * jnp.arange(HD // 2, dtype=jnp.float32)) / HD)
    angles = position.astype(jnp.float32)[:, None] * frequency[None, :]
    return (jnp.cos(angles), jnp.sin(angles))


def rotate(values_in, cos_table, sin_table):
    half_width = HD // 2
    lower_half = values_in[..., :half_width]
    upper_half = values_in[..., half_width:]
    cosines = cos_table[:, None, :]
    sine_part = sin_table[:, None, :]
    return jnp.concatenate(
        [
            lower_half * cosines - upper_half * sine_part,
            upper_half * cosines + lower_half * sine_part,
        ],
        axis=-1,
    )


def unrotate(values_in, cos_table, sin_table):
    half_width = HD // 2
    lower_half = values_in[..., :half_width]
    upper_half = values_in[..., half_width:]
    cosines = cos_table[:, None, :]
    sine_part = sin_table[:, None, :]
    return jnp.concatenate(
        [
            lower_half * cosines + upper_half * sine_part,
            upper_half * cosines - lower_half * sine_part,
        ],
        axis=-1,
    )


def attend_mask(query_segment, query_position, key_segment, key_position, key_bounds):
    same_sample = query_segment[:, None] == key_segment[None, :]
    visible = (key_position < key_bounds)[None, :] | (
        key_position[None, :] <= query_position[:, None]
    )
    return same_sample & visible


def project_keys(token_block, weight, cos_table, sin_table):
    row_count = token_block.shape[0]
    head_count = weight.shape[1] // (2 * HD)
    projected = jnp.dot(token_block, weight, preferred_element_type=jnp.float32).reshape(
        row_count, head_count, 2, HD
    )
    keys_rot = rotate(projected[:, :, 0], cos_table, sin_table)
    paired = jnp.stack([keys_rot, projected[:, :, 1]], axis=2).astype(jnp.bfloat16)
    return paired.reshape(row_count, head_count * 2 * HD)


def key_products(query_block, keys_all):
    return jnp.einsum("qhgd,khd->hgqk", query_block, keys_all, preferred_element_type=jnp.float32)


def back_products(weights_low, rows_block):
    return jnp.einsum("hgqk,qhgd->khd", weights_low, rows_block, preferred_element_type=jnp.float32)


def attention_grads(
    query_heads, grad_heads, kv_heads, segment, position, bounds, cos_table, sin_table, samples
):
    length = query_heads.shape[0]
    kv_local = kv_heads.shape[1] // (2 * HD)
    group_size = query_heads.shape[1] // (HD * kv_local)
    queries = query_heads.reshape(length, kv_local, group_size, HD)
    live_rows = (segment < samples)[:, None]
    grad_rows = jnp.where(live_rows, grad_heads, jnp.zeros_like(grad_heads)).reshape(
        length, kv_local, group_size, HD
    )
    paired = kv_heads.reshape(length, kv_local, 2, HD)
    keys_all = paired[:, :, 0]
    values_all = paired[:, :, 1]
    tile_span = length // 4
    score_scale = HD ** (-0.5)
    allowed = attend_mask(segment, position, segment, position, bounds)
    live_tiles = []
    for tile_index in range(4):
        tile_low = segment[tile_index * tile_span]
        tile_high = segment[(tile_index + 1) * tile_span - 1]
        live_tiles.append((tile_low <= segment[-1]) & (segment[0] <= tile_high))
    scores = key_products(queries, keys_all) * score_scale
    masked = jnp.where(allowed[None, None], scores, neg_fill)
    row_top = jnp.max(masked, axis=-1, keepdims=True)
    exponent = jnp.exp(masked - row_top)
    attention = exponent / jnp.sum(exponent, axis=-1, keepdims=True)
    grad_attention = key_products(grad_rows, values_all)
    row_delta = jnp.sum(attention * grad_attention, axis=-1, keepdims=True)
    grad_scores = (attention * (grad_attention - row_delta)).astype(jnp.bfloat16)
    attention_low = attention.astype(jnp.bfloat16)
    grad_values = back_products(attention_low, grad_rows)
    grad_keys = back_products(grad_scores, queries) * score_scale
    grad_keys = unrotate(grad_keys, cos_table, sin_table)
    stacked = jnp.stack([grad_keys, grad_values], axis=2).astype(jnp.bfloat16)
    return stacked.reshape(length, kv_local * 2 * HD)


def on_device(layer_input, query, out_grad, camera_counts, action_counts, kv_weight):
    tokens_here = layer_input.shape[1]
    seq_count = lax.axis_size("seq")
    length = tokens_here * seq_count
    row_total = lax.axis_size(("dp", "fsdp"))
    segment, position, bounds = token_layout(camera_counts[0], action_counts[0], length)
    cos_table, sin_table = rope_tables(position)
    weight = lax.all_gather(kv_weight, "fsdp", axis=0, tiled=True)
    heads_in = (
        lax.all_to_all(query[0], "seq", split_axis=1, concat_axis=0, tiled=True),
        lax.all_to_all(out_grad[0], "seq", split_axis=1, concat_axis=0, tiled=True),
    )
    offset = lax.axis_index("seq") * tokens_here
    cos_here = lax.dynamic_slice_in_dim(cos_table, offset, tokens_here, 0)
    sin_here = lax.dynamic_slice_in_dim(sin_table, offset, tokens_here, 0)
    kv_tokens = project_keys(layer_input[0], weight, cos_here, sin_here)
    kv_heads = lax.all_to_all(kv_tokens, "seq", split_axis=1, concat_axis=0, tiled=True)
    grads_heads = attention_grads(
        heads_in[0],
        heads_in[1],
        kv_heads,
        segment,
        position,
        bounds,
        cos_table,
        sin_table,
        camera_counts.shape[1],
    )
    grads_tokens = lax.all_to_all(grads_heads, "seq", split_axis=0, concat_axis=1, tiled=True)
    input_grad = lax.dot_general(
        grads_tokens, weight, (((1,), (1,)), ((), ())), preferred_element_type=jnp.float32
    ).astype(jnp.bfloat16)
    rows_part = layer_input[0]
    partial_rows = lax.psum_scatter(
        lax.dot_general(
            rows_part, grads_tokens, (((0,), (0,)), ((), ())), preferred_element_type=jnp.float32
        ),
        ("dp", "fsdp"),
        scatter_dimension=0,
        tiled=True,
    )
    summed = lax.psum_scatter(partial_rows, "seq", scatter_dimension=1, tiled=True)
    return (input_grad[None], summed / row_total)


def solution(mesh):
    placed = (
        P(("dp", "fsdp"), "seq", None),
        P(("dp", "fsdp"), "seq", None),
        P(("dp", "fsdp"), "seq", None),
        P(("dp", "fsdp"), None),
        P(("dp", "fsdp"), None),
        P("fsdp", None),
    )
    return jax.shard_map(
        on_device,
        mesh=mesh,
        in_specs=placed,
        out_specs=(P(("dp", "fsdp"), "seq", None), P(("dp", "fsdp"), "seq")),
        check_vma=False,
    )
```

profile of v0, /device:TPU:8, one launch (start us, length us, event | category | flops | bytes accessed | tf_op | source)
XLA Modules:
  0.0 501.4 jit_solution(9706812911983266527)
XLA Ops:
  7.2 0.0 all-gather.2.cloned.1.call-start
  7.2 0.7 all-gather.2.cloned.1.call-update
  7.9 0.4 copy-done.1
  8.4 1.1 copy.63
  9.4 8.5 %all-to-all-start.1 = ((bf16[128,4,640]{0,2,1:T(8,128)(2,1)}), bf16[128,4,640]{0,2,1:T(8,128)(2,1)S(1)}, u32[]{:S(2)}, u32[]{:S(2)}) async-start(bf16[128,4,640]{0,2,1:T(8,128)(2,1)} %bitcast.14), calls=%async_computation.1 | async-start | bytes 1310720 | tf_op jit(solution)/shard_map/all_to_all | solution.py:141
  19.2 0.1 concatenate.17
  19.3 1.1 copy.67
  20.4 0.1 pad_add_fusion
  20.5 0.1 select_reduce_fusion
  20.6 0.1 broadcast_multiply_fusion.1
  20.6 0.1 dynamic-slice_cosine_fusion
  20.8 0.3 or_and_fusion
  21.2 19.8 %all-gather.2.cloned.1.call-done = bf16[5120,1024]{1,0:T(8,128)(2,1)} async-done(((bf16[2560,1024]{1,0:T(8,128)(2,1)}), bf16[5120,1024]{1,0:T(8,128)(2,1)}) %all-gather.2.cloned.1.call-update) | async-done | bytes 10485776 | tf_op jit(solution)/shard_map/all_gather | solution.py:139
  41.0 13.8 %copy.59 = bf16[1024,5120]{1,0:T(8,128)(2,1)} copy(bf16[1024,5120]{0,1:T(8,128)(2,1)} %bitcast.161) | data formatting | bytes 20971520 | tf_op jit(solution)/shard_map/dot_general | solution.py:78
  54.8 7.0 %all-to-all-start.2 = ((bf16[128,4,640]{0,2,1:T(8,128)(2,1)}), bf16[128,4,640]{0,2,1:T(8,128)(2,1)S(1)}, u32[]{:S(2)}, u32[]{:S(2)}) async-start(bf16[128,4,640]{0,2,1:T(8,128)(2,1)} %bitcast.20), calls=%async_computation.2 | async-start | bytes 1310720 | tf_op jit(solution)/shard_map/all_to_all | solution.py:142
  61.8 5.6 %fusion.16 = f32[128,4,2,128]{0,3,2,1:T(8,128)S(1)} fusion(bf16[4,2,128,5120]{3,2,1,0:T(8,128)(2,1)} %bitcast.162, bf16[1,128,5120]{2,1,0:T(8,128)(2,1)S(1)} %copy-done), kind=kOutput, calls=%fused_computation.19 | convolution fusion | flops 1342177280 | bytes 12320768 | tf_op jit(solution)/shard_map/dot_general | solution.py:78
  67.6 0.9 copy.61
  68.4 11.9 %all-to-all-done.2 = bf16[128,4,640]{0,2,1:T(8,128)(2,1)S(1)} async-done(((bf16[128,4,640]{0,2,1:T(8,128)(2,1)}), bf16[128,4,640]{0,2,1:T(8,128)(2,1)S(1)}, u32[]{:S(2)}, u32[]{:S(2)}) %all-to-all-start.2) | async-done | bytes 655392 | tf_op jit(solution)/shard_map/all_to_all | solution.py:142
  80.3 4.1 all-to-all-start
  84.4 0.1 reduce-scatter.7.cloned.1.call-start
  84.6 0.5 copy.64
  85.1 0.2 reshape.330
  85.4 0.1 broadcast_select_fusion
  85.5 0.5 copy.68
  86.0 1.1 select_n.32
  87.1 0.5 copy.71
  87.6 1.1 all_to_all.56
  88.6 5.6 %all-to-all-done = bf16[128,4,256]{2,0,1:T(8,128)(2,1)} async-done(((bf16[128,4,256]{2,0,1:T(8,128)(2,1)}), bf16[128,4,256]{2,0,1:T(8,128)(2,1)}, u32[]{:S(2)}, u32[]{:S(2)}) %all-to-all-start) | async-done | bytes 262176 | tf_op jit(solution)/shard_map/all_to_all | solution.py:148
  94.2 1.0 reshape.328
  95.2 0.4 fusion.58
  95.6 1.1 fusion.6
  96.7 1.1 fusion.5
  97.8 1.8 fusion.1
  99.7 1.9 fusion.28
  101.6 0.6 fusion.45
  102.1 1.7 fusion.34
  103.9 0.1 convert_element_type.56
  104.0 14.3 %all_to_all.64 = bf16[4,128,256]{1,2,0:T(8,128)(2,1)S(1)} all-to-all(bf16[4,128,256]{1,2,0:T(8,128)(2,1)S(1)} %copy.73), channel_id=1, replica_groups=mesh['dp'=32,'seq'=4,'fsdp'=2] {'seq'}, dimensions={0} | all-to-all | bytes 524288 | tf_op jit(solution)/shard_map/all_to_all | solution.py:160
  118.2 8.5 %convolution_bitcast_fusion = f32[5120,1024]{0,1:T(8,128)} fusion(bf16[128,1024]{0,1:T(8,128)(2,1)S(1)} %bitcast.165, bf16[1,128,5120]{2,1,0:T(8,128)(2,1)S(1)} %copy-done), kind=kOutput, calls=%fused_computation | convolution fusion | flops 1342177280 | bytes 22544384 | tf_op jit(solution)/shard_map/dot_general | solution.py:166
  126.7 21.3 %copy.80 = f32[5120,1024]{1,0:T(8,128)} copy(f32[5120,1024]{0,1:T(8,128)} %convolution_bitcast_fusion) | data formatting | bytes 41943040
  148.1 0.0 reduce-scatter.7.cloned.1.call-update
  148.1 0.0 reduce-scatter.5.cloned.1.call-start
  148.2 311.7 %reduce-scatter.7.cloned.1.call-done = f32[80,1024]{1,0:T(8,128)} async-done(((f32[5120,1024]{1,0:T(8,128)}), f32[80,1024]{1,0:T(8,128)}) %reduce-scatter.7.cloned.1.call-update) | async-done | bytes 327696
  459.9 2.0 copy.81
  461.9 8.6 %fusion = bf16[1,128,5120]{2,1,0:T(8,128)(2,1)} fusion(bf16[128,1024]{0,1:T(8,128)(2,1)S(1)} %bitcast.166, bf16[5120,1024]{1,0:T(8,128)(2,1)} %all-gather.2.cloned.1.call-done), kind=kOutput, calls=%fused_computation.2 | convolution fusion | flops 1342832640 | bytes 12058624 | tf_op jit(solution)/shard_map/dot_general | solution.py:161
  470.5 22.7 %reduce-scatter.5.cloned.1.call-done = f32[80,256]{0,1:T(8,128)} async-done(((f32[80,1024]{0,1:T(8,128)}), f32[80,256]{0,1:T(8,128)}) %reduce-scatter.5.cloned.1.call-update) | async-done | bytes 81936 | tf_op jit(solution)/shard_map/reduce_scatter | solution.py:173
  493.2 0.9 broadcast_multiply_fusion
  494.1 0.7 copy.74
  (25 shorter events, 0.3 us)
Async XLA Ops:
  7.2 54.7 %copy-start = (bf16[1,128,5120]{2,1,0:T(8,128)(2,1)S(1)}, bf16[1,128,5120]{2,1,0:T(8,128)(2,1)}, u32[]{:S(2)}) copy-start(bf16[1,128,5120]{2,1,0:T(8,128)(2,1)} %param.6) | copy-start | bytes 3932164
  7.2 1.2 copy-start.1
  7.2 12.1 %copy-start.2 = (bf16[1,128,2560]{2,1,0:T(8,128)(2,1)S(1)}, bf16[1,128,2560]{2,1,0:T(8,128)(2,1)}, u32[]{:S(2)}) copy-start(bf16[1,128,2560]{2,1,0:T(8,128)(2,1)} %param.8) | copy-start | bytes 1966084
  7.2 33.8 %all-gather.2.cloned.1.call-start = ((), (), s32[]{:S(2)}) async-start(), calls=%async_computation.6 | async-start | bytes 15728640 | tf_op jit(solution)/shard_map/all_gather | solution.py:139
  9.4 45.4 %all-to-all-start.1 = ((bf16[128,4,640]{0,2,1:T(8,128)(2,1)}), bf16[128,4,640]{0,2,1:T(8,128)(2,1)S(1)}, u32[]{:S(2)}, u32[]{:S(2)}) async-start(bf16[128,4,640]{0,2,1:T(8,128)(2,1)} %bitcast.14), calls=%async_computation.1 | async-start | bytes 1310720 | tf_op jit(solution)/shard_map/all_to_all | solution.py:141
  54.8 25.5 %all-to-all-start.2 = ((bf16[128,4,640]{0,2,1:T(8,128)(2,1)}), bf16[128,4,640]{0,2,1:T(8,128)(2,1)S(1)}, u32[]{:S(2)}, u32[]{:S(2)}) async-start(bf16[128,4,640]{0,2,1:T(8,128)(2,1)} %bitcast.20), calls=%async_computation.2 | async-start | bytes 1310720 | tf_op jit(solution)/shard_map/all_to_all | solution.py:142
  80.3 13.9 %all-to-all-start = ((bf16[128,4,256]{2,0,1:T(8,128)(2,1)}), bf16[128,4,256]{2,0,1:T(8,128)(2,1)}, u32[]{:S(2)}, u32[]{:S(2)}) async-start(bf16[128,4,256]{2,0,1:T(8,128)(2,1)} %copy.61), calls=%async_computation | async-start | bytes 524288 | tf_op jit(solution)/shard_map/all_to_all | solution.py:148
  84.4 375.4 %reduce-scatter.7.cloned.1.call-start = ((), (), s32[]{:S(2)}) async-start(), calls=%async_computation.8 | async-start | bytes 21299200
  95.6 2.2 copy-start.4
  99.7 2.5 copy-start.3
  148.1 345.1 %reduce-scatter.5.cloned.1.call-start = ((), (), s32[]{:S(2)}) async-start(), calls=%async_computation.7 | async-start | bytes 655360 | tf_op jit(solution)/shard_map/reduce_scatter | solution.py:173
Sparse Core Ops, SparseCore 0:
  9.8 31.0 all-gather.1
  148.2 311.5 reduce-scatter.6
  462.4 30.7 reduce-scatter.4
where the time goes:
time: 502 us; the launch traced here: 501 us
  waiting for transfers between devices  372 us (74%)
  local copies, waits for them, and re-layouts  47 us (9%)
  matrix products  29.2 us (6%)
  starting transfers between devices  19.8 us (4%)
  between operations  15.3 us (3%)
  blocking collectives  14.3 us (3%)
    unnamed x4, waiting for transfers between devices  312 us
    unnamed x15, local copies, waits for them, and re-layouts  26.6 us
    reduce_scatter x1, waiting for transfers between devices, on_device(): lax.psum_scatter(partial_rows, 'seq', scatter_dimension=1, tiled=True)  22.7 us
    all_gather x1, waiting for transfers between devices, on_device(): weight = lax.all_gather(kv_weight, 'fsdp', axis=0, tiled=True)  19.8 us
    all_to_all x1, blocking collectives, on_device(): lax.all_to_all(grads_heads, 'seq', split_axis=0, concat_axis=1, tiled=True)  14.3 us
    dot_general x1, local copies, waits for them, and re-layouts, project_keys(): jnp.dot(token_block, weight, preferred_element_type=jnp.float32)  13.8 us
    all_to_all x1, waiting for transfers between devices, on_device(): lax.all_to_all(out_grad[0], 'seq', split_axis=1, concat_axis=0, tiled=True)  11.9 us
  transfers between devices with their start and end apart: 6, of which 5 were waited for; matrix products, arithmetic and copies ran while one was open for 7% of the time, Pallas kernels for 0%

commit v1 on v0

v1 whole, which is shorter than its diff:
```python
import functools

import jax
import jax.numpy as jnp
from jax import lax
from jax.experimental import pallas as pl
from jax.experimental.pallas import tpu as pltpu
from jax.sharding import PartitionSpec as P

HD = 128
GROUP = 5
KVH = 4
IMG_TOK = 64
TEXT = 32
TOK = 128
rope_base = 1000000.0
neg_fill = -1e30
far_away = 1 << 20
NC = 1
VMEM = pl.BlockSpec(memory_space=pltpu.VMEM)
SMEM = pl.BlockSpec(memory_space=pltpu.SMEM)
PARAMS = pltpu.CompilerParams(vmem_limit_bytes=48 * 1024 * 1024)
F32 = jnp.float32
BF16 = jnp.bfloat16
SWAP = ((0, 1), (1, 0))
AHEAD = ((0, 1), (1, 2))
CROSS = ((1, 0), (0, 2))


def reverse(perm):
    return tuple((b, a) for a, b in perm)


def dp_shift(dx=0, dy=0):
    pairs = []
    for d in range(32):
        z, x, y = d // 16, (d // 4) % 4, d % 4
        pairs.append((d, z * 16 + ((x + dx) % 4) * 4 + (y + dy) % 4))
    return pairs


def pair_perm(flip):
    pairs = []
    for d in range(32):
        zl, rest = d // 16, d % 16
        for c in range(2):
            pairs.append((d * 2 + c, (c * 16 + rest) * 2 + (zl ^ flip)))
    return pairs


def dot(a, b, ca, cb):
    return lax.dot_general(a, b, (((ca,), (cb,)), ((), ())), preferred_element_type=F32)


def swap_halves(block):
    half = HD // 2
    return jnp.concatenate([block[:, half:], block[:, :half]], axis=1)


def kv_kernel(own_ref, recv_ref, cos_ref, sin_ref, kv_ref):
    cos, sin = cos_ref[...], sin_ref[...]
    for h in range(kv_ref.shape[1] // (2 * HD)):
        at = h * 2 * HD
        k = own_ref[:, at : at + HD] + recv_ref[:, at : at + HD]
        v = own_ref[:, at + HD : at + 2 * HD] + recv_ref[:, at + HD : at + 2 * HD]
        kv_ref[:, at : at + HD] = (k * cos + swap_halves(k) * sin).astype(BF16)
        kv_ref[:, at + HD : at + 2 * HD] = v.astype(BF16)


def attention_kernel(meta, q_ref, g_ref, kv_ref, a_ref, b_ref, own_ref, sa_ref, sb_ref):
    place, prefix, total = meta[0], meta[1], meta[2]
    starts = (
        place * TOK,
        jnp.where((place == 1) | (place == 2), (place - 1) * TOK, far_away),
        jnp.where(place == 0, TOK, jnp.where(place == 2, 0, far_away)),
    )
    rows = lax.broadcasted_iota(jnp.int32, (TOK, TOK), 0)
    query_at = place * TOK + lax.broadcasted_iota(jnp.int32, (TOK, TOK), 1)
    bias = []
    for start in starts:
        key_at = start + rows
        allowed = (key_at < total) & ((key_at < prefix) | (key_at <= query_at))
        bias.append(jnp.where(allowed, 0.0, neg_fill))
    bias = jnp.concatenate(bias, axis=0)
    live = jnp.where(query_at[0:1] < total, 1.0, 0.0)
    bias = jnp.concatenate([bias] * GROUP, axis=1)
    live = jnp.concatenate([live] * GROUP, axis=1)
    scale = HD ** (-0.5)
    blocks = (kv_ref, a_ref, b_ref)
    for h in range(kv_ref.shape[1] // (2 * HD)):
        at = h * 2 * HD
        keys = jnp.concatenate([r[:, at : at + HD] for r in blocks], axis=0)
        values = jnp.concatenate([r[:, at + HD : at + 2 * HD] for r in blocks], axis=0)
        cols = [slice((h * GROUP + i) * HD, (h * GROUP + i + 1) * HD) for i in range(GROUP)]
        queries = jnp.concatenate([q_ref[:, c] for c in cols], axis=0)
        grads = jnp.concatenate([g_ref[:, c] for c in cols], axis=0)
        scores = dot(keys, queries, 1, 1) * scale + bias
        top = jnp.max(scores, axis=0, keepdims=True)
        exponent = jnp.exp(scores - top)
        inverse = live / jnp.sum(exponent, axis=0, keepdims=True)
        attention = exponent * inverse
        grad_attention = dot(values, grads, 1, 1)
        delta = jnp.sum(attention * grad_attention, axis=0, keepdims=True)
        grad_scores = (attention * (grad_attention - delta)).astype(BF16)
        grad_values = dot(attention.astype(BF16), grads, 1, 0)
        grad_keys = dot(grad_scores, queries, 1, 0) * scale
        for ref, lo in ((own_ref, 0), (sa_ref, TOK), (sb_ref, 2 * TOK)):
            ref[:, at : at + HD] = grad_keys[lo : lo + TOK].astype(ref.dtype)
            ref[:, at + HD : at + 2 * HD] = grad_values[lo : lo + TOK].astype(ref.dtype)


def kg_kernel(own_ref, a_ref, b_ref, cos_ref, sin_ref, kg_ref):
    cos, sin = cos_ref[...], sin_ref[...]
    for h in range(kg_ref.shape[1] // (2 * HD)):
        at = h * 2 * HD
        ks, vs = slice(at, at + HD), slice(at + HD, at + 2 * HD)
        k = own_ref[:, ks] + a_ref[:, ks].astype(F32) + b_ref[:, ks].astype(F32)
        v = own_ref[:, vs] + a_ref[:, vs].astype(F32) + b_ref[:, vs].astype(F32)
        kg_ref[:, ks] = (k * cos - swap_halves(k) * sin).astype(BF16)
        kg_ref[:, vs] = v.astype(BF16)


def weight_kernel(meta, *refs):
    x_refs, k_refs, outs, total = refs[:4], refs[4:12], refs[12:16], refs[16]
    y = meta[0]
    left = jnp.concatenate([r[...] for r in x_refs], axis=0)
    right = jnp.concatenate([r[...] for r in k_refs], axis=0)
    total[...] = dot(left, right, 0, 0)
    rows = total.shape[0] // 4
    for k, out in enumerate(outs):
        at = pl.multiple_of(lax.rem(y + k, 4) * rows, 16)
        out[...] = total[pl.ds(at, rows), :].astype(out.dtype)


def sum_kernel(meta, own_ref, a_ref, b_ref, c_ref, same_ref, flip_ref):
    zl = meta[1]
    rows = same_ref.shape[0]
    total = own_ref[...] + a_ref[...].astype(F32) + b_ref[...].astype(F32) + c_ref[...].astype(F32)
    lower, upper = total[:rows].astype(BF16), total[rows:].astype(BF16)
    same_ref[...] = jnp.where(zl == 0, lower, upper)
    flip_ref[...] = jnp.where(zl == 0, upper, lower)


def call(kernel, outs, *args, meta=False, scratch=(), specs=None):
    if specs is None:
        specs = [VMEM] * len(args)
        if meta:
            specs[0] = SMEM
    return pl.pallas_call(
        kernel,
        out_shape=outs,
        in_specs=specs,
        out_specs=jax.tree.map(lambda _: VMEM, outs),
        scratch_shapes=scratch,
        compiler_params=PARAMS,
    )(*args)


def shape(rows, cols, dtype):
    return jax.ShapeDtypeStruct((rows, cols), dtype)


def on_device(layer_input, query, out_grad, camera_counts, action_counts, kv_weight):
    seq, core, dp = lax.axis_index("seq"), lax.axis_index("fsdp"), lax.axis_index("dp")
    zl, x, y = dp // 16, (dp // 4) % 4, dp % 4
    tokens, queries, grads = layer_input[0], query[0], out_grad[0]
    half = kv_weight.shape[0]
    width = kv_weight.shape[1]
    cols = width // NC
    prefix = camera_counts[0, 0] * IMG_TOK + TEXT
    total = prefix + action_counts[0, 0]
    meta = jnp.stack([seq, prefix, total]).astype(jnp.int32)
    spot = jnp.stack([y, zl]).astype(jnp.int32)

    position = (seq * TOK + jnp.arange(TOK, dtype=jnp.int32)).astype(F32)
    frequency = rope_base ** (-(2.0 * jnp.arange(HD // 2, dtype=F32)) / HD)
    angles = position[:, None] * frequency[None, :]
    cos, sin = jnp.cos(angles), jnp.sin(angles)
    cos = jnp.concatenate([cos, cos], axis=1)
    sin = jnp.concatenate([-sin, sin], axis=1)

    mine = lax.dynamic_slice_in_dim(tokens, core * half, half, 1)
    other = lax.ppermute(lax.dynamic_slice_in_dim(tokens, (1 - core) * half, half, 1), "fsdp", SWAP)
    part_mine = dot(mine, kv_weight, 1, 0)
    part_other = dot(other, kv_weight, 1, 0)

    pieces = []
    span = half // 4
    for k in range(4):
        at = ((x + k) % 4) * span
        piece = jnp.concatenate(
            [lax.dynamic_slice_in_dim(mine, at, span, 1), lax.dynamic_slice_in_dim(other, at, span, 1)], axis=0
        )
        pieces.append(piece if k == 0 else lax.ppermute(piece, "dp", dp_shift(dx=k)))

    kv, ahead, cross = [], [], []
    for c in range(NC):
        at = slice(c * cols, (c + 1) * cols)
        back = lax.ppermute(part_other[:, at], "fsdp", SWAP)
        kv.append(call(kv_kernel, shape(TOK, cols, BF16), part_mine[:, at], back, cos, sin))
        ahead.append(lax.ppermute(kv[c], "seq", AHEAD))
        cross.append(lax.ppermute(kv[c], "seq", CROSS))

    sums = []
    key_grads = []
    for c in range(NC):
        qcols = queries.shape[1] // NC
        qs = slice(c * qcols, (c + 1) * qcols)
        own, to_a, to_b = call(
            attention_kernel,
            (shape(TOK, cols, F32), shape(TOK, cols, BF16), shape(TOK, cols, BF16)),
            meta, queries[:, qs], grads[:, qs], kv[c], ahead[c], cross[c],
            meta=True,
        )
        from_a = lax.ppermute(to_a, "seq", reverse(AHEAD))
        from_b = lax.ppermute(to_b, "seq", reverse(CROSS))
        kg = call(kg_kernel, shape(TOK, cols, BF16), own, from_a, from_b, cos, sin)
        gathered = [kg] + [lax.ppermute(kg, "dp", dp_shift(dx=k)) for k in (1, 2, 3)]
        swapped = [lax.ppermute(g, "fsdp", SWAP) for g in gathered]
        key_grads.append((kg, swapped[0]))
        both = [a for pair in zip(gathered, swapped) for a in pair]
        rows = span // 4
        parts = call(
            weight_kernel,
            (shape(rows, cols, F32),) + (shape(rows, cols, BF16),) * 3,
            spot, *pieces, *both,
            meta=True,
            scratch=[pltpu.VMEM((span, cols), F32)],
        )
        came = [lax.ppermute(parts[k], "dp", dp_shift(dy=k)) for k in (1, 2, 3)]
        same, flip = call(
            sum_kernel, (shape(rows // 2, cols, BF16),) * 2, spot, parts[0], *came, meta=True
        )
        same = lax.ppermute(same, ("dp", "fsdp"), pair_perm(0))
        flip = lax.ppermute(flip, ("dp", "fsdp"), pair_perm(1))
        sums.append(same.astype(F32) + flip.astype(F32))

    summed = jnp.concatenate(sums, axis=1)
    out_cols = width // 4
    out = lax.dynamic_slice_in_dim(summed, seq * out_cols, out_cols, 1)
    for k in (1, 2, 3):
        piece = lax.dynamic_slice_in_dim(summed, ((seq + k) % 4) * out_cols, out_cols, 1).astype(BF16)
        perm = [(i, (i + k) % 4) for i in range(3)]
        out = out + lax.ppermute(piece, "seq", perm).astype(F32)

    kg = jnp.concatenate([a for a, _ in key_grads], axis=1)
    kg_other = jnp.concatenate([b for _, b in key_grads], axis=1)
    in_mine = dot(kg, kv_weight, 1, 1).astype(BF16)
    in_back = lax.ppermute(dot(kg_other, kv_weight, 1, 1).astype(BF16), "fsdp", SWAP)
    input_grad = jnp.where(
        core == 0,
        jnp.concatenate([in_mine, in_back], axis=1),
        jnp.concatenate([in_back, in_mine], axis=1),
    )
    return input_grad[None], out / lax.axis_size(("dp", "fsdp"))


def solution(mesh):
    placed = (
        P(("dp", "fsdp"), "seq", None),
        P(("dp", "fsdp"), "seq", None),
        P(("dp", "fsdp"), "seq", None),
        P(("dp", "fsdp"), None),
        P(("dp", "fsdp"), None),
        P("fsdp", None),
    )
    return jax.shard_map(
        on_device,
        mesh=mesh,
        in_specs=placed,
        out_specs=(P(("dp", "fsdp"), "seq", None), P(("dp", "fsdp"), "seq")),
        check_vma=False,
    )
```

time: 502 us -> 131 us (0.26)
  waiting for transfers between devices: 372 us -> 53.4 us
  local copies, waits for them, and re-layouts: 47 us -> 4.12 us
  starting transfers between devices: 19.8 us -> 45.3 us
  matrix products: 29.2 us -> 13.9 us
  blocking collectives: 14.3 us -> 0 us
  between operations: 15.3 us -> 2.37 us
  Pallas kernels: 0 us -> 7.58 us
    unnamed x4 -> x0, waiting for transfers between devices: 312 us -> none
    ppermute x0 -> x25, waiting for transfers between devices: none -> 53.4 us  [the longest x1 11.5 us: on_device(): from_a = lax.ppermute(to_a, 'seq', reverse(AHEAD))]
    ppermute x0 -> x25, starting transfers between devices: none -> 45.3 us  [the longest x3 9.81 us: on_device(): out = out + lax.ppermute(piece, 'seq', perm).astype(F32)]
    unnamed x15 -> x16, local copies, waits for them, and re-layouts: 26.6 us -> 0.04 us
    reduce_scatter x1 -> x0, waiting for transfers between devices: 22.7 us -> none  [on_device(): lax.psum_scatter(partial_rows, 'seq', scatter_dimension=1, tiled=True)]
    all_gather x1 -> x0, waiting for transfers between devices: 19.8 us -> none  [on_device(): weight = lax.all_gather(kv_weight, 'fsdp', axis=0, tiled=True)]
    all_to_all x3 -> x0, starting transfers between devices: 19.6 us -> none  [the longest x1 8.46 us: on_device(): lax.all_to_all(query[0], 'seq', split_axis=1, concat_axis=0, tiled=True)]
    all_to_all x3 -> x0, waiting for transfers between devices: 17.4 us -> none  [the longest x1 11.9 us: on_device(): lax.all_to_all(out_grad[0], 'seq', split_axis=1, concat_axis=0, tiled=True)]
  transfers between devices with their start and end apart: 6 -> 25, of which waited for: 5 -> 11; matrix products, arithmetic and copies ran while one was open for 7% -> 12% of each run, Pallas kernels for 0% -> 1%
where the time goes in v1:
time: 131 us; the launch traced here: 130 us
  waiting for transfers between devices  53.4 us (41%)
  starting transfers between devices  45.3 us (35%)
  matrix products  13.9 us (11%)
  Pallas kernels  7.58 us (6%)
  local copies, waits for them, and re-layouts  4.12 us (3%)
  other arithmetic  3.47 us (3%)
  between operations  2.37 us (2%)
    dot_general x4, matrix products, dot(): lax.dot_general(a, b, (((ca,), (cb,)), ((), ())), preferred_element_type=...  13.9 us
    ppermute x1, waiting for transfers between devices, on_device(): from_a = lax.ppermute(to_a, 'seq', reverse(AHEAD))  11.5 us
    ppermute x3, waiting for transfers between devices, on_device(): lax.ppermute(kg, 'dp', dp_shift(dx=k))  10.1 us
    ppermute x3, starting transfers between devices, on_device(): out = out + lax.ppermute(piece, 'seq', perm).astype(F32)  9.81 us
    ppermute x1, waiting for transfers between devices, on_device(): cross.append(lax.ppermute(kv[c], 'seq', CROSS))  9.64 us
    ppermute x3, waiting for transfers between devices, on_device(): came = [lax.ppermute(parts[k], 'dp', dp_shift(dy=k)) for k in (1, 2, 3)]  8.48 us
    pallas_call x5, Pallas kernels, call(): pl.pallas_call(kernel, out_shape=outs, in_specs=specs, out_specs=jax.tree...  7.58 us
    ppermute x1, starting transfers between devices, on_device(): from_b = lax.ppermute(to_b, 'seq', reverse(CROSS))  6.35 us
  transfers between devices with their start and end apart: 25, of which 11 were waited for; matrix products, arithmetic and copies ran while one was open for 12% of the time, Pallas kernels for 1%

profile of v1, /device:TPU:8, one launch (start us, length us, event | category | flops | bytes accessed | tf_op | source)
XLA Modules:
  0.0 130.1 jit_solution(3171272757849563108)
XLA Ops:
  0.6 1.1 dynamic-slice_bitcast_fusion
  3.2 0.3 fusion.4
  3.5 0.4 collective-permute-done
  4.0 4.4 %fusion.6 = f32[128,1024]{1,0:T(8,128)} fusion(bf16[128,2560]{1,0:T(8,128)(2,1)S(1)} %collective-permute-done, bf16[2560,1024]{1,0:T(8,128)(2,1)} %param.11), kind=kOutput, calls=%fused_computation.35 | convolution fusion | flops 671088640 | bytes 6422528 | tf_op jit(solution)/shard_map/dot_general | solution.py:52
  8.3 0.2 collective-permute-start.1
  8.6 0.1 pad_maximum_fusion.4
  8.7 3.3 %fusion.1.own_ref = f32[128,1024]{1,0:T(8,128)S(1)} fusion(bf16[2560,1024]{1,0:T(8,128)(2,1)} %param.11, bf16[1,128,5120]{2,1,0:T(8,128)(2,1)S(1)} %copy-done.2, s32[]{:T(128)S(6)} %select_n.106), kind=kOutput, calls=%fused_computation.4 | convolution fusion | flops 671088640 | bytes 6422532 | tf_op jit(solution)/shard_map/dot_general | solution.py:52
  12.1 0.2 shard_map.77.kv_ref
  12.2 5.3 %collective-permute-start.2 = (bf16[128,1024]{1,0:T(8,128)(2,1)S(1)}, bf16[128,1024]{1,0:T(8,128)(2,1)S(1)}, u32[]{:S(2)}, u32[]{:S(2)}) collective-permute-start(bf16[128,1024]{1,0:T(8,128)(2,1)S(1)} %shard_map.77.kv_ref), channel_id=1, source_target_pairs={{0,2},{2,4},{1,3},{3,5},{8,10},{10,12},{9,11},{11,13},{16,18},{18,... | collective-permute-start | bytes 786440 | tf_op jit(solution)/shard_map/ppermute | solution.py:201
  17.6 5.2 %collective-permute-start.3 = (bf16[128,1024]{1,0:T(8,128)(2,1)S(1)}, bf16[128,1024]{1,0:T(8,128)(2,1)S(1)}, u32[]{:S(2)}, u32[]{:S(2)}) collective-permute-start(bf16[128,1024]{1,0:T(8,128)(2,1)S(1)} %shard_map.77.kv_ref), channel_id=1, source_target_pairs={{2,0},{0,4},{3,1},{1,5},{10,8},{8,12},{11,9},{9,13},{18,16},{16,20... | collective-permute-start | bytes 786440 | tf_op jit(solution)/shard_map/ppermute | solution.py:202
  22.9 1.0 dynamic-slice_bitcast_fusion.1
  24.0 1.9 %constant_dynamic-slice_fusion = (bf16[128,640]{1,0:T(8,128)(2,1)S(1)}, bf16[128,640]{1,0:T(8,128)(2,1)S(1)}, bf16[128,640]{1,0:T(8,128)(2,1)S(1)}, bf16[128,640]{1,0:T(8,128)(2,1)}) fusion(bf16[128,2560]{1,0:T(8,128)(2,1)} %copy-done.3, s32[]{:T(128)S(6)} %select_n.124, s32[]{:T(128)S(6)} %select_n.121, s32[]{:T(128)S(6)} %select_n.118, s32[]{:T(128)S(6)} %select_n.114), kind=kLoop, calls=%fused_computation.26 | loop fusion | bytes 1310736 | tf_op jit(solution)/shard_map/dynamic_slice | solution.py:192
  25.8 9.6 %collective-permute-done.3.b_ref = bf16[128,1024]{1,0:T(8,128)(2,1)S(1)} collective-permute-done((bf16[128,1024]{1,0:T(8,128)(2,1)S(1)}, bf16[128,1024]{1,0:T(8,128)(2,1)S(1)}, u32[]{:S(2)}, u32[]{:S(2)}) %collective-permute-start.3) | collective-permute-done | bytes 262176 | tf_op jit(solution)/shard_map/ppermute | solution.py:202
  35.5 4.2 %shard_map.78 = (f32[128,1024]{1,0:T(8,128)S(1)}, bf16[128,1024]{1,0:T(8,128)(2,1)S(1)}, bf16[128,1024]{1,0:T(8,128)(2,1)S(1)}) custom-call(s32[3]{0:T(128)S(1)} %pad_add_fusion.meta, bf16[128,2560]{1,0:T(8,128)(2,1)S(1)} %bitcast.30, bf16[128,2560]{1,0:T(8,128)(2,1)S(1)} %bitcast.31, bf16[128,1024]{1,0:T(8,128)(2,1)S(1)} %shard_map.77.kv_ref, ...), custom_call_target="tpu_custom_call" | custom-call | tf_op jit(solution)/shard_map/pallas_call | solution.py:149
  39.7 1.4 %collective-permute-start.4 = (bf16[128,1024]{1,0:T(8,128)(2,1)S(1)}, bf16[128,1024]{1,0:T(8,128)(2,1)S(1)}, u32[]{:S(2)}, u32[]{:S(2)}) collective-permute-start(bf16[128,1024]{1,0:T(8,128)(2,1)S(1)} %get-tuple-element.12), channel_id=1, source_target_pairs={{2,0},{4,2},{3,1},{5,3},{10,8},{12,10},{11,9},{13,11},{18,16},{20,... | collective-permute-start | bytes 786440 | tf_op jit(solution)/shard_map/ppermute | solution.py:215
  41.2 6.3 %collective-permute-start.5 = (bf16[128,1024]{1,0:T(8,128)(2,1)S(1)}, bf16[128,1024]{1,0:T(8,128)(2,1)S(1)}, u32[]{:S(2)}, u32[]{:S(2)}) collective-permute-start(bf16[128,1024]{1,0:T(8,128)(2,1)S(1)} %get-tuple-element.13), channel_id=1, source_target_pairs={{0,2},{4,0},{1,3},{5,1},{8,10},{12,8},{9,11},{13,9},{16,18},{20,16... | collective-permute-start | bytes 786440 | tf_op jit(solution)/shard_map/ppermute | solution.py:216
  47.5 2.8 %collective-permute-start.10 = (bf16[256,640]{1,0:T(8,128)(2,1)S(1)}, bf16[256,640]{1,0:T(8,128)(2,1)S(1)}, u32[]{:S(2)}, u32[]{:S(2)}) collective-permute-start(bf16[256,640]{1,0:T(8,128)(2,1)S(1)} %pad_maximum_fusion.3), channel_id=1, source_target_pairs={{0,96},{8,104},{16,112},{24,120},{32,0},{40,8},{48,16},{56,24},{64... | collective-permute-start | bytes 983048 | tf_op jit(solution)/shard_map/ppermute | solution.py:194
  50.4 0.9 collective-permute-start.9
  51.3 11.5 %collective-permute-done.4.a_ref = bf16[128,1024]{1,0:T(8,128)(2,1)S(1)} collective-permute-done((bf16[128,1024]{1,0:T(8,128)(2,1)S(1)}, bf16[128,1024]{1,0:T(8,128)(2,1)S(1)}, u32[]{:S(2)}, u32[]{:S(2)}) %collective-permute-start.4) | collective-permute-done | bytes 262176 | tf_op jit(solution)/shard_map/ppermute | solution.py:215
  62.8 0.2 shard_map.79.refs_4_
  63.0 1.6 %collective-permute-start.11 = (bf16[128,1024]{1,0:T(8,128)(2,1)S(1)}, bf16[128,1024]{1,0:T(8,128)(2,1)S(1)}, u32[]{:S(2)}, u32[]{:S(2)}) collective-permute-start(bf16[128,1024]{1,0:T(8,128)(2,1)S(1)} %shard_map.79.refs_4_), channel_id=1, source_target_pairs={{0,32},{8,40},{16,48},{24,56},{32,64},{40,72},{48,80},{56,88},{64,... | collective-permute-start | bytes 786440 | tf_op jit(solution)/shard_map/ppermute | solution.py:218
  64.6 2.7 %collective-permute-start.13 = (bf16[128,1024]{1,0:T(8,128)(2,1)S(1)}, bf16[128,1024]{1,0:T(8,128)(2,1)S(1)}, u32[]{:S(2)}, u32[]{:S(2)}) collective-permute-start(bf16[128,1024]{1,0:T(8,128)(2,1)S(1)} %shard_map.79.refs_4_), channel_id=1, source_target_pairs={{0,64},{8,72},{16,80},{24,88},{32,96},{40,104},{48,112},{56,120},{... | collective-permute-start | bytes 786440 | tf_op jit(solution)/shard_map/ppermute | solution.py:218
  67.3 1.4 %collective-permute-start.15 = (bf16[128,1024]{1,0:T(8,128)(2,1)S(1)}, bf16[128,1024]{1,0:T(8,128)(2,1)S(1)}, u32[]{:S(2)}, u32[]{:S(2)}) collective-permute-start(bf16[128,1024]{1,0:T(8,128)(2,1)S(1)} %shard_map.79.refs_4_), channel_id=1, source_target_pairs={{0,96},{8,104},{16,112},{24,120},{32,0},{40,8},{48,16},{56,24},{64... | collective-permute-start | bytes 786440 | tf_op jit(solution)/shard_map/ppermute | solution.py:218
  68.7 0.8 pad_maximum_fusion.1
  69.5 0.6 collective-permute-start.8
  70.1 2.5 %collective-permute-done.11.refs_6_ = bf16[128,1024]{1,0:T(8,128)(2,1)S(1)} collective-permute-done((bf16[128,1024]{1,0:T(8,128)(2,1)S(1)}, bf16[128,1024]{1,0:T(8,128)(2,1)S(1)}, u32[]{:S(2)}, u32[]{:S(2)}) %collective-permute-start.11) | collective-permute-done | bytes 262176 | tf_op jit(solution)/shard_map/ppermute | solution.py:218
  72.6 7.5 %collective-permute-done.13.refs_8_ = bf16[128,1024]{1,0:T(8,128)(2,1)S(1)} collective-permute-done((bf16[128,1024]{1,0:T(8,128)(2,1)S(1)}, bf16[128,1024]{1,0:T(8,128)(2,1)S(1)}, u32[]{:S(2)}, u32[]{:S(2)}) %collective-permute-start.13) | collective-permute-done | bytes 262176 | tf_op jit(solution)/shard_map/ppermute | solution.py:218
  80.2 0.5 collective-permute-start.16
  80.8 3.9 %collective-permute-done.8.refs_1_ = bf16[256,640]{1,0:T(8,128)(2,1)S(1)} collective-permute-done((bf16[256,640]{1,0:T(8,128)(2,1)}, bf16[256,640]{1,0:T(8,128)(2,1)S(1)}, u32[]{:S(2)}, u32[]{:S(2)}) %collective-permute-start.8) | collective-permute-done | bytes 327712 | tf_op jit(solution)/shard_map/ppermute | solution.py:194
  84.7 2.3 %shard_map.80 = (f32[160,1024]{1,0:T(8,128)S(1)}, bf16[160,1024]{1,0:T(8,128)(2,1)S(1)}, bf16[160,1024]{1,0:T(8,128)(2,1)S(1)}, bf16[160,1024]{1,0:T(8,128)(2,1)S(1)}) custom-call(s32[2]{0:T(128)S(1)} %pad_add_fusion.1.meta, bf16[256,640]{1,0:T(8,128)(2,1)S(1)} %pad_maximum_fusion.refs_0_, bf16[256,640]{1,0:T(8,128)(2,1)S(1)} %collective-permute-done.8.refs_1_, ...), custom_call_target="tpu_custom_call" | custom-call | tf_op jit(solution)/shard_map/pallas_call | solution.py:149
  87.1 1.7 %collective-permute-start.17 = (bf16[160,1024]{1,0:T(8,128)(2,1)S(1)}, bf16[160,1024]{1,0:T(8,128)(2,1)S(1)}, u32[]{:S(2)}, u32[]{:S(2)}) collective-permute-start(bf16[160,1024]{1,0:T(8,128)(2,1)S(1)} %get-tuple-element.15), channel_id=1, source_target_pairs={{0,8},{8,16},{16,24},{24,0},{32,40},{40,48},{48,56},{56,32},{64,72... | collective-permute-start | bytes 983048 | tf_op jit(solution)/shard_map/ppermute | solution.py:230
  88.7 0.9 collective-permute-start.18
  89.7 2.4 %collective-permute-start.19 = (bf16[160,1024]{1,0:T(8,128)(2,1)S(1)}, bf16[160,1024]{1,0:T(8,128)(2,1)S(1)}, u32[]{:S(2)}, u32[]{:S(2)}) collective-permute-start(bf16[160,1024]{1,0:T(8,128)(2,1)S(1)} %get-tuple-element.17), channel_id=1, source_target_pairs={{0,24},{8,0},{16,8},{24,16},{32,56},{40,32},{48,40},{56,48},{64,88... | collective-permute-start | bytes 983048 | tf_op jit(solution)/shard_map/ppermute | solution.py:230
  92.1 4.3 %convolution_convert_fusion = bf16[128,2560]{1,0:T(8,128)(2,1)S(1)} fusion(bf16[128,1024]{1,0:T(8,128)(2,1)S(1)} %collective-permute-done.6.refs_5_, bf16[2560,1024]{1,0:T(8,128)(2,1)} %param.11), kind=kOutput, calls=%fused_computation | convolution fusion | flops 671416320 | bytes 6160384 | tf_op jit(solution)/shard_map/dot_general | solution.py:52
  96.5 1.3 collective-permute-done.17.a_ref
  97.8 3.1 %collective-permute-done.18.b_ref = bf16[160,1024]{1,0:T(8,128)(2,1)S(1)} collective-permute-done((bf16[160,1024]{1,0:T(8,128)(2,1)S(1)}, bf16[160,1024]{1,0:T(8,128)(2,1)S(1)}, u32[]{:S(2)}, u32[]{:S(2)}) %collective-permute-start.18) | collective-permute-done | bytes 327712 | tf_op jit(solution)/shard_map/ppermute | solution.py:230
  100.9 4.1 %collective-permute-done.19.c_ref = bf16[160,1024]{1,0:T(8,128)(2,1)S(1)} collective-permute-done((bf16[160,1024]{1,0:T(8,128)(2,1)S(1)}, bf16[160,1024]{1,0:T(8,128)(2,1)S(1)}, u32[]{:S(2)}, u32[]{:S(2)}) %collective-permute-start.19) | collective-permute-done | bytes 327712 | tf_op jit(solution)/shard_map/ppermute | solution.py:230
  105.0 0.7 shard_map.81
  105.7 0.7 collective-permute-start.20
  106.4 0.6 collective-permute-start.21
  107.0 1.8 %fusion = bf16[1,128,2560]{2,1,0:T(8,128)(2,1)S(1)} fusion(bf16[128,1024]{1,0:T(8,128)(2,1)S(1)} %shard_map.79.refs_4_, bf16[2560,1024]{1,0:T(8,128)(2,1)S(1)} %bitcast.33), kind=kOutput, calls=%fused_computation.2 | convolution fusion | flops 671416320 | bytes 6160384 | tf_op jit(solution)/shard_map/dot_general | solution.py:52
  108.9 4.7 %collective-permute-done.21 = bf16[80,1024]{1,0:T(8,128)(2,1)S(1)} collective-permute-done((bf16[80,1024]{1,0:T(8,128)(2,1)S(1)}, bf16[80,1024]{1,0:T(8,128)(2,1)S(1)}, u32[]{:S(2)}, u32[]{:S(2)}) %collective-permute-start.21) | collective-permute-done | bytes 163872 | tf_op jit(solution)/shard_map/ppermute | solution.py:235
  113.6 6.0 %collective-permute-start.22 = (bf16[80,256]{1,0:T(8,128)(2,1)S(1)}, bf16[80,256]{1,0:T(8,128)(2,1)S(1)}, u32[]{:S(2)}, u32[]{:S(2)}) collective-permute-start(bf16[80,256]{1,0:T(8,128)(2,1)S(1)} %get-tuple-element.28), channel_id=1, source_target_pairs={{0,2},{2,4},{4,6},{1,3},{3,5},{5,7},{8,10},{10,12},{12,14},{9,11},... | collective-permute-start | bytes 122888 | tf_op jit(solution)/shard_map/ppermute | solution.py:244
  119.6 1.9 %collective-permute-start.23 = (bf16[80,256]{1,0:T(8,128)(2,1)S(1)}, bf16[80,256]{1,0:T(8,128)(2,1)S(1)}, u32[]{:S(2)}, u32[]{:S(2)}) collective-permute-start(bf16[80,256]{1,0:T(8,128)(2,1)S(1)} %get-tuple-element.30), channel_id=1, source_target_pairs={{0,4},{2,6},{4,0},{1,5},{3,7},{5,1},{8,12},{10,14},{12,8},{9,13},{... | collective-permute-start | bytes 122888 | tf_op jit(solution)/shard_map/ppermute | solution.py:244
  121.5 1.9 %collective-permute-start.24 = (bf16[80,256]{1,0:T(8,128)(2,1)S(1)}, bf16[80,256]{1,0:T(8,128)(2,1)S(1)}, u32[]{:S(2)}, u32[]{:S(2)}) collective-permute-start(bf16[80,256]{1,0:T(8,128)(2,1)S(1)} %get-tuple-element.29), channel_id=1, source_target_pairs={{0,6},{2,0},{4,2},{1,7},{3,1},{5,3},{8,14},{10,8},{12,10},{9,15},{... | collective-permute-start | bytes 122888 | tf_op jit(solution)/shard_map/ppermute | solution.py:244
  123.5 1.4 %maximum_select_fusion = bf16[1,128,5120]{2,1,0:T(8,128)(2,1)} fusion(bf16[1,128,2560]{2,1,0:T(8,128)(2,1)S(1)} %bitcast.34, bf16[1,128,2560]{2,1,0:T(8,128)(2,1)S(1)} %fusion, pred[]{:T(512)S(6)} %eq.13), kind=kLoop, calls=%fused_computation.3 | loop fusion | flops 5898240 | bytes 2621441 | tf_op jit(solution)/shard_map/jit(_where)/select_n | solution.py:250
  124.8 4.6 %collective-permute-done.23 = bf16[80,256]{1,0:T(8,128)(2,1)S(1)} collective-permute-done((bf16[80,256]{1,0:T(8,128)(2,1)S(1)}, bf16[80,256]{1,0:T(8,128)(2,1)S(1)}, u32[]{:S(2)}, u32[]{:S(2)}) %collective-permute-start.23) | collective-permute-done | bytes 40992 | tf_op jit(solution)/shard_map/ppermute | solution.py:244
  129.4 0.7 add_multiply_fusion
  (45 shorter events, 0.6 us)
Async XLA Ops:
  1.8 2.2 %collective-permute-start = (bf16[128,2560]{1,0:T(8,128)(2,1)S(1)}, bf16[128,2560]{1,0:T(8,128)(2,1)S(1)}, u32[]{:S(2)}, u32[]{:S(2)}) collective-permute-start(bf16[128,2560]{1,0:T(8,128)(2,1)S(1)} %dynamic-slice_bitcast_fusion), channel_id=1, source_target_pairs={{0,1},{1,0},{2,3},{3,2},{4,5},{5,4},{6,7},{7,6},{8,9},{9,8},{10,11... | collective-permute-start | bytes 1966088 | tf_op jit(solution)/shard_map/ppermute | solution.py:183
  3.5 5.2 %copy-start.2 = (bf16[1,128,5120]{2,1,0:T(8,128)(2,1)S(1)}, bf16[1,128,5120]{2,1,0:T(8,128)(2,1)}, u32[]{:S(2)}) copy-start(bf16[1,128,5120]{2,1,0:T(8,128)(2,1)} %param.6) | copy-start | bytes 3932164
  4.0 4.4 %copy-start.3 = (bf16[128,2560]{1,0:T(8,128)(2,1)}, bf16[128,2560]{1,0:T(8,128)(2,1)S(1)}, u32[]{:S(2)}) copy-start(bf16[128,2560]{1,0:T(8,128)(2,1)S(1)} %collective-permute-done) | copy-start | bytes 1966084
  8.3 3.8 %collective-permute-start.1 = (f32[128,1024]{1,0:T(8,128)}, f32[128,1024]{1,0:T(8,128)S(1)}, u32[]{:S(2)}, u32[]{:S(2)}) collective-permute-start(f32[128,1024]{1,0:T(8,128)} %fusion.6), channel_id=1, source_target_pairs={{0,1},{1,0},{2,3},{3,2},{4,5},{5,4},{6,7},{7,6},{8,9},{9,8},{10,11... | collective-permute-start | bytes 1572872 | tf_op jit(solution)/shard_map/ppermute | solution.py:199
  12.0 23.4 %copy-start = (bf16[1,128,2560]{2,1,0:T(8,128)(2,1)S(1)}, bf16[1,128,2560]{2,1,0:T(8,128)(2,1)}, u32[]{:S(2)}) copy-start(bf16[1,128,2560]{2,1,0:T(8,128)(2,1)} %param.7) | copy-start | bytes 1966084
  12.1 23.4 %copy-start.1 = (bf16[1,128,2560]{2,1,0:T(8,128)(2,1)S(1)}, bf16[1,128,2560]{2,1,0:T(8,128)(2,1)}, u32[]{:S(2)}) copy-start(bf16[1,128,2560]{2,1,0:T(8,128)(2,1)} %param.8) | copy-start | bytes 1966084
  12.2 13.6 %collective-permute-start.2 = (bf16[128,1024]{1,0:T(8,128)(2,1)S(1)}, bf16[128,1024]{1,0:T(8,128)(2,1)S(1)}, u32[]{:S(2)}, u32[]{:S(2)}) collective-permute-start(bf16[128,1024]{1,0:T(8,128)(2,1)S(1)} %shard_map.77.kv_ref), channel_id=1, source_target_pairs={{0,2},{2,4},{1,3},{3,5},{8,10},{10,12},{9,11},{11,13},{16,18},{18,... | collective-permute-start | bytes 786440 | tf_op jit(solution)/shard_map/ppermute | solution.py:201
  17.6 17.9 %collective-permute-start.3 = (bf16[128,1024]{1,0:T(8,128)(2,1)S(1)}, bf16[128,1024]{1,0:T(8,128)(2,1)S(1)}, u32[]{:S(2)}, u32[]{:S(2)}) collective-permute-start(bf16[128,1024]{1,0:T(8,128)(2,1)S(1)} %shard_map.77.kv_ref), channel_id=1, source_target_pairs={{2,0},{0,4},{3,1},{1,5},{10,8},{8,12},{11,9},{9,13},{18,16},{16,20... | collective-permute-start | bytes 786440 | tf_op jit(solution)/shard_map/ppermute | solution.py:202
  39.7 41.1 %copy-start.4 = (bf16[128,640]{1,0:T(8,128)(2,1)S(1)}, bf16[128,640]{1,0:T(8,128)(2,1)}, u32[]{:S(2)}) copy-start(bf16[128,640]{1,0:T(8,128)(2,1)} %get-tuple-element.22) | copy-start | bytes 491524
  39.7 41.0 %copy-start.5 = (bf16[128,640]{1,0:T(8,128)(2,1)S(1)}, bf16[128,640]{1,0:T(8,128)(2,1)}, u32[]{:S(2)}) copy-start(bf16[128,640]{1,0:T(8,128)(2,1)} %get-tuple-element.27) | copy-start | bytes 491524
  39.7 23.1 %collective-permute-start.4 = (bf16[128,1024]{1,0:T(8,128)(2,1)S(1)}, bf16[128,1024]{1,0:T(8,128)(2,1)S(1)}, u32[]{:S(2)}, u32[]{:S(2)}) collective-permute-start(bf16[128,1024]{1,0:T(8,128)(2,1)S(1)} %get-tuple-element.12), channel_id=1, source_target_pairs={{2,0},{4,2},{3,1},{5,3},{10,8},{12,10},{11,9},{13,11},{18,16},{20,... | collective-permute-start | bytes 786440 | tf_op jit(solution)/shard_map/ppermute | solution.py:215
  41.2 21.7 %collective-permute-start.5 = (bf16[128,1024]{1,0:T(8,128)(2,1)S(1)}, bf16[128,1024]{1,0:T(8,128)(2,1)S(1)}, u32[]{:S(2)}, u32[]{:S(2)}) collective-permute-start(bf16[128,1024]{1,0:T(8,128)(2,1)S(1)} %get-tuple-element.13), channel_id=1, source_target_pairs={{0,2},{4,0},{1,3},{5,1},{8,10},{12,8},{9,11},{13,9},{16,18},{20,16... | collective-permute-start | bytes 786440 | tf_op jit(solution)/shard_map/ppermute | solution.py:216
  47.5 21.9 %collective-permute-start.10 = (bf16[256,640]{1,0:T(8,128)(2,1)S(1)}, bf16[256,640]{1,0:T(8,128)(2,1)S(1)}, u32[]{:S(2)}, u32[]{:S(2)}) collective-permute-start(bf16[256,640]{1,0:T(8,128)(2,1)S(1)} %pad_maximum_fusion.3), channel_id=1, source_target_pairs={{0,96},{8,104},{16,112},{24,120},{32,0},{40,8},{48,16},{56,24},{64... | collective-permute-start | bytes 983048 | tf_op jit(solution)/shard_map/ppermute | solution.py:194
  50.4 19.7 %collective-permute-start.9 = (bf16[256,640]{1,0:T(8,128)(2,1)S(1)}, bf16[256,640]{1,0:T(8,128)(2,1)S(1)}, u32[]{:S(2)}, u32[]{:S(2)}) collective-permute-start(bf16[256,640]{1,0:T(8,128)(2,1)S(1)} %pad_maximum_fusion.2), channel_id=1, source_target_pairs={{0,64},{8,72},{16,80},{24,88},{32,96},{40,104},{48,112},{56,120},{... | collective-permute-start | bytes 983048 | tf_op jit(solution)/shard_map/ppermute | solution.py:194
  63.0 9.6 %collective-permute-start.11 = (bf16[128,1024]{1,0:T(8,128)(2,1)S(1)}, bf16[128,1024]{1,0:T(8,128)(2,1)S(1)}, u32[]{:S(2)}, u32[]{:S(2)}) collective-permute-start(bf16[128,1024]{1,0:T(8,128)(2,1)S(1)} %shard_map.79.refs_4_), channel_id=1, source_target_pairs={{0,32},{8,40},{16,48},{24,56},{32,64},{40,72},{48,80},{56,88},{64,... | collective-permute-start | bytes 786440 | tf_op jit(solution)/shard_map/ppermute | solution.py:218
  64.6 15.6 %collective-permute-start.13 = (bf16[128,1024]{1,0:T(8,128)(2,1)S(1)}, bf16[128,1024]{1,0:T(8,128)(2,1)S(1)}, u32[]{:S(2)}, u32[]{:S(2)}) collective-permute-start(bf16[128,1024]{1,0:T(8,128)(2,1)S(1)} %shard_map.79.refs_4_), channel_id=1, source_target_pairs={{0,64},{8,72},{16,80},{24,88},{32,96},{40,104},{48,112},{56,120},{... | collective-permute-start | bytes 786440 | tf_op jit(solution)/shard_map/ppermute | solution.py:218
  67.3 12.9 %collective-permute-start.15 = (bf16[128,1024]{1,0:T(8,128)(2,1)S(1)}, bf16[128,1024]{1,0:T(8,128)(2,1)S(1)}, u32[]{:S(2)}, u32[]{:S(2)}) collective-permute-start(bf16[128,1024]{1,0:T(8,128)(2,1)S(1)} %shard_map.79.refs_4_), channel_id=1, source_target_pairs={{0,96},{8,104},{16,112},{24,120},{32,0},{40,8},{48,16},{56,24},{64... | collective-permute-start | bytes 786440 | tf_op jit(solution)/shard_map/ppermute | solution.py:218
  69.5 15.2 %collective-permute-start.8 = (bf16[256,640]{1,0:T(8,128)(2,1)}, bf16[256,640]{1,0:T(8,128)(2,1)S(1)}, u32[]{:S(2)}, u32[]{:S(2)}) collective-permute-start(bf16[256,640]{1,0:T(8,128)(2,1)} %pad_maximum_fusion.1), channel_id=1, source_target_pairs={{0,32},{8,40},{16,48},{24,56},{32,64},{40,72},{48,80},{56,88},{64,... | collective-permute-start | bytes 983048 | tf_op jit(solution)/shard_map/ppermute | solution.py:194
  70.1 14.6 %collective-permute-start.6 = (bf16[128,1024]{1,0:T(8,128)(2,1)S(1)}, bf16[128,1024]{1,0:T(8,128)(2,1)S(1)}, u32[]{:S(2)}, u32[]{:S(2)}) collective-permute-start(bf16[128,1024]{1,0:T(8,128)(2,1)S(1)} %shard_map.79.refs_4_), channel_id=1, source_target_pairs={{0,1},{1,0},{2,3},{3,2},{4,5},{5,4},{6,7},{7,6},{8,9},{9,8},{10,11... | collective-permute-start | bytes 786440 | tf_op jit(solution)/shard_map/ppermute | solution.py:219
  72.6 12.1 %collective-permute-start.12 = (bf16[128,1024]{1,0:T(8,128)(2,1)S(1)}, bf16[128,1024]{1,0:T(8,128)(2,1)S(1)}, u32[]{:S(2)}, u32[]{:S(2)}) collective-permute-start(bf16[128,1024]{1,0:T(8,128)(2,1)S(1)} %collective-permute-done.11.refs_6_), channel_id=1, source_target_pairs={{0,1},{1,0},{2,3},{3,2},{4,5},{5,4},{6,7},{7,6},{8,9},{9,8},{10,11... | collective-permute-start | bytes 786440 | tf_op jit(solution)/shard_map/ppermute | solution.py:219
  80.2 4.6 %collective-permute-start.14 = (bf16[128,1024]{1,0:T(8,128)(2,1)S(1)}, bf16[128,1024]{1,0:T(8,128)(2,1)S(1)}, u32[]{:S(2)}, u32[]{:S(2)}) collective-permute-start(bf16[128,1024]{1,0:T(8,128)(2,1)S(1)} %collective-permute-done.13.refs_8_), channel_id=1, source_target_pairs={{0,1},{1,0},{2,3},{3,2},{4,5},{5,4},{6,7},{7,6},{8,9},{9,8},{10,11... | collective-permute-start | bytes 786440 | tf_op jit(solution)/shard_map/ppermute | solution.py:219
  80.2 4.6 %collective-permute-start.16 = (bf16[128,1024]{1,0:T(8,128)(2,1)S(1)}, bf16[128,1024]{1,0:T(8,128)(2,1)S(1)}, u32[]{:S(2)}, u32[]{:S(2)}) collective-permute-start(bf16[128,1024]{1,0:T(8,128)(2,1)S(1)} %collective-permute-done.15.refs_10_), channel_id=1, source_target_pairs={{0,1},{1,0},{2,3},{3,2},{4,5},{5,4},{6,7},{7,6},{8,9},{9,8},{10,11... | collective-permute-start | bytes 786440 | tf_op jit(solution)/shard_map/ppermute | solution.py:219
  84.7 22.3 %slice-start = ((s8[5242880]{0:T(1024)(128)(4,1)}), s8[1048576]{0:T(1024)(128)(4,1)S(1)}, s32[]{:S(2)}) async-start(s8[5242880]{0:T(1024)(128)(4,1)} %bitcast.32), calls=%async_computation | async-start | bytes 2097152
  87.1 10.7 %collective-permute-start.17 = (bf16[160,1024]{1,0:T(8,128)(2,1)S(1)}, bf16[160,1024]{1,0:T(8,128)(2,1)S(1)}, u32[]{:S(2)}, u32[]{:S(2)}) collective-permute-start(bf16[160,1024]{1,0:T(8,128)(2,1)S(1)} %get-tuple-element.15), channel_id=1, source_target_pairs={{0,8},{8,16},{16,24},{24,0},{32,40},{40,48},{48,56},{56,32},{64,72... | collective-permute-start | bytes 983048 | tf_op jit(solution)/shard_map/ppermute | solution.py:230
  88.7 12.2 %collective-permute-start.18 = (bf16[160,1024]{1,0:T(8,128)(2,1)S(1)}, bf16[160,1024]{1,0:T(8,128)(2,1)S(1)}, u32[]{:S(2)}, u32[]{:S(2)}) collective-permute-start(bf16[160,1024]{1,0:T(8,128)(2,1)S(1)} %get-tuple-element.16), channel_id=1, source_target_pairs={{0,16},{8,24},{16,0},{24,8},{32,48},{40,56},{48,32},{56,40},{64,80... | collective-permute-start | bytes 983048 | tf_op jit(solution)/shard_map/ppermute | solution.py:230
  89.7 17.3 %slice-start.1 = ((s8[5242880]{0:T(1024)(128)(4,1)}), s8[4194304]{0:T(1024)(128)(4,1)S(1)}, s32[]{:S(2)}) async-start(s8[5242880]{0:T(1024)(128)(4,1)} %bitcast.32), calls=%async_computation.1 | async-start | bytes 8388608
  89.7 15.3 %collective-permute-start.19 = (bf16[160,1024]{1,0:T(8,128)(2,1)S(1)}, bf16[160,1024]{1,0:T(8,128)(2,1)S(1)}, u32[]{:S(2)}, u32[]{:S(2)}) collective-permute-start(bf16[160,1024]{1,0:T(8,128)(2,1)S(1)} %get-tuple-element.17), channel_id=1, source_target_pairs={{0,24},{8,0},{16,8},{24,16},{32,56},{40,32},{48,40},{56,48},{64,88... | collective-permute-start | bytes 983048 | tf_op jit(solution)/shard_map/ppermute | solution.py:230
  96.4 27.1 %collective-permute-start.7 = (bf16[128,2560]{1,0:T(8,128)(2,1)S(1)}, bf16[128,2560]{1,0:T(8,128)(2,1)S(1)}, u32[]{:S(2)}, u32[]{:S(2)}) collective-permute-start(bf16[128,2560]{1,0:T(8,128)(2,1)S(1)} %convolution_convert_fusion), channel_id=1, source_target_pairs={{0,1},{1,0},{2,3},{3,2},{4,5},{5,4},{6,7},{7,6},{8,9},{9,8},{10,11... | collective-permute-start | bytes 1966088 | tf_op jit(solution)/shard_map/ppermute | solution.py:249
  105.7 3.1 %collective-permute-start.20 = (bf16[80,1024]{1,0:T(8,128)(2,1)S(1)}, bf16[80,1024]{1,0:T(8,128)(2,1)S(1)}, u32[]{:S(2)}, u32[]{:S(2)}) collective-permute-start(bf16[80,1024]{1,0:T(8,128)(2,1)S(1)} %get-tuple-element.18), channel_id=1, source_target_pairs={{0,0},{1,128},{8,8},{9,136},{16,16},{17,144},{24,24},{25,152},{32,... | collective-permute-start | bytes 491528 | tf_op jit(solution)/shard_map/ppermute | solution.py:234
  106.4 7.2 %collective-permute-start.21 = (bf16[80,1024]{1,0:T(8,128)(2,1)S(1)}, bf16[80,1024]{1,0:T(8,128)(2,1)S(1)}, u32[]{:S(2)}, u32[]{:S(2)}) collective-permute-start(bf16[80,1024]{1,0:T(8,128)(2,1)S(1)} %get-tuple-element.19), channel_id=1, source_target_pairs={{0,1},{1,129},{8,9},{9,137},{16,17},{17,145},{24,25},{25,153},{32,... | collective-permute-start | bytes 491528 | tf_op jit(solution)/shard_map/ppermute | solution.py:235
  113.6 11.2 %collective-permute-start.22 = (bf16[80,256]{1,0:T(8,128)(2,1)S(1)}, bf16[80,256]{1,0:T(8,128)(2,1)S(1)}, u32[]{:S(2)}, u32[]{:S(2)}) collective-permute-start(bf16[80,256]{1,0:T(8,128)(2,1)S(1)} %get-tuple-element.28), channel_id=1, source_target_pairs={{0,2},{2,4},{4,6},{1,3},{3,5},{5,7},{8,10},{10,12},{12,14},{9,11},... | collective-permute-start | bytes 122888 | tf_op jit(solution)/shard_map/ppermute | solution.py:244
  119.6 9.8 %collective-permute-start.23 = (bf16[80,256]{1,0:T(8,128)(2,1)S(1)}, bf16[80,256]{1,0:T(8,128)(2,1)S(1)}, u32[]{:S(2)}, u32[]{:S(2)}) collective-permute-start(bf16[80,256]{1,0:T(8,128)(2,1)S(1)} %get-tuple-element.30), channel_id=1, source_target_pairs={{0,4},{2,6},{4,0},{1,5},{3,7},{5,1},{8,12},{10,14},{12,8},{9,13},{... | collective-permute-start | bytes 122888 | tf_op jit(solution)/shard_map/ppermute | solution.py:244
  121.5 7.9 %collective-permute-start.24 = (bf16[80,256]{1,0:T(8,128)(2,1)S(1)}, bf16[80,256]{1,0:T(8,128)(2,1)S(1)}, u32[]{:S(2)}, u32[]{:S(2)}) collective-permute-start(bf16[80,256]{1,0:T(8,128)(2,1)S(1)} %get-tuple-element.29), channel_id=1, source_target_pairs={{0,6},{2,0},{4,2},{1,7},{3,1},{5,3},{8,14},{10,8},{12,10},{9,15},{... | collective-permute-start | bytes 122888 | tf_op jit(solution)/shard_map/ppermute | solution.py:244

commit v2 on v1

v2 whole, which is shorter than its diff:
```python
import jax
import jax.numpy as jnp
from jax import lax
from jax.experimental import pallas as pl
from jax.experimental.pallas import tpu as pltpu
from jax.sharding import PartitionSpec as P

HD = 128
GROUP = 5
IMG_TOK = 64
TEXT = 32
TOK = 128
TAIL = 32
TAIL_AT = 256
NG = 1
rope_base = 1000000.0
neg_fill = -1e30
VMEM = pl.BlockSpec(memory_space=pltpu.VMEM)
SMEM = pl.BlockSpec(memory_space=pltpu.SMEM)
F32 = jnp.float32
BF16 = jnp.bfloat16
SWAP = ((0, 1), (1, 0))
DOWN = ((0, 3), (1, 0), (2, 1), (3, 2))
UP = ((0, 1), (1, 2), (2, 3), (3, 0))
NEXT = ((0, 1), (1, 0), (2, 3), (3, 2))
ACROSS = ((0, 3), (1, 2), (2, 1), (3, 0))


def dp_shift(dx=0, dy=0, dz=0):
    pairs = []
    for d in range(32):
        z, x, y = d // 16, (d // 4) % 4, d % 4
        pairs.append((d, ((z + dz) % 2) * 16 + ((x + dx) % 4) * 4 + (y + dy) % 4))
    return pairs


def y_perm(dy):
    pairs = []
    for d in range(32):
        z, x, y = d // 16, (d // 4) % 4, d % 4
        for c in range(2):
            pairs.append((d * 2 + c, (c * 16 + x * 4 + (y + dy) % 4) * 2 + z))
    return pairs


def dot(a, b, ca, cb):
    return lax.dot_general(a, b, (((ca,), (cb,)), ((), ())), preferred_element_type=F32)


def swap_halves(block):
    half = HD // 2
    return jnp.concatenate([block[:, half:], block[:, :half]], axis=1)


def project_kernel(core, x_ref, w_ref, out_ref):
    half = w_ref.shape[0]
    out_ref[...] = dot(x_ref[:, pl.ds(pl.multiple_of(core[0] * half, HD), half)], w_ref[...], 1, 0)


def kv_kernel(own_ref, recv_ref, cos_ref, sin_ref, kv_ref, tail_ref):
    cos, sin = cos_ref[...], sin_ref[...]
    for h in range(kv_ref.shape[1] // (2 * HD)):
        at = h * 2 * HD
        ks, vs = slice(at, at + HD), slice(at + HD, at + 2 * HD)
        k = own_ref[:, ks] + recv_ref[:, ks]
        v = own_ref[:, vs] + recv_ref[:, vs]
        kv_ref[:, ks] = (k * cos + swap_halves(k) * sin).astype(BF16)
        kv_ref[:, vs] = v.astype(BF16)
    tail_ref[...] = kv_ref[:TAIL, :]


def attention_kernel(
    meta, q_ref, g_ref, tail_ref, kv_ref, next_ref, end_ref, own_out, next_out, end_out
):
    place, prefix, total = meta[0], meta[1], meta[2]
    n_own, n_all = GROUP * TOK, GROUP * (TOK + TAIL)
    n_keys = 2 * TOK + TAIL
    lane = lax.broadcasted_iota(jnp.int32, (1, n_all), 1)
    query_at = jnp.where(
        lane < n_own, place * TOK + lax.rem(lane, TOK), TAIL_AT + lax.rem(lane, TAIL)
    )
    live = (query_at < total) & (place < 2) & ((lane < n_own) | (place == 1))
    live = jnp.where(live, 1.0, 0.0)
    row = lax.broadcasted_iota(jnp.int32, (n_keys, 1), 0)
    key_at = jnp.where(
        row < TOK, place * TOK + row, jnp.where(row < 2 * TOK, (1 - place) * TOK + row - TOK, row)
    )
    key_at = jnp.where((row >= 2 * TOK) & (place != 1), total, key_at)
    allowed = (key_at < total) & ((key_at < prefix) | (key_at <= query_at))
    bias = jnp.where(allowed, 0.0, neg_fill)
    scale = HD ** (-0.5)
    width = tail_ref.shape[1] // 2
    for h in range(kv_ref.shape[1] // (2 * HD)):
        at = h * 2 * HD
        ks, vs = slice(at, at + HD), slice(at + HD, at + 2 * HD)

        def joined(cut):
            return jnp.concatenate([r[:, cut] for r in (kv_ref, next_ref, end_ref)], axis=0)

        keys, values = joined(ks), joined(vs)
        cols = [(h * GROUP + i) * HD for i in range(GROUP)]
        queries = jnp.concatenate(
            [q_ref[:, c : c + HD] for c in cols]
            + [tail_ref[:, c : c + HD] for c in cols],
            axis=0,
        )
        grads = jnp.concatenate(
            [g_ref[:, c : c + HD] for c in cols]
            + [tail_ref[:, width + c : width + c + HD] for c in cols],
            axis=0,
        )
        scores = dot(keys, queries, 1, 1) * scale + bias
        top = jnp.max(scores, axis=0, keepdims=True)
        exponent = jnp.exp(scores - top)
        inverse = live / jnp.sum(exponent, axis=0, keepdims=True)
        attention = exponent * inverse
        grad_attention = dot(values, grads, 1, 1)
        delta = jnp.sum(attention * grad_attention, axis=0, keepdims=True)
        grad_scores = (attention * (grad_attention - delta)).astype(BF16)
        grad_values = dot(attention.astype(BF16), grads, 1, 0)
        grad_keys = dot(grad_scores, queries, 1, 0) * scale
        for made, cut in ((grad_keys, ks), (grad_values, vs)):
            own_out[:, cut] = made[:TOK]
            next_out[:, cut] = made[TOK : 2 * TOK].astype(BF16)
            end_out[:, cut] = made[2 * TOK :].astype(BF16)


def kg_kernel(own_ref, next_ref, end_ref, cos_ref, sin_ref, *outs):
    cos, sin = cos_ref[...], sin_ref[...]
    cols = outs[0].shape[1]

    def total(cut):
        both = own_ref[:, cut] + next_ref[:, cut].astype(F32)
        return jnp.concatenate([both[:TAIL] + end_ref[:, cut].astype(F32), both[TAIL:]], axis=0)

    for c, out in enumerate(outs):
        for h in range(cols // (2 * HD)):
            at = h * 2 * HD
            k = total(slice(c * cols + at, c * cols + at + HD))
            out[:, at : at + HD] = (k * cos - swap_halves(k) * sin).astype(BF16)
            out[:, at + HD : at + 2 * HD] = total(
                slice(c * cols + at + HD, c * cols + at + 2 * HD)
            ).astype(BF16)


def weight_kernel(meta, *refs):
    mains, direct, swapped, outs, total = refs[:4], refs[4:8], refs[8:12], refs[12:16], refs[16]
    y = meta[0]
    left = jnp.concatenate([r[...] for r in mains], axis=0)
    right = jnp.concatenate([r[...] for pair in zip(direct, swapped) for r in pair], axis=0)
    total[...] = dot(left, right, 0, 0)
    rows = total.shape[0] // 4
    for k, out in enumerate(outs):
        out[...] = total[pl.ds(pl.multiple_of(lax.rem(y + k, 4) * rows, 16), rows), :].astype(BF16)


def sum_kernel(meta, a_ref, b_ref, c_ref, d_ref, keep_ref, give_ref):
    core = meta[1]
    rows = keep_ref.shape[0]
    total = a_ref[...].astype(F32) + b_ref[...].astype(F32)
    total = total + (c_ref[...].astype(F32) + d_ref[...].astype(F32))
    lower, upper = total[:rows], total[rows:]
    keep_ref[...] = jnp.where(core == 0, lower, upper)
    give_ref[...] = jnp.where(core == 0, upper, lower).astype(BF16)


def call(kernel, outs, *args, meta=False, scratch=(), cut=(), grid=(), vmem=40):
    specs = [VMEM] * len(args)
    if meta:
        specs[0] = SMEM
    for at, spec in cut:
        specs[at] = spec
    return pl.pallas_call(
        kernel,
        grid=grid,
        out_shape=outs,
        in_specs=specs,
        out_specs=jax.tree.map(lambda _: VMEM, outs),
        scratch_shapes=scratch,
        compiler_params=pltpu.CompilerParams(vmem_limit_bytes=vmem * 1024 * 1024),
    )(*args)


def shape(rows, cols, dtype):
    return jax.ShapeDtypeStruct((rows, cols), dtype)


def rope(position):
    frequency = rope_base ** (-(2.0 * jnp.arange(HD // 2, dtype=F32)) / HD)
    angles = position.astype(F32)[:, None] * frequency[None, :]
    cos, sin = jnp.cos(angles), jnp.sin(angles)
    return jnp.concatenate([cos, cos], axis=1), jnp.concatenate([-sin, sin], axis=1)


def on_device(layer_input, query, out_grad, camera_counts, action_counts, kv_weight):
    seq, core, dp = lax.axis_index("seq"), lax.axis_index("fsdp"), lax.axis_index("dp")
    x, y = (dp // 4) % 4, dp % 4
    tokens, queries, grads = layer_input[0], query[0], out_grad[0]
    half, width = kv_weight.shape
    prefix = camera_counts[0, 0] * IMG_TOK + TEXT
    total = prefix + action_counts[0, 0]
    meta = jnp.stack([seq, prefix, total]).astype(jnp.int32)
    spot = jnp.stack([y, core]).astype(jnp.int32)
    cos, sin = rope(seq * TOK + jnp.arange(TOK, dtype=jnp.int32))
    theirs = lax.ppermute(tokens, "fsdp", SWAP)
    which = core.astype(jnp.int32)[None]
    part_mine, part_other = [
        call(project_kernel, shape(TOK, width, F32), which, rows, kv_weight, meta=True)
        for rows in (tokens, theirs)
    ]
    tails = jnp.concatenate([queries[:TAIL], grads[:TAIL]], axis=1)
    back = lax.ppermute(part_other, "fsdp", SWAP)
    tails = lax.ppermute(tails, "seq", ACROSS)
    kv, kv_end = call(
        kv_kernel, (shape(TOK, width, BF16), shape(TAIL, width, BF16)), part_mine, back, cos, sin
    )
    kv_next = lax.ppermute(kv, "seq", NEXT)
    kv_end = lax.ppermute(kv_end, "seq", DOWN)

    span = half // 4
    kv, tokens, theirs = lax.optimization_barrier((kv, tokens, theirs))
    mains = []
    for k in range(4):
        at = core * half + ((x + k) % 4) * span
        mains.append(
            jnp.concatenate([lax.dynamic_slice_in_dim(r, at, span, 1) for r in (tokens, theirs)], axis=0)
        )
    tails, mains[2] = lax.optimization_barrier((tails, mains[2]))
    for k in (1, 2, 3):
        mains[k] = lax.ppermute(mains[k], "dp", dp_shift(dx=k))
    own, to_next, to_end = call(
        attention_kernel,
        (shape(TOK, width, F32), shape(TOK, width, BF16), shape(TAIL, width, BF16)),
        meta, queries, grads, tails, kv, kv_next, kv_end,
        meta=True,
    )
    from_next = lax.ppermute(to_next, "seq", NEXT)
    from_end = lax.ppermute(to_end, "seq", UP)
    from_next, mains = lax.optimization_barrier((from_next, mains))
    cols = width // NG
    kgs = call(kg_kernel, (shape(TOK, cols, BF16),) * NG, own, from_next, from_end, cos, sin)
    key_grads, finals = {}, {}
    for c in range(NG):
        kg = kgs[c]
        direct = [kg] + [lax.ppermute(kg, "dp", dp_shift(dx=k)) for k in (1, 2, 3)]
        swapped = [lax.ppermute(g, "fsdp", SWAP) for g in direct]
        rows = span // 4
        parts = call(
            weight_kernel, (shape(rows, cols, BF16),) * 4, spot, *mains, *direct, *swapped,
            meta=True,
            scratch=[pltpu.VMEM((span, cols), F32)],
        )
        parts = [lax.ppermute(p, ("dp", "fsdp"), y_perm(k)) for k, p in enumerate(parts)]
        key_grads[c] = (kg, swapped[0])
        if c == NG - 1:
            kg, kg_other = [jnp.concatenate([key_grads[i][j] for i in range(NG)], axis=1) for j in (0, 1)]
            in_mine = dot(kg, kv_weight, 1, 1).astype(BF16)
            in_back = lax.ppermute(dot(kg_other, kv_weight, 1, 1).astype(BF16), "fsdp", SWAP)
            parts[2], in_mine, in_back = lax.optimization_barrier((parts[2], in_mine, in_back))
        keep, give = call(
            sum_kernel, (shape(rows // 2, cols, F32), shape(rows // 2, cols, BF16)),
            spot, *parts, meta=True,
        )
        finals[c] = keep + lax.ppermute(give, "fsdp", SWAP).astype(F32)

    summed = jnp.concatenate([finals[c] for c in range(NG)], axis=1)
    head = width // 4
    parts = []
    for k in range(4):
        piece = lax.dynamic_slice_in_dim(summed, ((seq + k) % 4) * head, head, 1)
        parts.append(piece if k == 0 else piece.astype(BF16))
    for k in (2, 1, 3):
        parts[k] = lax.ppermute(parts[k], "seq", [(i, (i + k) % 4) for i in range(4)]).astype(F32)
    out = parts[0] + parts[1] + parts[2] + parts[3]

    input_grad = jnp.where(
        core == 0,
        jnp.concatenate([in_mine, in_back], axis=1),
        jnp.concatenate([in_back, in_mine], axis=1),
    )
    return input_grad[None], out / lax.axis_size(("dp", "fsdp"))


def solution(mesh):
    placed = (
        P(("dp", "fsdp"), "seq", None),
        P(("dp", "fsdp"), "seq", None),
        P(("dp", "fsdp"), "seq", None),
        P(("dp", "fsdp"), None),
        P(("dp", "fsdp"), None),
        P("fsdp", None),
    )
    return jax.shard_map(
        on_device,
        mesh=mesh,
        in_specs=placed,
        out_specs=(P(("dp", "fsdp"), "seq", None), P(("dp", "fsdp"), "seq")),
        check_vma=False,
    )
```

time: 131 us -> 107 us (0.82)
  waiting for transfers between devices: 53.4 us -> 38.3 us
  matrix products: 13.9 us -> 7 us
  starting transfers between devices: 45.3 us -> 40.5 us
  Pallas kernels: 7.58 us -> 9.4 us
    ppermute x24 -> x25, waiting for transfers between devices: 53.3 us -> 38.3 us  [the longest x1 10.9 us: on_device(): from_next = lax.ppermute(to_next, 'seq', NEXT)]
    dot_general x4 -> x2, matrix products: 13.9 us -> 7 us  [dot(): lax.dot_general(a, b, (((ca,), (cb,)), ((), ())), preferred_element_type=...]
    ppermute x24 -> x25, starting transfers between devices: 45.2 us -> 40.5 us  [the longest x3 6.97 us: on_device(): lax.ppermute(parts[k], 'seq', [(i, (i + k) % 4) for i in range(4)])]
    dynamic_slice x3 -> x2, local copies, waits for them, and re-layouts: 4.05 us -> 0.18 us  [on_device(): lax.dynamic_slice_in_dim(r, at, span, 1)]
    unnamed x16 -> x12, local copies, waits for them, and re-layouts: 0.04 us -> 2.51 us
    pallas_call x5 -> x7, Pallas kernels: 7.58 us -> 9.4 us  [call(): pl.pallas_call(kernel, grid=grid, out_shape=outs, in_specs=specs, out_spe...]
    select_n x1, other arithmetic: 1.36 us -> 2.69 us  [on_device(): jnp.where(core == 0, jnp.concatenate([in_mine, in_back], axis=1), jnp.con...]
  transfers between devices with their start and end apart: 25 -> 26, of which waited for: 11 -> 12; matrix products, arithmetic and copies ran while one was open for 12% -> 11% of each run, Pallas kernels for 1% -> 8%
where the time goes in v2:
time: 107 us; the launch traced here: 105 us
  starting transfers between devices  40.5 us (38%)
  waiting for transfers between devices  38.3 us (36%)
  Pallas kernels  9.4 us (9%)
  matrix products  7 us (7%)
  other arithmetic  4.11 us (4%)
  local copies, waits for them, and re-layouts  3.82 us (4%)
  between operations  2.3 us (2%)
    ppermute x1, waiting for transfers between devices, on_device(): from_next = lax.ppermute(to_next, 'seq', NEXT)  10.9 us
    ppermute x4, waiting for transfers between devices, on_device(): lax.ppermute(p, ('dp', 'fsdp'), y_perm(k))  9.86 us
    pallas_call x7, Pallas kernels, call(): pl.pallas_call(kernel, grid=grid, out_shape=outs, in_specs=specs, out_spe...  9.4 us
    ppermute x3, waiting for transfers between devices, on_device(): direct = [kg] + [lax.ppermute(kg, 'dp', dp_shift(dx=k)) for k in (1, 2, 3)]  8.11 us
    dot_general x2, matrix products, dot(): lax.dot_general(a, b, (((ca,), (cb,)), ((), ())), preferred_element_type=...  7 us
    ppermute x3, starting transfers between devices, on_device(): lax.ppermute(parts[k], 'seq', [(i, (i + k) % 4) for i in range(4)])  6.97 us
    ppermute x1, starting transfers between devices, on_device(): tails = lax.ppermute(tails, 'seq', ACROSS)  6.39 us
    ppermute x3, starting transfers between devices, on_device(): mains[k] = lax.ppermute(mains[k], 'dp', dp_shift(dx=k))  5.94 us
  transfers between devices with their start and end apart: 26, of which 12 were waited for; matrix products, arithmetic and copies ran while one was open for 11% of the time, Pallas kernels for 8%

profile of v2, /device:TPU:8, one launch (start us, length us, event | category | flops | bytes accessed | tf_op | source)
XLA Modules:
  0.0 105.4 jit_solution(11803230686076226177)
XLA Ops:
  0.7 1.1 %slice_bitcast_fusion = (bf16[32,2560]{1,0:T(8,128)(2,1)S(1)}, bf16[32,2560]{1,0:T(8,128)(2,1)S(1)}) fusion(bf16[1,128,2560]{2,1,0:T(8,128)(2,1)} %param.8, bf16[1,128,2560]{2,1,0:T(8,128)(2,1)} %param.7), kind=kLoop, calls=%fused_computation.9 | loop fusion | bytes 655360 | tf_op jit(solution)/shard_map/slice | solution.py:211
  1.9 6.4 %collective-permute-start = (bf16[32,5120]{1,0:T(8,128)(2,1)S(1)}, bf16[32,5120]{1,0:T(8,128)(2,1)S(1)}, u32[]{:S(2)}, u32[]{:S(2)}) collective-permute-start(bf16[32,5120]{1,0:T(8,128)(2,1)S(1)} %pad_maximum_fusion), channel_id=1, source_target_pairs={{0,6},{2,4},{4,2},{6,0},{1,7},{3,5},{5,3},{7,1},{8,14},{10,12},{12... | collective-permute-start | bytes 983048 | tf_op jit(solution)/shard_map/ppermute | solution.py:213
  9.6 2.5 %copy-done = bf16[2560,1024]{1,0:T(8,128)(2,1)S(1)} copy-done((bf16[2560,1024]{1,0:T(8,128)(2,1)S(1)}, bf16[2560,1024]{1,0:T(8,128)(2,1)}, u32[]{:S(2)}) %copy-start) | copy-done | bytes 5242904
  12.1 0.9 shard_map.77.own_ref
  13.0 0.9 shard_map.78
  13.8 0.3 collective-permute-start.2
  14.1 0.3 fusion
  14.4 0.1 pad_maximum_fusion.5
  14.6 1.3 %collective-permute-done.2.recv_ref = f32[128,1024]{1,0:T(8,128)S(1)} collective-permute-done((f32[128,1024]{1,0:T(8,128)S(1)}, f32[128,1024]{1,0:T(8,128)S(1)}, u32[]{:S(2)}, u32[]{:S(2)}) %collective-permute-start.2) | collective-permute-done | bytes 524320 | tf_op jit(solution)/shard_map/ppermute | solution.py:212
  15.8 0.2 shard_map.79
  16.0 1.5 %collective-permute-start.3 = (bf16[128,1024]{1,0:T(8,128)(2,1)S(1)}, bf16[128,1024]{1,0:T(8,128)(2,1)S(1)}, u32[]{:S(2)}, u32[]{:S(2)}) collective-permute-start(bf16[128,1024]{1,0:T(8,128)(2,1)S(1)} %get-tuple-element.30.kv_ref), channel_id=1, source_target_pairs={{0,2},{2,0},{4,6},{6,4},{1,3},{3,1},{5,7},{7,5},{8,10},{10,8},{12,... | collective-permute-start | bytes 786440 | tf_op jit(solution)/shard_map/ppermute | solution.py:217
  17.6 0.1 constant_dynamic-slice_fusion
  17.8 2.8 %collective-permute-start.8 = (bf16[256,640]{1,0:T(8,128)(2,1)S(1)}, bf16[256,640]{1,0:T(8,128)(2,1)S(1)}, u32[]{:S(2)}, u32[]{:S(2)}) collective-permute-start(bf16[256,640]{1,0:T(8,128)(2,1)S(1)} %pad_maximum_fusion.4), channel_id=1, source_target_pairs={{0,96},{8,104},{16,112},{24,120},{32,0},{40,8},{48,16},{56,24},{64... | collective-permute-start | bytes 983048 | tf_op jit(solution)/shard_map/ppermute | solution.py:230
  20.8 2.1 %collective-permute-done.tail_ref = bf16[32,5120]{1,0:T(8,128)(2,1)S(1)} collective-permute-done((bf16[32,5120]{1,0:T(8,128)(2,1)S(1)}, bf16[32,5120]{1,0:T(8,128)(2,1)S(1)}, u32[]{:S(2)}, u32[]{:S(2)}) %collective-permute-start) | collective-permute-done | bytes 327712 | tf_op jit(solution)/shard_map/ppermute | solution.py:213
  22.9 4.6 %collective-permute-start.4 = (bf16[32,1024]{1,0:T(8,128)(2,1)S(1)}, bf16[32,1024]{1,0:T(8,128)(2,1)S(1)}, u32[]{:S(2)}, u32[]{:S(2)}) collective-permute-start(bf16[32,1024]{1,0:T(8,128)(2,1)S(1)} %get-tuple-element.31), channel_id=1, source_target_pairs={{0,6},{2,0},{4,2},{6,4},{1,7},{3,1},{5,3},{7,5},{8,14},{10,8},{12,... | collective-permute-start | bytes 196616 | tf_op jit(solution)/shard_map/ppermute | solution.py:218
  27.5 3.0 %collective-permute-start.7 = (bf16[256,640]{1,0:T(8,128)(2,1)S(1)}, bf16[256,640]{1,0:T(8,128)(2,1)S(1)}, u32[]{:S(2)}, u32[]{:S(2)}) collective-permute-start(bf16[256,640]{1,0:T(8,128)(2,1)S(1)} %pad_maximum_fusion.1), channel_id=1, source_target_pairs={{0,64},{8,72},{16,80},{24,88},{32,96},{40,104},{48,112},{56,120},{... | collective-permute-start | bytes 983048 | tf_op jit(solution)/shard_map/ppermute | solution.py:230
  30.6 3.2 %collective-permute-done.4.end_ref = bf16[32,1024]{1,0:T(8,128)(2,1)S(1)} collective-permute-done((bf16[32,1024]{1,0:T(8,128)(2,1)S(1)}, bf16[32,1024]{1,0:T(8,128)(2,1)S(1)}, u32[]{:S(2)}, u32[]{:S(2)}) %collective-permute-start.4) | collective-permute-done | bytes 65568 | tf_op jit(solution)/shard_map/ppermute | solution.py:218
  33.8 4.4 %shard_map.80 = (f32[128,1024]{1,0:T(8,128)S(1)}, bf16[128,1024]{1,0:T(8,128)(2,1)S(1)}, bf16[32,1024]{1,0:T(8,128)(2,1)S(1)}) custom-call(s32[3]{0:T(128)S(1)} %pad_add_fusion.1.meta, bf16[128,2560]{1,0:T(8,128)(2,1)S(1)} %bitcast.23, bf16[128,2560]{1,0:T(8,128)(2,1)S(1)} %bitcast.24, bf16[32,5120]{1,0:T(8,128)(2,1)S(1)} %collective-permute-done.tail_ref, ...), custom_call_target="tpu_custom_call" | custom-call | tf_op jit(solution)/shard_map/pallas_call | solution.py:173
  38.2 0.1 collective-permute-start.5
  38.3 2.9 %collective-permute-start.9 = (bf16[32,1024]{1,0:T(8,128)(2,1)S(1)}, bf16[32,1024]{1,0:T(8,128)(2,1)S(1)}, u32[]{:S(2)}, u32[]{:S(2)}) collective-permute-start(bf16[32,1024]{1,0:T(8,128)(2,1)S(1)} %get-tuple-element.40), channel_id=1, source_target_pairs={{0,2},{2,4},{4,6},{6,0},{1,3},{3,5},{5,7},{7,1},{8,10},{10,12},{12... | collective-permute-start | bytes 196616 | tf_op jit(solution)/shard_map/ppermute | solution.py:238
  41.3 10.9 %collective-permute-done.5.next_ref = bf16[128,1024]{1,0:T(8,128)(2,1)S(1)} collective-permute-done((bf16[128,1024]{1,0:T(8,128)(2,1)S(1)}, bf16[128,1024]{1,0:T(8,128)(2,1)S(1)}, u32[]{:S(2)}, u32[]{:S(2)}) %collective-permute-start.5) | collective-permute-done | bytes 262176 | tf_op jit(solution)/shard_map/ppermute | solution.py:237
  52.2 0.2 shard_map.81.refs_4_
  52.4 0.1 collective-permute-start.13
  52.5 1.6 %collective-permute-start.10 = (bf16[128,1024]{1,0:T(8,128)(2,1)S(1)}, bf16[128,1024]{1,0:T(8,128)(2,1)S(1)}, u32[]{:S(2)}, u32[]{:S(2)}) collective-permute-start(bf16[128,1024]{1,0:T(8,128)(2,1)S(1)} %shard_map.81.refs_4_), channel_id=1, source_target_pairs={{0,32},{8,40},{16,48},{24,56},{32,64},{40,72},{48,80},{56,88},{64,... | collective-permute-start | bytes 786440 | tf_op jit(solution)/shard_map/ppermute | solution.py:245
  54.0 2.7 %collective-permute-start.11 = (bf16[128,1024]{1,0:T(8,128)(2,1)S(1)}, bf16[128,1024]{1,0:T(8,128)(2,1)S(1)}, u32[]{:S(2)}, u32[]{:S(2)}) collective-permute-start(bf16[128,1024]{1,0:T(8,128)(2,1)S(1)} %shard_map.81.refs_4_), channel_id=1, source_target_pairs={{0,64},{8,72},{16,80},{24,88},{32,96},{40,104},{48,112},{56,120},{... | collective-permute-start | bytes 786440 | tf_op jit(solution)/shard_map/ppermute | solution.py:245
  56.8 1.4 %collective-permute-start.12 = (bf16[128,1024]{1,0:T(8,128)(2,1)S(1)}, bf16[128,1024]{1,0:T(8,128)(2,1)S(1)}, u32[]{:S(2)}, u32[]{:S(2)}) collective-permute-start(bf16[128,1024]{1,0:T(8,128)(2,1)S(1)} %shard_map.81.refs_4_), channel_id=1, source_target_pairs={{0,96},{8,104},{16,112},{24,120},{32,0},{40,8},{48,16},{56,24},{64... | collective-permute-start | bytes 786440 | tf_op jit(solution)/shard_map/ppermute | solution.py:245
  58.2 2.7 %convolution_convert_fusion = bf16[128,2560]{1,0:T(8,128)(2,1)} fusion(bf16[128,1024]{1,0:T(8,128)(2,1)S(1)} %collective-permute-done.13.refs_8_, bf16[2560,1024]{1,0:T(8,128)(2,1)S(1)} %bitcast.19), kind=kOutput, calls=%fused_computation | convolution fusion | flops 671416320 | bytes 6160384 | tf_op jit(solution)/shard_map/dot_general | solution.py:47
  60.9 1.5 %collective-permute-done.10.refs_5_ = bf16[128,1024]{1,0:T(8,128)(2,1)S(1)} collective-permute-done((bf16[128,1024]{1,0:T(8,128)(2,1)S(1)}, bf16[128,1024]{1,0:T(8,128)(2,1)S(1)}, u32[]{:S(2)}, u32[]{:S(2)}) %collective-permute-start.10) | collective-permute-done | bytes 262176 | tf_op jit(solution)/shard_map/ppermute | solution.py:245
  62.4 6.6 %collective-permute-done.11.refs_6_ = bf16[128,1024]{1,0:T(8,128)(2,1)S(1)} collective-permute-done((bf16[128,1024]{1,0:T(8,128)(2,1)S(1)}, bf16[128,1024]{1,0:T(8,128)(2,1)S(1)}, u32[]{:S(2)}, u32[]{:S(2)}) %collective-permute-start.11) | collective-permute-done | bytes 262176 | tf_op jit(solution)/shard_map/ppermute | solution.py:245
  69.0 0.5 collective-permute-start.16
  69.6 0.9 collective-permute-done.15.refs_10_
  70.6 0.4 collective-permute-done.16.refs_11_
  70.9 2.3 %shard_map.82 = (bf16[160,1024]{1,0:T(8,128)(2,1)S(1)}, bf16[160,1024]{1,0:T(8,128)(2,1)S(1)}, bf16[160,1024]{1,0:T(8,128)(2,1)S(1)}, bf16[160,1024]{1,0:T(8,128)(2,1)S(1)}) custom-call(s32[2]{0:T(128)S(1)} %pad_add_fusion.meta, bf16[256,640]{1,0:T(8,128)(2,1)S(1)} %pad_maximum_fusion.2.refs_0_, bf16[256,640]{1,0:T(8,128)(2,1)S(1)} %collective-permute-done.6.refs_1_, ...), custom_call_target="tpu_custom_call" | custom-call | tf_op jit(solution)/shard_map/pallas_call | solution.py:173
  73.2 2.4 %collective-permute-start.17 = (bf16[160,1024]{1,0:T(8,128)(2,1)S(1)}, bf16[160,1024]{1,0:T(8,128)(2,1)S(1)}, u32[]{:S(2)}, u32[]{:S(2)}) collective-permute-start(bf16[160,1024]{1,0:T(8,128)(2,1)S(1)} %get-tuple-element.41), channel_id=1, source_target_pairs={{0,16},{1,144},{8,24},{9,152},{16,0},{17,128},{24,8},{25,136},{32,... | collective-permute-start | bytes 983048 | tf_op jit(solution)/shard_map/ppermute | solution.py:253
  75.6 0.7 collective-permute-start.19
  76.4 2.0 %collective-permute-start.21 = (bf16[160,1024]{1,0:T(8,128)(2,1)S(1)}, bf16[160,1024]{1,0:T(8,128)(2,1)S(1)}, u32[]{:S(2)}, u32[]{:S(2)}) collective-permute-start(bf16[160,1024]{1,0:T(8,128)(2,1)S(1)} %get-tuple-element.47), channel_id=1, source_target_pairs={{0,24},{1,152},{8,0},{9,128},{16,8},{17,136},{24,16},{25,144},{32,... | collective-permute-start | bytes 983048 | tf_op jit(solution)/shard_map/ppermute | solution.py:253
  78.4 4.3 %convolution_convert_fusion.1 = bf16[128,2560]{1,0:T(8,128)(2,1)S(1)} fusion(bf16[128,1024]{1,0:T(8,128)(2,1)S(1)} %shard_map.81.refs_4_, bf16[2560,1024]{1,0:T(8,128)(2,1)} %w_ref.3), kind=kOutput, calls=%fused_computation.1 | convolution fusion | flops 671416320 | bytes 6160384 | tf_op jit(solution)/shard_map/dot_general | solution.py:47
  82.7 2.8 %collective-permute-done.17.c_ref = bf16[160,1024]{1,0:T(8,128)(2,1)S(1)} collective-permute-done((bf16[160,1024]{1,0:T(8,128)(2,1)S(1)}, bf16[160,1024]{1,0:T(8,128)(2,1)S(1)}, u32[]{:S(2)}, u32[]{:S(2)}) %collective-permute-start.17) | collective-permute-done | bytes 327712 | tf_op jit(solution)/shard_map/ppermute | solution.py:253
  85.5 7.1 %collective-permute-done.20.b_ref = bf16[160,1024]{1,0:T(8,128)(2,1)S(1)} collective-permute-done((bf16[160,1024]{1,0:T(8,128)(2,1)S(1)}, bf16[160,1024]{1,0:T(8,128)(2,1)S(1)}, u32[]{:S(2)}, u32[]{:S(2)}) %collective-permute-start.20) | collective-permute-done | bytes 327712 | tf_op jit(solution)/shard_map/ppermute | solution.py:253
  92.6 0.7 shard_map.83
  93.3 0.1 collective-permute-start.22
  93.5 1.3 %collective-permute-done.22 = bf16[80,1024]{1,0:T(8,128)(2,1)S(1)} collective-permute-done((bf16[80,1024]{1,0:T(8,128)(2,1)S(1)}, bf16[80,1024]{1,0:T(8,128)(2,1)S(1)}, u32[]{:S(2)}, u32[]{:S(2)}) %collective-permute-start.22) | collective-permute-done | bytes 163872 | tf_op jit(solution)/shard_map/ppermute | solution.py:264
  94.9 0.7 collective-permute-start.23
  95.5 3.0 %collective-permute-start.24 = (bf16[80,256]{1,0:T(8,128)(2,1)S(1)}, bf16[80,256]{1,0:T(8,128)(2,1)S(1)}, u32[]{:S(2)}, u32[]{:S(2)}) collective-permute-start(bf16[80,256]{1,0:T(8,128)(2,1)S(1)} %get-tuple-element.60), channel_id=1, source_target_pairs={{0,4},{2,6},{4,0},{6,2},{1,5},{3,7},{5,1},{7,3},{8,12},{10,14},{12... | collective-permute-start | bytes 122888 | tf_op jit(solution)/shard_map/ppermute | solution.py:273
  98.5 3.4 %collective-permute-start.25 = (bf16[80,256]{1,0:T(8,128)(2,1)S(1)}, bf16[80,256]{1,0:T(8,128)(2,1)S(1)}, u32[]{:S(2)}, u32[]{:S(2)}) collective-permute-start(bf16[80,256]{1,0:T(8,128)(2,1)S(1)} %get-tuple-element.59), channel_id=1, source_target_pairs={{0,6},{2,0},{4,2},{6,4},{1,7},{3,1},{5,3},{7,5},{8,14},{10,8},{12,... | collective-permute-start | bytes 122888 | tf_op jit(solution)/shard_map/ppermute | solution.py:273
  101.8 2.7 %maximum_select_fusion = bf16[1,128,5120]{2,1,0:T(8,128)(2,1)} fusion(bf16[1,128,2560]{2,1,0:T(8,128)(2,1)} %bitcast.11, bf16[1,128,2560]{2,1,0:T(8,128)(2,1)S(1)} %bitcast.25, pred[]{:T(512)S(6)} %eq.14), kind=kLoop, calls=%fused_computation.2 | loop fusion | flops 5898240 | bytes 2621441 | tf_op jit(solution)/shard_map/jit(_where)/select_n | solution.py:276
  104.5 0.2 collective-permute-done.25
  104.7 0.7 add_multiply_fusion
  (44 shorter events, 0.8 us)
Async XLA Ops:
  0.6 8.9 %copy-start.1 = (bf16[1,128,5120]{2,1,0:T(8,128)(2,1)S(1)}, bf16[1,128,5120]{2,1,0:T(8,128)(2,1)}, u32[]{:S(2)}) copy-start(bf16[1,128,5120]{2,1,0:T(8,128)(2,1)} %param.6) | copy-start | bytes 3932164
  0.6 12.3 %collective-permute-start.1 = (bf16[128,5120]{1,0:T(8,128)(2,1)}, bf16[128,5120]{1,0:T(8,128)(2,1)S(1)}, u32[]{:S(2)}, u32[]{:S(2)}) collective-permute-start(bf16[128,5120]{1,0:T(8,128)(2,1)} %bitcast.20), channel_id=1, source_target_pairs={{0,1},{1,0},{2,3},{3,2},{4,5},{5,4},{6,7},{7,6},{8,9},{9,8},{10,11... | collective-permute-start | bytes 3932168 | tf_op jit(solution)/shard_map/ppermute | solution.py:205
  1.9 21.0 %collective-permute-start = (bf16[32,5120]{1,0:T(8,128)(2,1)S(1)}, bf16[32,5120]{1,0:T(8,128)(2,1)S(1)}, u32[]{:S(2)}, u32[]{:S(2)}) collective-permute-start(bf16[32,5120]{1,0:T(8,128)(2,1)S(1)} %pad_maximum_fusion), channel_id=1, source_target_pairs={{0,6},{2,4},{4,2},{6,0},{1,7},{3,5},{5,3},{7,1},{8,14},{10,12},{12... | collective-permute-start | bytes 983048 | tf_op jit(solution)/shard_map/ppermute | solution.py:213
  9.6 2.5 %copy-start = (bf16[2560,1024]{1,0:T(8,128)(2,1)S(1)}, bf16[2560,1024]{1,0:T(8,128)(2,1)}, u32[]{:S(2)}) copy-start(bf16[2560,1024]{1,0:T(8,128)(2,1)} %w_ref.3) | copy-start | bytes 15728644
  12.9 45.3 %slice-start = ((s8[5242880]{0:T(1024)(128)(4,1)}), s8[1048576]{0:T(1024)(128)(4,1)S(1)}, s32[]{:S(2)}) async-start(s8[5242880]{0:T(1024)(128)(4,1)} %bitcast.18), calls=%async_computation | async-start | bytes 2097152
  13.8 2.0 %collective-permute-start.2 = (f32[128,1024]{1,0:T(8,128)S(1)}, f32[128,1024]{1,0:T(8,128)S(1)}, u32[]{:S(2)}, u32[]{:S(2)}) collective-permute-start(f32[128,1024]{1,0:T(8,128)S(1)} %shard_map.78), channel_id=1, source_target_pairs={{0,1},{1,0},{2,3},{3,2},{4,5},{5,4},{6,7},{7,6},{8,9},{9,8},{10,11... | collective-permute-start | bytes 1572872 | tf_op jit(solution)/shard_map/ppermute | solution.py:212
  15.8 42.4 %slice-start.1 = ((s8[5242880]{0:T(1024)(128)(4,1)}), s8[4194304]{0:T(1024)(128)(4,1)S(1)}, s32[]{:S(2)}) async-start(s8[5242880]{0:T(1024)(128)(4,1)} %bitcast.18), calls=%async_computation.1 | async-start | bytes 8388608
  16.0 17.8 %collective-permute-start.3 = (bf16[128,1024]{1,0:T(8,128)(2,1)S(1)}, bf16[128,1024]{1,0:T(8,128)(2,1)S(1)}, u32[]{:S(2)}, u32[]{:S(2)}) collective-permute-start(bf16[128,1024]{1,0:T(8,128)(2,1)S(1)} %get-tuple-element.30.kv_ref), channel_id=1, source_target_pairs={{0,2},{2,0},{4,6},{6,4},{1,3},{3,1},{5,7},{7,5},{8,10},{10,8},{12,... | collective-permute-start | bytes 786440 | tf_op jit(solution)/shard_map/ppermute | solution.py:217
  17.7 16.1 %copy-start.2 = (bf16[1,128,2560]{2,1,0:T(8,128)(2,1)S(1)}, bf16[1,128,2560]{2,1,0:T(8,128)(2,1)}, u32[]{:S(2)}) copy-start(bf16[1,128,2560]{2,1,0:T(8,128)(2,1)} %param.7) | copy-start | bytes 1966084
  17.7 16.1 %copy-start.3 = (bf16[1,128,2560]{2,1,0:T(8,128)(2,1)S(1)}, bf16[1,128,2560]{2,1,0:T(8,128)(2,1)}, u32[]{:S(2)}) copy-start(bf16[1,128,2560]{2,1,0:T(8,128)(2,1)} %param.8) | copy-start | bytes 1966084
  17.8 23.5 %collective-permute-start.8 = (bf16[256,640]{1,0:T(8,128)(2,1)S(1)}, bf16[256,640]{1,0:T(8,128)(2,1)S(1)}, u32[]{:S(2)}, u32[]{:S(2)}) collective-permute-start(bf16[256,640]{1,0:T(8,128)(2,1)S(1)} %pad_maximum_fusion.4), channel_id=1, source_target_pairs={{0,96},{8,104},{16,112},{24,120},{32,0},{40,8},{48,16},{56,24},{64... | collective-permute-start | bytes 983048 | tf_op jit(solution)/shard_map/ppermute | solution.py:230
  20.6 20.6 %collective-permute-start.6 = (bf16[256,640]{1,0:T(8,128)(2,1)S(1)}, bf16[256,640]{1,0:T(8,128)(2,1)S(1)}, u32[]{:S(2)}, u32[]{:S(2)}) collective-permute-start(bf16[256,640]{1,0:T(8,128)(2,1)S(1)} %pad_maximum_fusion.3), channel_id=1, source_target_pairs={{0,32},{8,40},{16,48},{24,56},{32,64},{40,72},{48,80},{56,88},{64,... | collective-permute-start | bytes 983048 | tf_op jit(solution)/shard_map/ppermute | solution.py:230
  22.9 10.9 %collective-permute-start.4 = (bf16[32,1024]{1,0:T(8,128)(2,1)S(1)}, bf16[32,1024]{1,0:T(8,128)(2,1)S(1)}, u32[]{:S(2)}, u32[]{:S(2)}) collective-permute-start(bf16[32,1024]{1,0:T(8,128)(2,1)S(1)} %get-tuple-element.31), channel_id=1, source_target_pairs={{0,6},{2,0},{4,2},{6,4},{1,7},{3,1},{5,3},{7,5},{8,14},{10,8},{12,... | collective-permute-start | bytes 196616 | tf_op jit(solution)/shard_map/ppermute | solution.py:218
  27.5 13.7 %collective-permute-start.7 = (bf16[256,640]{1,0:T(8,128)(2,1)S(1)}, bf16[256,640]{1,0:T(8,128)(2,1)S(1)}, u32[]{:S(2)}, u32[]{:S(2)}) collective-permute-start(bf16[256,640]{1,0:T(8,128)(2,1)S(1)} %pad_maximum_fusion.1), channel_id=1, source_target_pairs={{0,64},{8,72},{16,80},{24,88},{32,96},{40,104},{48,112},{56,120},{... | collective-permute-start | bytes 983048 | tf_op jit(solution)/shard_map/ppermute | solution.py:230
  38.2 14.0 %collective-permute-start.5 = (bf16[128,1024]{1,0:T(8,128)(2,1)S(1)}, bf16[128,1024]{1,0:T(8,128)(2,1)S(1)}, u32[]{:S(2)}, u32[]{:S(2)}) collective-permute-start(bf16[128,1024]{1,0:T(8,128)(2,1)S(1)} %get-tuple-element.32), channel_id=1, source_target_pairs={{0,2},{2,0},{4,6},{6,4},{1,3},{3,1},{5,7},{7,5},{8,10},{10,8},{12,... | collective-permute-start | bytes 786440 | tf_op jit(solution)/shard_map/ppermute | solution.py:237
  38.3 13.9 %collective-permute-start.9 = (bf16[32,1024]{1,0:T(8,128)(2,1)S(1)}, bf16[32,1024]{1,0:T(8,128)(2,1)S(1)}, u32[]{:S(2)}, u32[]{:S(2)}) collective-permute-start(bf16[32,1024]{1,0:T(8,128)(2,1)S(1)} %get-tuple-element.40), channel_id=1, source_target_pairs={{0,2},{2,4},{4,6},{6,0},{1,3},{3,5},{5,7},{7,1},{8,10},{10,12},{12... | collective-permute-start | bytes 196616 | tf_op jit(solution)/shard_map/ppermute | solution.py:238
  52.4 5.8 %collective-permute-start.13 = (bf16[128,1024]{1,0:T(8,128)(2,1)S(1)}, bf16[128,1024]{1,0:T(8,128)(2,1)S(1)}, u32[]{:S(2)}, u32[]{:S(2)}) collective-permute-start(bf16[128,1024]{1,0:T(8,128)(2,1)S(1)} %shard_map.81.refs_4_), channel_id=1, source_target_pairs={{0,1},{1,0},{2,3},{3,2},{4,5},{5,4},{6,7},{7,6},{8,9},{9,8},{10,11... | collective-permute-start | bytes 786440 | tf_op jit(solution)/shard_map/ppermute | solution.py:246
  52.5 9.9 %collective-permute-start.10 = (bf16[128,1024]{1,0:T(8,128)(2,1)S(1)}, bf16[128,1024]{1,0:T(8,128)(2,1)S(1)}, u32[]{:S(2)}, u32[]{:S(2)}) collective-permute-start(bf16[128,1024]{1,0:T(8,128)(2,1)S(1)} %shard_map.81.refs_4_), channel_id=1, source_target_pairs={{0,32},{8,40},{16,48},{24,56},{32,64},{40,72},{48,80},{56,88},{64,... | collective-permute-start | bytes 786440 | tf_op jit(solution)/shard_map/ppermute | solution.py:245
  54.0 15.0 %collective-permute-start.11 = (bf16[128,1024]{1,0:T(8,128)(2,1)S(1)}, bf16[128,1024]{1,0:T(8,128)(2,1)S(1)}, u32[]{:S(2)}, u32[]{:S(2)}) collective-permute-start(bf16[128,1024]{1,0:T(8,128)(2,1)S(1)} %shard_map.81.refs_4_), channel_id=1, source_target_pairs={{0,64},{8,72},{16,80},{24,88},{32,96},{40,104},{48,112},{56,120},{... | collective-permute-start | bytes 786440 | tf_op jit(solution)/shard_map/ppermute | solution.py:245
  56.8 12.2 %collective-permute-start.12 = (bf16[128,1024]{1,0:T(8,128)(2,1)S(1)}, bf16[128,1024]{1,0:T(8,128)(2,1)S(1)}, u32[]{:S(2)}, u32[]{:S(2)}) collective-permute-start(bf16[128,1024]{1,0:T(8,128)(2,1)S(1)} %shard_map.81.refs_4_), channel_id=1, source_target_pairs={{0,96},{8,104},{16,112},{24,120},{32,0},{40,8},{48,16},{56,24},{64... | collective-permute-start | bytes 786440 | tf_op jit(solution)/shard_map/ppermute | solution.py:245
  60.9 24.6 %collective-permute-start.18 = (bf16[128,2560]{1,0:T(8,128)(2,1)}, bf16[128,2560]{1,0:T(8,128)(2,1)}, u32[]{:S(2)}, u32[]{:S(2)}) collective-permute-start(bf16[128,2560]{1,0:T(8,128)(2,1)} %convolution_convert_fusion), channel_id=1, source_target_pairs={{0,1},{1,0},{2,3},{3,2},{4,5},{5,4},{6,7},{7,6},{8,9},{9,8},{10,11... | collective-permute-start | bytes 1966088 | tf_op jit(solution)/shard_map/ppermute | solution.py:258
  62.4 7.2 %collective-permute-start.14 = (bf16[128,1024]{1,0:T(8,128)(2,1)S(1)}, bf16[128,1024]{1,0:T(8,128)(2,1)S(1)}, u32[]{:S(2)}, u32[]{:S(2)}) collective-permute-start(bf16[128,1024]{1,0:T(8,128)(2,1)S(1)} %collective-permute-done.10.refs_5_), channel_id=1, source_target_pairs={{0,1},{1,0},{2,3},{3,2},{4,5},{5,4},{6,7},{7,6},{8,9},{9,8},{10,11... | collective-permute-start | bytes 786440 | tf_op jit(solution)/shard_map/ppermute | solution.py:246
  69.0 1.5 %collective-permute-start.15 = (bf16[128,1024]{1,0:T(8,128)(2,1)S(1)}, bf16[128,1024]{1,0:T(8,128)(2,1)S(1)}, u32[]{:S(2)}, u32[]{:S(2)}) collective-permute-start(bf16[128,1024]{1,0:T(8,128)(2,1)S(1)} %collective-permute-done.11.refs_6_), channel_id=1, source_target_pairs={{0,1},{1,0},{2,3},{3,2},{4,5},{5,4},{6,7},{7,6},{8,9},{9,8},{10,11... | collective-permute-start | bytes 786440 | tf_op jit(solution)/shard_map/ppermute | solution.py:246
  69.0 1.9 %collective-permute-start.16 = (bf16[128,1024]{1,0:T(8,128)(2,1)S(1)}, bf16[128,1024]{1,0:T(8,128)(2,1)S(1)}, u32[]{:S(2)}, u32[]{:S(2)}) collective-permute-start(bf16[128,1024]{1,0:T(8,128)(2,1)S(1)} %collective-permute-done.12.refs_7_), channel_id=1, source_target_pairs={{0,1},{1,0},{2,3},{3,2},{4,5},{5,4},{6,7},{7,6},{8,9},{9,8},{10,11... | collective-permute-start | bytes 786440 | tf_op jit(solution)/shard_map/ppermute | solution.py:246
  73.2 12.3 %collective-permute-start.17 = (bf16[160,1024]{1,0:T(8,128)(2,1)S(1)}, bf16[160,1024]{1,0:T(8,128)(2,1)S(1)}, u32[]{:S(2)}, u32[]{:S(2)}) collective-permute-start(bf16[160,1024]{1,0:T(8,128)(2,1)S(1)} %get-tuple-element.41), channel_id=1, source_target_pairs={{0,16},{1,144},{8,24},{9,152},{16,0},{17,128},{24,8},{25,136},{32,... | collective-permute-start | bytes 983048 | tf_op jit(solution)/shard_map/ppermute | solution.py:253
  75.6 9.9 %collective-permute-start.19 = (bf16[160,1024]{1,0:T(8,128)(2,1)S(1)}, bf16[160,1024]{1,0:T(8,128)(2,1)S(1)}, u32[]{:S(2)}, u32[]{:S(2)}) collective-permute-start(bf16[160,1024]{1,0:T(8,128)(2,1)S(1)} %get-tuple-element.44), channel_id=1, source_target_pairs={{0,0},{1,128},{8,8},{9,136},{16,16},{17,144},{24,24},{25,152},{32,... | collective-permute-start | bytes 983048 | tf_op jit(solution)/shard_map/ppermute | solution.py:253
  76.3 16.3 %collective-permute-start.20 = (bf16[160,1024]{1,0:T(8,128)(2,1)S(1)}, bf16[160,1024]{1,0:T(8,128)(2,1)S(1)}, u32[]{:S(2)}, u32[]{:S(2)}) collective-permute-start(bf16[160,1024]{1,0:T(8,128)(2,1)S(1)} %get-tuple-element.45), channel_id=1, source_target_pairs={{0,8},{1,136},{8,16},{9,144},{16,24},{17,152},{24,0},{25,128},{32,... | collective-permute-start | bytes 983048 | tf_op jit(solution)/shard_map/ppermute | solution.py:253
  76.4 16.2 %collective-permute-start.21 = (bf16[160,1024]{1,0:T(8,128)(2,1)S(1)}, bf16[160,1024]{1,0:T(8,128)(2,1)S(1)}, u32[]{:S(2)}, u32[]{:S(2)}) collective-permute-start(bf16[160,1024]{1,0:T(8,128)(2,1)S(1)} %get-tuple-element.47), channel_id=1, source_target_pairs={{0,24},{1,152},{8,0},{9,128},{16,8},{17,136},{24,16},{25,144},{32,... | collective-permute-start | bytes 983048 | tf_op jit(solution)/shard_map/ppermute | solution.py:253
  93.3 1.5 %collective-permute-start.22 = (bf16[80,1024]{1,0:T(8,128)(2,1)S(1)}, bf16[80,1024]{1,0:T(8,128)(2,1)S(1)}, u32[]{:S(2)}, u32[]{:S(2)}) collective-permute-start(bf16[80,1024]{1,0:T(8,128)(2,1)S(1)} %get-tuple-element.49), channel_id=1, source_target_pairs={{0,1},{1,0},{2,3},{3,2},{4,5},{5,4},{6,7},{7,6},{8,9},{9,8},{10,11... | collective-permute-start | bytes 491528 | tf_op jit(solution)/shard_map/ppermute | solution.py:264
  94.9 9.7 %collective-permute-start.23 = (bf16[80,256]{1,0:T(8,128)(2,1)S(1)}, bf16[80,256]{1,0:T(8,128)(2,1)S(1)}, u32[]{:S(2)}, u32[]{:S(2)}) collective-permute-start(bf16[80,256]{1,0:T(8,128)(2,1)S(1)} %get-tuple-element.58), channel_id=1, source_target_pairs={{0,2},{2,4},{4,6},{6,0},{1,3},{3,5},{5,7},{7,1},{8,10},{10,12},{12... | collective-permute-start | bytes 122888 | tf_op jit(solution)/shard_map/ppermute | solution.py:273
  95.5 9.0 %collective-permute-start.24 = (bf16[80,256]{1,0:T(8,128)(2,1)S(1)}, bf16[80,256]{1,0:T(8,128)(2,1)S(1)}, u32[]{:S(2)}, u32[]{:S(2)}) collective-permute-start(bf16[80,256]{1,0:T(8,128)(2,1)S(1)} %get-tuple-element.60), channel_id=1, source_target_pairs={{0,4},{2,6},{4,0},{6,2},{1,5},{3,7},{5,1},{7,3},{8,12},{10,14},{12... | collective-permute-start | bytes 122888 | tf_op jit(solution)/shard_map/ppermute | solution.py:273
  98.5 6.2 %collective-permute-start.25 = (bf16[80,256]{1,0:T(8,128)(2,1)S(1)}, bf16[80,256]{1,0:T(8,128)(2,1)S(1)}, u32[]{:S(2)}, u32[]{:S(2)}) collective-permute-start(bf16[80,256]{1,0:T(8,128)(2,1)S(1)} %get-tuple-element.59), channel_id=1, source_target_pairs={{0,6},{2,0},{4,2},{6,4},{1,7},{3,1},{5,3},{7,5},{8,14},{10,8},{12,... | collective-permute-start | bytes 122888 | tf_op jit(solution)/shard_map/ppermute | solution.py:273

commit v3 on v2

--- a/solution.py
+++ b/solution.py
@@ -20,8 +20,8 @@
 F32 = jnp.float32
 BF16 = jnp.bfloat16
 SWAP = ((0, 1), (1, 0))
-DOWN = ((0, 3), (1, 0), (2, 1), (3, 2))
-UP = ((0, 1), (1, 2), (2, 3), (3, 0))
+TAIL_DOWN = ((2, 1),)
+TAIL_BACK = ((1, 2),)
 NEXT = ((0, 1), (1, 0), (2, 3), (3, 2))
 ACROSS = ((0, 3), (1, 2), (2, 1), (3, 0))
 
@@ -215,7 +215,7 @@
         kv_kernel, (shape(TOK, width, BF16), shape(TAIL, width, BF16)), part_mine, back, cos, sin
     )
     kv_next = lax.ppermute(kv, "seq", NEXT)
-    kv_end = lax.ppermute(kv_end, "seq", DOWN)
+    kv_end = lax.ppermute(kv_end, "seq", TAIL_DOWN)
 
     span = half // 4
     kv, tokens, theirs = lax.optimization_barrier((kv, tokens, theirs))
@@ -235,7 +235,7 @@
         meta=True,
     )
     from_next = lax.ppermute(to_next, "seq", NEXT)
-    from_end = lax.ppermute(to_end, "seq", UP)
+    from_end = lax.ppermute(to_end, "seq", TAIL_BACK)
     from_next, mains = lax.optimization_barrier((from_next, mains))
     cols = width // NG
     kgs = call(kg_kernel, (shape(TOK, cols, BF16),) * NG, own, from_next, from_end, cos, sin)

time: 107 us -> 104 us (0.972)
  starting transfers between devices: 40.5 us -> 36.9 us
    ppermute x2, starting transfers between devices: 7.56 us -> 1.31 us  [the longest x1 0.65 us: on_device(): from_end = lax.ppermute(to_end, 'seq', TAIL_BACK)]
    ppermute x1, waiting for transfers between devices: 0.01 us -> 4.27 us  [on_device(): kv_next = lax.ppermute(kv, 'seq', NEXT)]
    ppermute x2, waiting for transfers between devices: 3.18 us -> 0.01 us  [the longest x1 0.01 us: on_device(): from_end = lax.ppermute(to_end, 'seq', TAIL_BACK)]
    ppermute x1, starting transfers between devices: 0.09 us -> 3.05 us  [on_device(): from_next = lax.ppermute(to_next, 'seq', NEXT)]
where the time goes in v3:
time: 104 us; the launch traced here: 102 us
  waiting for transfers between devices  38.7 us (37%)
  starting transfers between devices  36.9 us (35%)
  Pallas kernels  9.39 us (9%)
  matrix products  7.01 us (7%)
  other arithmetic  4.11 us (4%)
  local copies, waits for them, and re-layouts  3.82 us (4%)
  between operations  2.31 us (2%)
    ppermute x1, waiting for transfers between devices, on_device(): from_next = lax.ppermute(to_next, 'seq', NEXT)  10.2 us
    ppermute x4, waiting for transfers between devices, on_device(): lax.ppermute(p, ('dp', 'fsdp'), y_perm(k))  9.86 us
    pallas_call x7, Pallas kernels, call(): pl.pallas_call(kernel, grid=grid, out_shape=outs, in_specs=specs, out_spe...  9.39 us
    ppermute x3, waiting for transfers between devices, on_device(): direct = [kg] + [lax.ppermute(kg, 'dp', dp_shift(dx=k)) for k in (1, 2, 3)]  7.9 us
    dot_general x2, matrix products, dot(): lax.dot_general(a, b, (((ca,), (cb,)), ((), ())), preferred_element_type=...  7.01 us
    ppermute x3, starting transfers between devices, on_device(): lax.ppermute(parts[k], 'seq', [(i, (i + k) % 4) for i in range(4)])  6.45 us
    ppermute x1, starting transfers between devices, on_device(): tails = lax.ppermute(tails, 'seq', ACROSS)  6.39 us
    ppermute x3, starting transfers between devices, on_device(): mains[k] = lax.ppermute(mains[k], 'dp', dp_shift(dx=k))  6.03 us
  transfers between devices with their start and end apart: 26, of which 12 were waited for; matrix products, arithmetic and copies ran while one was open for 11% of the time, Pallas kernels for 8%

profile of v3, /device:TPU:8, one launch (start us, length us, event | category | flops | bytes accessed | tf_op | source)
XLA Modules:
  0.0 102.3 jit_solution(2102514419713435295)
XLA Ops:
  0.6 0.1 collective-permute-start.1
  0.7 1.1 %slice_bitcast_fusion = (bf16[32,2560]{1,0:T(8,128)(2,1)S(1)}, bf16[32,2560]{1,0:T(8,128)(2,1)S(1)}) fusion(bf16[1,128,2560]{2,1,0:T(8,128)(2,1)} %param.8, bf16[1,128,2560]{2,1,0:T(8,128)(2,1)} %param.7), kind=kLoop, calls=%fused_computation.9 | loop fusion | bytes 655360 | tf_op jit(solution)/shard_map/slice | solution.py:211
  1.9 6.4 %collective-permute-start = (bf16[32,5120]{1,0:T(8,128)(2,1)S(1)}, bf16[32,5120]{1,0:T(8,128)(2,1)S(1)}, u32[]{:S(2)}, u32[]{:S(2)}) collective-permute-start(bf16[32,5120]{1,0:T(8,128)(2,1)S(1)} %pad_maximum_fusion), channel_id=1, source_target_pairs={{0,6},{2,4},{4,2},{6,0},{1,7},{3,5},{5,3},{7,1},{8,14},{10,12},{12... | collective-permute-start | bytes 983048 | tf_op jit(solution)/shard_map/ppermute | solution.py:213
  9.6 2.5 %copy-done = bf16[2560,1024]{1,0:T(8,128)(2,1)S(1)} copy-done((bf16[2560,1024]{1,0:T(8,128)(2,1)S(1)}, bf16[2560,1024]{1,0:T(8,128)(2,1)}, u32[]{:S(2)}) %copy-start) | copy-done | bytes 5242904
  12.1 0.9 shard_map.77.own_ref
  13.0 0.9 shard_map.78
  13.8 0.3 collective-permute-start.2
  14.1 0.3 fusion
  14.4 0.1 pad_maximum_fusion.5
  14.6 1.3 %collective-permute-done.2.recv_ref = f32[128,1024]{1,0:T(8,128)S(1)} collective-permute-done((f32[128,1024]{1,0:T(8,128)S(1)}, f32[128,1024]{1,0:T(8,128)S(1)}, u32[]{:S(2)}, u32[]{:S(2)}) %collective-permute-start.2) | collective-permute-done | bytes 524320 | tf_op jit(solution)/shard_map/ppermute | solution.py:212
  15.8 0.2 shard_map.79
  16.0 1.5 %collective-permute-start.3 = (bf16[128,1024]{1,0:T(8,128)(2,1)S(1)}, bf16[128,1024]{1,0:T(8,128)(2,1)S(1)}, u32[]{:S(2)}, u32[]{:S(2)}) collective-permute-start(bf16[128,1024]{1,0:T(8,128)(2,1)S(1)} %get-tuple-element.30.kv_ref), channel_id=1, source_target_pairs={{0,2},{2,0},{4,6},{6,4},{1,3},{3,1},{5,7},{7,5},{8,10},{10,8},{12,... | collective-permute-start | bytes 786440 | tf_op jit(solution)/shard_map/ppermute | solution.py:217
  17.6 0.1 constant_dynamic-slice_fusion
  17.8 2.8 %collective-permute-start.8 = (bf16[256,640]{1,0:T(8,128)(2,1)S(1)}, bf16[256,640]{1,0:T(8,128)(2,1)S(1)}, u32[]{:S(2)}, u32[]{:S(2)}) collective-permute-start(bf16[256,640]{1,0:T(8,128)(2,1)S(1)} %pad_maximum_fusion.4), channel_id=1, source_target_pairs={{0,96},{8,104},{16,112},{24,120},{32,0},{40,8},{48,16},{56,24},{64... | collective-permute-start | bytes 983048 | tf_op jit(solution)/shard_map/ppermute | solution.py:230
  20.8 2.1 %collective-permute-done.tail_ref = bf16[32,5120]{1,0:T(8,128)(2,1)S(1)} collective-permute-done((bf16[32,5120]{1,0:T(8,128)(2,1)S(1)}, bf16[32,5120]{1,0:T(8,128)(2,1)S(1)}, u32[]{:S(2)}, u32[]{:S(2)}) %collective-permute-start) | collective-permute-done | bytes 327712 | tf_op jit(solution)/shard_map/ppermute | solution.py:213
  22.9 0.7 collective-permute-start.4
  23.6 3.1 %collective-permute-start.7 = (bf16[256,640]{1,0:T(8,128)(2,1)S(1)}, bf16[256,640]{1,0:T(8,128)(2,1)S(1)}, u32[]{:S(2)}, u32[]{:S(2)}) collective-permute-start(bf16[256,640]{1,0:T(8,128)(2,1)S(1)} %pad_maximum_fusion.1), channel_id=1, source_target_pairs={{0,64},{8,72},{16,80},{24,88},{32,96},{40,104},{48,112},{56,120},{... | collective-permute-start | bytes 983048 | tf_op jit(solution)/shard_map/ppermute | solution.py:230
  26.7 4.3 %collective-permute-done.3.next_ref = bf16[128,1024]{1,0:T(8,128)(2,1)S(1)} collective-permute-done((bf16[128,1024]{1,0:T(8,128)(2,1)S(1)}, bf16[128,1024]{1,0:T(8,128)(2,1)S(1)}, u32[]{:S(2)}, u32[]{:S(2)}) %collective-permute-start.3) | collective-permute-done | bytes 262176 | tf_op jit(solution)/shard_map/ppermute | solution.py:217
  31.0 4.4 %shard_map.80 = (f32[128,1024]{1,0:T(8,128)S(1)}, bf16[128,1024]{1,0:T(8,128)(2,1)S(1)}, bf16[32,1024]{1,0:T(8,128)(2,1)S(1)}) custom-call(s32[3]{0:T(128)S(1)} %pad_add_fusion.1.meta, bf16[128,2560]{1,0:T(8,128)(2,1)S(1)} %bitcast.23, bf16[128,2560]{1,0:T(8,128)(2,1)S(1)} %bitcast.24, bf16[32,5120]{1,0:T(8,128)(2,1)S(1)} %collective-permute-done.tail_ref, ...), custom_call_target="tpu_custom_call" | custom-call | tf_op jit(solution)/shard_map/pallas_call | solution.py:173
  35.4 3.0 %collective-permute-start.5 = (bf16[128,1024]{1,0:T(8,128)(2,1)S(1)}, bf16[128,1024]{1,0:T(8,128)(2,1)S(1)}, u32[]{:S(2)}, u32[]{:S(2)}) collective-permute-start(bf16[128,1024]{1,0:T(8,128)(2,1)S(1)} %get-tuple-element.32), channel_id=1, source_target_pairs={{0,2},{2,0},{4,6},{6,4},{1,3},{3,1},{5,7},{7,5},{8,10},{10,8},{12,... | collective-permute-start | bytes 786440 | tf_op jit(solution)/shard_map/ppermute | solution.py:237
  38.4 0.7 collective-permute-start.9
  39.2 10.2 %collective-permute-done.5.next_ref = bf16[128,1024]{1,0:T(8,128)(2,1)S(1)} collective-permute-done((bf16[128,1024]{1,0:T(8,128)(2,1)S(1)}, bf16[128,1024]{1,0:T(8,128)(2,1)S(1)}, u32[]{:S(2)}, u32[]{:S(2)}) %collective-permute-start.5) | collective-permute-done | bytes 262176 | tf_op jit(solution)/shard_map/ppermute | solution.py:237
  49.4 0.2 shard_map.81.refs_4_
  49.5 0.1 collective-permute-start.13
  49.6 1.7 %collective-permute-start.10 = (bf16[128,1024]{1,0:T(8,128)(2,1)S(1)}, bf16[128,1024]{1,0:T(8,128)(2,1)S(1)}, u32[]{:S(2)}, u32[]{:S(2)}) collective-permute-start(bf16[128,1024]{1,0:T(8,128)(2,1)S(1)} %shard_map.81.refs_4_), channel_id=1, source_target_pairs={{0,32},{8,40},{16,48},{24,56},{32,64},{40,72},{48,80},{56,88},{64,... | collective-permute-start | bytes 786440 | tf_op jit(solution)/shard_map/ppermute | solution.py:245
  51.4 2.7 %collective-permute-start.11 = (bf16[128,1024]{1,0:T(8,128)(2,1)S(1)}, bf16[128,1024]{1,0:T(8,128)(2,1)S(1)}, u32[]{:S(2)}, u32[]{:S(2)}) collective-permute-start(bf16[128,1024]{1,0:T(8,128)(2,1)S(1)} %shard_map.81.refs_4_), channel_id=1, source_target_pairs={{0,64},{8,72},{16,80},{24,88},{32,96},{40,104},{48,112},{56,120},{... | collective-permute-start | bytes 786440 | tf_op jit(solution)/shard_map/ppermute | solution.py:245
  54.1 1.4 %collective-permute-start.12 = (bf16[128,1024]{1,0:T(8,128)(2,1)S(1)}, bf16[128,1024]{1,0:T(8,128)(2,1)S(1)}, u32[]{:S(2)}, u32[]{:S(2)}) collective-permute-start(bf16[128,1024]{1,0:T(8,128)(2,1)S(1)} %shard_map.81.refs_4_), channel_id=1, source_target_pairs={{0,96},{8,104},{16,112},{24,120},{32,0},{40,8},{48,16},{56,24},{64... | collective-permute-start | bytes 786440 | tf_op jit(solution)/shard_map/ppermute | solution.py:245
  55.6 2.7 %convolution_convert_fusion = bf16[128,2560]{1,0:T(8,128)(2,1)} fusion(bf16[128,1024]{1,0:T(8,128)(2,1)S(1)} %collective-permute-done.13.refs_8_, bf16[2560,1024]{1,0:T(8,128)(2,1)S(1)} %bitcast.19), kind=kOutput, calls=%fused_computation | convolution fusion | flops 671416320 | bytes 6160384 | tf_op jit(solution)/shard_map/dot_general | solution.py:47
  58.2 1.3 %collective-permute-done.10.refs_5_ = bf16[128,1024]{1,0:T(8,128)(2,1)S(1)} collective-permute-done((bf16[128,1024]{1,0:T(8,128)(2,1)S(1)}, bf16[128,1024]{1,0:T(8,128)(2,1)S(1)}, u32[]{:S(2)}, u32[]{:S(2)}) %collective-permute-start.10) | collective-permute-done | bytes 262176 | tf_op jit(solution)/shard_map/ppermute | solution.py:245
  59.5 6.6 %collective-permute-done.11.refs_6_ = bf16[128,1024]{1,0:T(8,128)(2,1)S(1)} collective-permute-done((bf16[128,1024]{1,0:T(8,128)(2,1)S(1)}, bf16[128,1024]{1,0:T(8,128)(2,1)S(1)}, u32[]{:S(2)}, u32[]{:S(2)}) %collective-permute-start.11) | collective-permute-done | bytes 262176 | tf_op jit(solution)/shard_map/ppermute | solution.py:245
  66.1 0.5 collective-permute-start.16
  66.7 0.9 collective-permute-done.15.refs_10_
  67.7 0.4 collective-permute-done.16.refs_11_
  68.1 2.3 %shard_map.82 = (bf16[160,1024]{1,0:T(8,128)(2,1)S(1)}, bf16[160,1024]{1,0:T(8,128)(2,1)S(1)}, bf16[160,1024]{1,0:T(8,128)(2,1)S(1)}, bf16[160,1024]{1,0:T(8,128)(2,1)S(1)}) custom-call(s32[2]{0:T(128)S(1)} %pad_add_fusion.meta, bf16[256,640]{1,0:T(8,128)(2,1)S(1)} %pad_maximum_fusion.2.refs_0_, bf16[256,640]{1,0:T(8,128)(2,1)S(1)} %collective-permute-done.6.refs_1_, ...), custom_call_target="tpu_custom_call" | custom-call | tf_op jit(solution)/shard_map/pallas_call | solution.py:173
  70.3 2.4 %collective-permute-start.17 = (bf16[160,1024]{1,0:T(8,128)(2,1)S(1)}, bf16[160,1024]{1,0:T(8,128)(2,1)S(1)}, u32[]{:S(2)}, u32[]{:S(2)}) collective-permute-start(bf16[160,1024]{1,0:T(8,128)(2,1)S(1)} %get-tuple-element.41), channel_id=1, source_target_pairs={{0,16},{1,144},{8,24},{9,152},{16,0},{17,128},{24,8},{25,136},{32,... | collective-permute-start | bytes 983048 | tf_op jit(solution)/shard_map/ppermute | solution.py:253
  72.7 0.7 collective-permute-start.19
  73.5 2.0 %collective-permute-start.21 = (bf16[160,1024]{1,0:T(8,128)(2,1)S(1)}, bf16[160,1024]{1,0:T(8,128)(2,1)S(1)}, u32[]{:S(2)}, u32[]{:S(2)}) collective-permute-start(bf16[160,1024]{1,0:T(8,128)(2,1)S(1)} %get-tuple-element.47), channel_id=1, source_target_pairs={{0,24},{1,152},{8,0},{9,128},{16,8},{17,136},{24,16},{25,144},{32,... | collective-permute-start | bytes 983048 | tf_op jit(solution)/shard_map/ppermute | solution.py:253
  75.5 4.3 %convolution_convert_fusion.1 = bf16[128,2560]{1,0:T(8,128)(2,1)S(1)} fusion(bf16[128,1024]{1,0:T(8,128)(2,1)S(1)} %shard_map.81.refs_4_, bf16[2560,1024]{1,0:T(8,128)(2,1)} %w_ref.3), kind=kOutput, calls=%fused_computation.1 | convolution fusion | flops 671416320 | bytes 6160384 | tf_op jit(solution)/shard_map/dot_general | solution.py:47
  79.8 2.8 %collective-permute-done.17.c_ref = bf16[160,1024]{1,0:T(8,128)(2,1)S(1)} collective-permute-done((bf16[160,1024]{1,0:T(8,128)(2,1)S(1)}, bf16[160,1024]{1,0:T(8,128)(2,1)S(1)}, u32[]{:S(2)}, u32[]{:S(2)}) %collective-permute-start.17) | collective-permute-done | bytes 327712 | tf_op jit(solution)/shard_map/ppermute | solution.py:253
  82.6 7.1 %collective-permute-done.20.b_ref = bf16[160,1024]{1,0:T(8,128)(2,1)S(1)} collective-permute-done((bf16[160,1024]{1,0:T(8,128)(2,1)S(1)}, bf16[160,1024]{1,0:T(8,128)(2,1)S(1)}, u32[]{:S(2)}, u32[]{:S(2)}) %collective-permute-start.20) | collective-permute-done | bytes 327712 | tf_op jit(solution)/shard_map/ppermute | solution.py:253
  89.7 0.7 shard_map.83
  90.4 0.1 collective-permute-start.22
  90.6 1.3 %collective-permute-done.22 = bf16[80,1024]{1,0:T(8,128)(2,1)S(1)} collective-permute-done((bf16[80,1024]{1,0:T(8,128)(2,1)S(1)}, bf16[80,1024]{1,0:T(8,128)(2,1)S(1)}, u32[]{:S(2)}, u32[]{:S(2)}) %collective-permute-start.22) | collective-permute-done | bytes 163872 | tf_op jit(solution)/shard_map/ppermute | solution.py:264
  92.1 2.3 %collective-permute-start.24 = (bf16[80,256]{1,0:T(8,128)(2,1)S(1)}, bf16[80,256]{1,0:T(8,128)(2,1)S(1)}, u32[]{:S(2)}, u32[]{:S(2)}) collective-permute-start(bf16[80,256]{1,0:T(8,128)(2,1)S(1)} %get-tuple-element.60), channel_id=1, source_target_pairs={{0,4},{2,6},{4,0},{6,2},{1,5},{3,7},{5,1},{7,3},{8,12},{10,14},{12... | collective-permute-start | bytes 122888 | tf_op jit(solution)/shard_map/ppermute | solution.py:273
  94.4 4.0 %collective-permute-start.25 = (bf16[80,256]{1,0:T(8,128)(2,1)S(1)}, bf16[80,256]{1,0:T(8,128)(2,1)S(1)}, u32[]{:S(2)}, u32[]{:S(2)}) collective-permute-start(bf16[80,256]{1,0:T(8,128)(2,1)S(1)} %get-tuple-element.59), channel_id=1, source_target_pairs={{0,6},{2,0},{4,2},{6,4},{1,7},{3,1},{5,3},{7,5},{8,14},{10,8},{12,... | collective-permute-start | bytes 122888 | tf_op jit(solution)/shard_map/ppermute | solution.py:273
  98.5 2.7 %maximum_select_fusion = bf16[1,128,5120]{2,1,0:T(8,128)(2,1)} fusion(bf16[1,128,2560]{2,1,0:T(8,128)(2,1)} %bitcast.11, bf16[1,128,2560]{2,1,0:T(8,128)(2,1)S(1)} %bitcast.25, pred[]{:T(512)S(6)} %eq.14), kind=kLoop, calls=%fused_computation.2 | loop fusion | flops 5898240 | bytes 2621441 | tf_op jit(solution)/shard_map/jit(_where)/select_n | solution.py:276
  101.2 0.5 collective-permute-done.25
  101.6 0.7 add_multiply_fusion
  (44 shorter events, 0.8 us)
Async XLA Ops:
  0.6 8.9 %copy-start.1 = (bf16[1,128,5120]{2,1,0:T(8,128)(2,1)S(1)}, bf16[1,128,5120]{2,1,0:T(8,128)(2,1)}, u32[]{:S(2)}) copy-start(bf16[1,128,5120]{2,1,0:T(8,128)(2,1)} %param.6) | copy-start | bytes 3932164
  0.6 12.3 %collective-permute-start.1 = (bf16[128,5120]{1,0:T(8,128)(2,1)}, bf16[128,5120]{1,0:T(8,128)(2,1)S(1)}, u32[]{:S(2)}, u32[]{:S(2)}) collective-permute-start(bf16[128,5120]{1,0:T(8,128)(2,1)} %bitcast.20), channel_id=1, source_target_pairs={{0,1},{1,0},{2,3},{3,2},{4,5},{5,4},{6,7},{7,6},{8,9},{9,8},{10,11... | collective-permute-start | bytes 3932168 | tf_op jit(solution)/shard_map/ppermute | solution.py:205
  1.9 21.0 %collective-permute-start = (bf16[32,5120]{1,0:T(8,128)(2,1)S(1)}, bf16[32,5120]{1,0:T(8,128)(2,1)S(1)}, u32[]{:S(2)}, u32[]{:S(2)}) collective-permute-start(bf16[32,5120]{1,0:T(8,128)(2,1)S(1)} %pad_maximum_fusion), channel_id=1, source_target_pairs={{0,6},{2,4},{4,2},{6,0},{1,7},{3,5},{5,3},{7,1},{8,14},{10,12},{12... | collective-permute-start | bytes 983048 | tf_op jit(solution)/shard_map/ppermute | solution.py:213
  9.6 2.5 %copy-start = (bf16[2560,1024]{1,0:T(8,128)(2,1)S(1)}, bf16[2560,1024]{1,0:T(8,128)(2,1)}, u32[]{:S(2)}) copy-start(bf16[2560,1024]{1,0:T(8,128)(2,1)} %w_ref.3) | copy-start | bytes 15728644
  12.9 42.6 %slice-start = ((s8[5242880]{0:T(1024)(128)(4,1)}), s8[1048576]{0:T(1024)(128)(4,1)S(1)}, s32[]{:S(2)}) async-start(s8[5242880]{0:T(1024)(128)(4,1)} %bitcast.18), calls=%async_computation | async-start | bytes 2097152
  13.8 2.0 %collective-permute-start.2 = (f32[128,1024]{1,0:T(8,128)S(1)}, f32[128,1024]{1,0:T(8,128)S(1)}, u32[]{:S(2)}, u32[]{:S(2)}) collective-permute-start(f32[128,1024]{1,0:T(8,128)S(1)} %shard_map.78), channel_id=1, source_target_pairs={{0,1},{1,0},{2,3},{3,2},{4,5},{5,4},{6,7},{7,6},{8,9},{9,8},{10,11... | collective-permute-start | bytes 1572872 | tf_op jit(solution)/shard_map/ppermute | solution.py:212
  15.8 39.7 %slice-start.1 = ((s8[5242880]{0:T(1024)(128)(4,1)}), s8[4194304]{0:T(1024)(128)(4,1)S(1)}, s32[]{:S(2)}) async-start(s8[5242880]{0:T(1024)(128)(4,1)} %bitcast.18), calls=%async_computation.1 | async-start | bytes 8388608
  16.0 15.0 %collective-permute-start.3 = (bf16[128,1024]{1,0:T(8,128)(2,1)S(1)}, bf16[128,1024]{1,0:T(8,128)(2,1)S(1)}, u32[]{:S(2)}, u32[]{:S(2)}) collective-permute-start(bf16[128,1024]{1,0:T(8,128)(2,1)S(1)} %get-tuple-element.30.kv_ref), channel_id=1, source_target_pairs={{0,2},{2,0},{4,6},{6,4},{1,3},{3,1},{5,7},{7,5},{8,10},{10,8},{12,... | collective-permute-start | bytes 786440 | tf_op jit(solution)/shard_map/ppermute | solution.py:217
  17.7 13.3 %copy-start.2 = (bf16[1,128,2560]{2,1,0:T(8,128)(2,1)S(1)}, bf16[1,128,2560]{2,1,0:T(8,128)(2,1)}, u32[]{:S(2)}) copy-start(bf16[1,128,2560]{2,1,0:T(8,128)(2,1)} %param.7) | copy-start | bytes 1966084
  17.7 13.3 %copy-start.3 = (bf16[1,128,2560]{2,1,0:T(8,128)(2,1)S(1)}, bf16[1,128,2560]{2,1,0:T(8,128)(2,1)}, u32[]{:S(2)}) copy-start(bf16[1,128,2560]{2,1,0:T(8,128)(2,1)} %param.8) | copy-start | bytes 1966084
  17.8 21.3 %collective-permute-start.8 = (bf16[256,640]{1,0:T(8,128)(2,1)S(1)}, bf16[256,640]{1,0:T(8,128)(2,1)S(1)}, u32[]{:S(2)}, u32[]{:S(2)}) collective-permute-start(bf16[256,640]{1,0:T(8,128)(2,1)S(1)} %pad_maximum_fusion.4), channel_id=1, source_target_pairs={{0,96},{8,104},{16,112},{24,120},{32,0},{40,8},{48,16},{56,24},{64... | collective-permute-start | bytes 983048 | tf_op jit(solution)/shard_map/ppermute | solution.py:230
  20.6 18.5 %collective-permute-start.6 = (bf16[256,640]{1,0:T(8,128)(2,1)S(1)}, bf16[256,640]{1,0:T(8,128)(2,1)S(1)}, u32[]{:S(2)}, u32[]{:S(2)}) collective-permute-start(bf16[256,640]{1,0:T(8,128)(2,1)S(1)} %pad_maximum_fusion.3), channel_id=1, source_target_pairs={{0,32},{8,40},{16,48},{24,56},{32,64},{40,72},{48,80},{56,88},{64,... | collective-permute-start | bytes 983048 | tf_op jit(solution)/shard_map/ppermute | solution.py:230
  22.9 3.9 %collective-permute-start.4 = (bf16[32,1024]{1,0:T(8,128)(2,1)S(1)}, bf16[32,1024]{1,0:T(8,128)(2,1)S(1)}, u32[]{:S(2)}, u32[]{:S(2)}) collective-permute-start(bf16[32,1024]{1,0:T(8,128)(2,1)S(1)} %get-tuple-element.31), channel_id=1, source_target_pairs={{4,2},{5,3},{12,10},{13,11},{20,18},{21,19},{28,26},{29,27},{36,34... | collective-permute-start | bytes 196616 | tf_op jit(solution)/shard_map/ppermute | solution.py:218
  23.6 15.6 %collective-permute-start.7 = (bf16[256,640]{1,0:T(8,128)(2,1)S(1)}, bf16[256,640]{1,0:T(8,128)(2,1)S(1)}, u32[]{:S(2)}, u32[]{:S(2)}) collective-permute-start(bf16[256,640]{1,0:T(8,128)(2,1)S(1)} %pad_maximum_fusion.1), channel_id=1, source_target_pairs={{0,64},{8,72},{16,80},{24,88},{32,96},{40,104},{48,112},{56,120},{... | collective-permute-start | bytes 983048 | tf_op jit(solution)/shard_map/ppermute | solution.py:230
  35.4 14.0 %collective-permute-start.5 = (bf16[128,1024]{1,0:T(8,128)(2,1)S(1)}, bf16[128,1024]{1,0:T(8,128)(2,1)S(1)}, u32[]{:S(2)}, u32[]{:S(2)}) collective-permute-start(bf16[128,1024]{1,0:T(8,128)(2,1)S(1)} %get-tuple-element.32), channel_id=1, source_target_pairs={{0,2},{2,0},{4,6},{6,4},{1,3},{3,1},{5,7},{7,5},{8,10},{10,8},{12,... | collective-permute-start | bytes 786440 | tf_op jit(solution)/shard_map/ppermute | solution.py:237
  38.4 10.9 %collective-permute-start.9 = (bf16[32,1024]{1,0:T(8,128)(2,1)S(1)}, bf16[32,1024]{1,0:T(8,128)(2,1)S(1)}, u32[]{:S(2)}, u32[]{:S(2)}) collective-permute-start(bf16[32,1024]{1,0:T(8,128)(2,1)S(1)} %get-tuple-element.40), channel_id=1, source_target_pairs={{2,4},{3,5},{10,12},{11,13},{18,20},{19,21},{26,28},{27,29},{34,36... | collective-permute-start | bytes 196616 | tf_op jit(solution)/shard_map/ppermute | solution.py:238
  49.5 6.0 %collective-permute-start.13 = (bf16[128,1024]{1,0:T(8,128)(2,1)S(1)}, bf16[128,1024]{1,0:T(8,128)(2,1)S(1)}, u32[]{:S(2)}, u32[]{:S(2)}) collective-permute-start(bf16[128,1024]{1,0:T(8,128)(2,1)S(1)} %shard_map.81.refs_4_), channel_id=1, source_target_pairs={{0,1},{1,0},{2,3},{3,2},{4,5},{5,4},{6,7},{7,6},{8,9},{9,8},{10,11... | collective-permute-start | bytes 786440 | tf_op jit(solution)/shard_map/ppermute | solution.py:246
  49.6 9.9 %collective-permute-start.10 = (bf16[128,1024]{1,0:T(8,128)(2,1)S(1)}, bf16[128,1024]{1,0:T(8,128)(2,1)S(1)}, u32[]{:S(2)}, u32[]{:S(2)}) collective-permute-start(bf16[128,1024]{1,0:T(8,128)(2,1)S(1)} %shard_map.81.refs_4_), channel_id=1, source_target_pairs={{0,32},{8,40},{16,48},{24,56},{32,64},{40,72},{48,80},{56,88},{64,... | collective-permute-start | bytes 786440 | tf_op jit(solution)/shard_map/ppermute | solution.py:245
  51.4 14.8 %collective-permute-start.11 = (bf16[128,1024]{1,0:T(8,128)(2,1)S(1)}, bf16[128,1024]{1,0:T(8,128)(2,1)S(1)}, u32[]{:S(2)}, u32[]{:S(2)}) collective-permute-start(bf16[128,1024]{1,0:T(8,128)(2,1)S(1)} %shard_map.81.refs_4_), channel_id=1, source_target_pairs={{0,64},{8,72},{16,80},{24,88},{32,96},{40,104},{48,112},{56,120},{... | collective-permute-start | bytes 786440 | tf_op jit(solution)/shard_map/ppermute | solution.py:245
  54.1 12.0 %collective-permute-start.12 = (bf16[128,1024]{1,0:T(8,128)(2,1)S(1)}, bf16[128,1024]{1,0:T(8,128)(2,1)S(1)}, u32[]{:S(2)}, u32[]{:S(2)}) collective-permute-start(bf16[128,1024]{1,0:T(8,128)(2,1)S(1)} %shard_map.81.refs_4_), channel_id=1, source_target_pairs={{0,96},{8,104},{16,112},{24,120},{32,0},{40,8},{48,16},{56,24},{64... | collective-permute-start | bytes 786440 | tf_op jit(solution)/shard_map/ppermute | solution.py:245
  58.2 24.4 %collective-permute-start.18 = (bf16[128,2560]{1,0:T(8,128)(2,1)}, bf16[128,2560]{1,0:T(8,128)(2,1)}, u32[]{:S(2)}, u32[]{:S(2)}) collective-permute-start(bf16[128,2560]{1,0:T(8,128)(2,1)} %convolution_convert_fusion), channel_id=1, source_target_pairs={{0,1},{1,0},{2,3},{3,2},{4,5},{5,4},{6,7},{7,6},{8,9},{9,8},{10,11... | collective-permute-start | bytes 1966088 | tf_op jit(solution)/shard_map/ppermute | solution.py:258
  59.5 7.2 %collective-permute-start.14 = (bf16[128,1024]{1,0:T(8,128)(2,1)S(1)}, bf16[128,1024]{1,0:T(8,128)(2,1)S(1)}, u32[]{:S(2)}, u32[]{:S(2)}) collective-permute-start(bf16[128,1024]{1,0:T(8,128)(2,1)S(1)} %collective-permute-done.10.refs_5_), channel_id=1, source_target_pairs={{0,1},{1,0},{2,3},{3,2},{4,5},{5,4},{6,7},{7,6},{8,9},{9,8},{10,11... | collective-permute-start | bytes 786440 | tf_op jit(solution)/shard_map/ppermute | solution.py:246
  66.1 1.5 %collective-permute-start.15 = (bf16[128,1024]{1,0:T(8,128)(2,1)S(1)}, bf16[128,1024]{1,0:T(8,128)(2,1)S(1)}, u32[]{:S(2)}, u32[]{:S(2)}) collective-permute-start(bf16[128,1024]{1,0:T(8,128)(2,1)S(1)} %collective-permute-done.11.refs_6_), channel_id=1, source_target_pairs={{0,1},{1,0},{2,3},{3,2},{4,5},{5,4},{6,7},{7,6},{8,9},{9,8},{10,11... | collective-permute-start | bytes 786440 | tf_op jit(solution)/shard_map/ppermute | solution.py:246
  66.1 1.9 %collective-permute-start.16 = (bf16[128,1024]{1,0:T(8,128)(2,1)S(1)}, bf16[128,1024]{1,0:T(8,128)(2,1)S(1)}, u32[]{:S(2)}, u32[]{:S(2)}) collective-permute-start(bf16[128,1024]{1,0:T(8,128)(2,1)S(1)} %collective-permute-done.12.refs_7_), channel_id=1, source_target_pairs={{0,1},{1,0},{2,3},{3,2},{4,5},{5,4},{6,7},{7,6},{8,9},{9,8},{10,11... | collective-permute-start | bytes 786440 | tf_op jit(solution)/shard_map/ppermute | solution.py:246
  70.3 12.3 %collective-permute-start.17 = (bf16[160,1024]{1,0:T(8,128)(2,1)S(1)}, bf16[160,1024]{1,0:T(8,128)(2,1)S(1)}, u32[]{:S(2)}, u32[]{:S(2)}) collective-permute-start(bf16[160,1024]{1,0:T(8,128)(2,1)S(1)} %get-tuple-element.41), channel_id=1, source_target_pairs={{0,16},{1,144},{8,24},{9,152},{16,0},{17,128},{24,8},{25,136},{32,... | collective-permute-start | bytes 983048 | tf_op jit(solution)/shard_map/ppermute | solution.py:253
  72.7 9.9 %collective-permute-start.19 = (bf16[160,1024]{1,0:T(8,128)(2,1)S(1)}, bf16[160,1024]{1,0:T(8,128)(2,1)S(1)}, u32[]{:S(2)}, u32[]{:S(2)}) collective-permute-start(bf16[160,1024]{1,0:T(8,128)(2,1)S(1)} %get-tuple-element.44), channel_id=1, source_target_pairs={{0,0},{1,128},{8,8},{9,136},{16,16},{17,144},{24,24},{25,152},{32,... | collective-permute-start | bytes 983048 | tf_op jit(solution)/shard_map/ppermute | solution.py:253
  73.4 16.3 %collective-permute-start.20 = (bf16[160,1024]{1,0:T(8,128)(2,1)S(1)}, bf16[160,1024]{1,0:T(8,128)(2,1)S(1)}, u32[]{:S(2)}, u32[]{:S(2)}) collective-permute-start(bf16[160,1024]{1,0:T(8,128)(2,1)S(1)} %get-tuple-element.45), channel_id=1, source_target_pairs={{0,8},{1,136},{8,16},{9,144},{16,24},{17,152},{24,0},{25,128},{32,... | collective-permute-start | bytes 983048 | tf_op jit(solution)/shard_map/ppermute | solution.py:253
  73.5 16.2 %collective-permute-start.21 = (bf16[160,1024]{1,0:T(8,128)(2,1)S(1)}, bf16[160,1024]{1,0:T(8,128)(2,1)S(1)}, u32[]{:S(2)}, u32[]{:S(2)}) collective-permute-start(bf16[160,1024]{1,0:T(8,128)(2,1)S(1)} %get-tuple-element.47), channel_id=1, source_target_pairs={{0,24},{1,152},{8,0},{9,128},{16,8},{17,136},{24,16},{25,144},{32,... | collective-permute-start | bytes 983048 | tf_op jit(solution)/shard_map/ppermute | solution.py:253
  90.4 1.5 %collective-permute-start.22 = (bf16[80,1024]{1,0:T(8,128)(2,1)S(1)}, bf16[80,1024]{1,0:T(8,128)(2,1)S(1)}, u32[]{:S(2)}, u32[]{:S(2)}) collective-permute-start(bf16[80,1024]{1,0:T(8,128)(2,1)S(1)} %get-tuple-element.49), channel_id=1, source_target_pairs={{0,1},{1,0},{2,3},{3,2},{4,5},{5,4},{6,7},{7,6},{8,9},{9,8},{10,11... | collective-permute-start | bytes 491528 | tf_op jit(solution)/shard_map/ppermute | solution.py:264
  92.0 9.2 %collective-permute-start.23 = (bf16[80,256]{1,0:T(8,128)(2,1)S(1)}, bf16[80,256]{1,0:T(8,128)(2,1)S(1)}, u32[]{:S(2)}, u32[]{:S(2)}) collective-permute-start(bf16[80,256]{1,0:T(8,128)(2,1)S(1)} %get-tuple-element.58), channel_id=1, source_target_pairs={{0,2},{2,4},{4,6},{6,0},{1,3},{3,5},{5,7},{7,1},{8,10},{10,12},{12... | collective-permute-start | bytes 122888 | tf_op jit(solution)/shard_map/ppermute | solution.py:273
  92.1 9.1 %collective-permute-start.24 = (bf16[80,256]{1,0:T(8,128)(2,1)S(1)}, bf16[80,256]{1,0:T(8,128)(2,1)S(1)}, u32[]{:S(2)}, u32[]{:S(2)}) collective-permute-start(bf16[80,256]{1,0:T(8,128)(2,1)S(1)} %get-tuple-element.60), channel_id=1, source_target_pairs={{0,4},{2,6},{4,0},{6,2},{1,5},{3,7},{5,1},{7,3},{8,12},{10,14},{12... | collective-permute-start | bytes 122888 | tf_op jit(solution)/shard_map/ppermute | solution.py:273
  94.4 7.2 %collective-permute-start.25 = (bf16[80,256]{1,0:T(8,128)(2,1)S(1)}, bf16[80,256]{1,0:T(8,128)(2,1)S(1)}, u32[]{:S(2)}, u32[]{:S(2)}) collective-permute-start(bf16[80,256]{1,0:T(8,128)(2,1)S(1)} %get-tuple-element.59), channel_id=1, source_target_pairs={{0,6},{2,0},{4,2},{6,4},{1,7},{3,1},{5,3},{7,5},{8,14},{10,8},{12,... | collective-permute-start | bytes 122888 | tf_op jit(solution)/shard_map/ppermute | solution.py:273

commit v4 on v3

--- a/solution.py
+++ b/solution.py
@@ -21,6 +21,7 @@
 BF16 = jnp.bfloat16
 SWAP = ((0, 1), (1, 0))
 TAIL_DOWN = ((2, 1),)
+TAIL_UP = ((2, 1), (3, 3))
 TAIL_BACK = ((1, 2),)
 NEXT = ((0, 1), (1, 0), (2, 3), (3, 2))
 ACROSS = ((0, 3), (1, 2), (2, 1), (3, 0))
@@ -210,7 +211,7 @@
     ]
     tails = jnp.concatenate([queries[:TAIL], grads[:TAIL]], axis=1)
     back = lax.ppermute(part_other, "fsdp", SWAP)
-    tails = lax.ppermute(tails, "seq", ACROSS)
+    tails = lax.ppermute(tails, "seq", TAIL_UP)
     kv, kv_end = call(
         kv_kernel, (shape(TOK, width, BF16), shape(TAIL, width, BF16)), part_mine, back, cos, sin
     )
@@ -267,10 +268,10 @@
     head = width // 4
     parts = []
     for k in range(4):
-        piece = lax.dynamic_slice_in_dim(summed, ((seq + k) % 4) * head, head, 1)
+        piece = lax.dynamic_slice_in_dim(summed, (seq ^ k) * head, head, 1)
         parts.append(piece if k == 0 else piece.astype(BF16))
     for k in (2, 1, 3):
-        parts[k] = lax.ppermute(parts[k], "seq", [(i, (i + k) % 4) for i in range(4)]).astype(F32)
+        parts[k] = lax.ppermute(parts[k], "seq", [(i, i ^ k) for i in range(4)]).astype(F32)
     out = parts[0] + parts[1] + parts[2] + parts[3]
 
     input_grad = jnp.where(

time: 104 us -> 103 us (level)
  waiting for transfers between devices: 38.7 us -> 34 us
  starting transfers between devices: 36.9 us -> 40.5 us
    ppermute x1, starting transfers between devices: 3.05 us -> 10.3 us  [on_device(): from_next = lax.ppermute(to_next, 'seq', NEXT)]
    ppermute x4, starting transfers between devices: 12.8 us -> 7.26 us  [the longest x3 6.58 us: on_device(): lax.ppermute(parts[k], 'seq', [(i, i ^ k) for i in range(4)]).astype(F32)]
    ppermute x1, waiting for transfers between devices: 10.2 us -> 7.47 us  [on_device(): from_next = lax.ppermute(to_next, 'seq', NEXT)]
    ppermute x1, starting transfers between devices: 1.54 us -> 3.99 us  [on_device(): kv_next = lax.ppermute(kv, 'seq', NEXT)]
    ppermute x4, waiting for transfers between devices: 2.61 us -> 1.36 us  [the longest x3 1.36 us: on_device(): lax.ppermute(parts[k], 'seq', [(i, i ^ k) for i in range(4)]).astype(F32)]
  transfers between devices with their start and end apart: 26 -> 26, of which waited for: 12 -> 11; matrix products, arithmetic and copies ran while one was open for 11% -> 12% of each run, Pallas kernels for 8% -> 8%
where the time goes in v4:
time: 103 us; the launch traced here: 101 us
  starting transfers between devices  40.5 us (39%)
  waiting for transfers between devices  34 us (33%)
  Pallas kernels  9.39 us (9%)
  matrix products  7.01 us (7%)
  other arithmetic  4.11 us (4%)
  local copies, waits for them, and re-layouts  3.82 us (4%)
  between operations  2.39 us (2%)
    ppermute x1, starting transfers between devices, on_device(): from_next = lax.ppermute(to_next, 'seq', NEXT)  10.3 us
    ppermute x4, waiting for transfers between devices, on_device(): lax.ppermute(p, ('dp', 'fsdp'), y_perm(k))  9.86 us
    pallas_call x7, Pallas kernels, call(): pl.pallas_call(kernel, grid=grid, out_shape=outs, in_specs=specs, out_spe...  9.39 us
    ppermute x3, waiting for transfers between devices, on_device(): direct = [kg] + [lax.ppermute(kg, 'dp', dp_shift(dx=k)) for k in (1, 2, 3)]  7.9 us
    ppermute x1, waiting for transfers between devices, on_device(): from_next = lax.ppermute(to_next, 'seq', NEXT)  7.47 us
    dot_general x2, matrix products, dot(): lax.dot_general(a, b, (((ca,), (cb,)), ((), ())), preferred_element_type=...  7.01 us
    ppermute x3, starting transfers between devices, on_device(): lax.ppermute(parts[k], 'seq', [(i, i ^ k) for i in range(4)]).astype(F32)  6.58 us
    ppermute x3, starting transfers between devices, on_device(): direct = [kg] + [lax.ppermute(kg, 'dp', dp_shift(dx=k)) for k in (1, 2, 3)]  5.9 us
  transfers between devices with their start and end apart: 26, of which 11 were waited for; matrix products, arithmetic and copies ran while one was open for 12% of the time, Pallas kernels for 8%

profile of v4, /device:TPU:8, one launch (start us, length us, event | category | flops | bytes accessed | tf_op | source)
XLA Modules:
  0.0 101.2 jit_solution(1953139827654450630)
XLA Ops:
  0.6 0.1 collective-permute-start.1
  0.7 1.1 %slice_bitcast_fusion = (bf16[32,2560]{1,0:T(8,128)(2,1)S(1)}, bf16[32,2560]{1,0:T(8,128)(2,1)S(1)}) fusion(bf16[1,128,2560]{2,1,0:T(8,128)(2,1)} %param.8, bf16[1,128,2560]{2,1,0:T(8,128)(2,1)} %param.7), kind=kLoop, calls=%fused_computation.9 | loop fusion | bytes 655360 | tf_op jit(solution)/shard_map/slice | solution.py:212
  1.9 0.7 collective-permute-start
  4.0 2.5 %copy-done = bf16[2560,1024]{1,0:T(8,128)(2,1)S(1)} copy-done((bf16[2560,1024]{1,0:T(8,128)(2,1)S(1)}, bf16[2560,1024]{1,0:T(8,128)(2,1)}, u32[]{:S(2)}) %copy-start) | copy-done | bytes 5242904
  6.5 0.8 shard_map.77.own_ref
  7.4 0.9 shard_map.78
  8.2 0.6 collective-permute-start.2
  8.8 0.3 fusion
  9.1 0.1 pad_maximum_fusion.5
  9.2 1.1 %collective-permute-done.2.recv_ref = f32[128,1024]{1,0:T(8,128)S(1)} collective-permute-done((f32[128,1024]{1,0:T(8,128)S(1)}, f32[128,1024]{1,0:T(8,128)S(1)}, u32[]{:S(2)}, u32[]{:S(2)}) %collective-permute-start.2) | collective-permute-done | bytes 524320 | tf_op jit(solution)/shard_map/ppermute | solution.py:213
  10.3 0.2 shard_map.79
  10.5 4.0 %collective-permute-start.3 = (bf16[128,1024]{1,0:T(8,128)(2,1)S(1)}, bf16[128,1024]{1,0:T(8,128)(2,1)S(1)}, u32[]{:S(2)}, u32[]{:S(2)}) collective-permute-start(bf16[128,1024]{1,0:T(8,128)(2,1)S(1)} %get-tuple-element.30.kv_ref), channel_id=1, source_target_pairs={{0,2},{2,0},{4,6},{6,4},{1,3},{3,1},{5,7},{7,5},{8,10},{10,8},{12,... | collective-permute-start | bytes 786440 | tf_op jit(solution)/shard_map/ppermute | solution.py:218
  14.6 0.1 constant_dynamic-slice_fusion
  14.7 2.8 %collective-permute-start.8 = (bf16[256,640]{1,0:T(8,128)(2,1)S(1)}, bf16[256,640]{1,0:T(8,128)(2,1)S(1)}, u32[]{:S(2)}, u32[]{:S(2)}) collective-permute-start(bf16[256,640]{1,0:T(8,128)(2,1)S(1)} %pad_maximum_fusion.4), channel_id=1, source_target_pairs={{0,96},{8,104},{16,112},{24,120},{32,0},{40,8},{48,16},{56,24},{64... | collective-permute-start | bytes 983048 | tf_op jit(solution)/shard_map/ppermute | solution.py:231
  17.7 0.7 collective-permute-start.4
  18.4 2.4 %collective-permute-start.7 = (bf16[256,640]{1,0:T(8,128)(2,1)S(1)}, bf16[256,640]{1,0:T(8,128)(2,1)S(1)}, u32[]{:S(2)}, u32[]{:S(2)}) collective-permute-start(bf16[256,640]{1,0:T(8,128)(2,1)S(1)} %pad_maximum_fusion.1), channel_id=1, source_target_pairs={{0,64},{8,72},{16,80},{24,88},{32,96},{40,104},{48,112},{56,120},{... | collective-permute-start | bytes 983048 | tf_op jit(solution)/shard_map/ppermute | solution.py:231
  20.8 3.6 %collective-permute-done.3.next_ref = bf16[128,1024]{1,0:T(8,128)(2,1)S(1)} collective-permute-done((bf16[128,1024]{1,0:T(8,128)(2,1)S(1)}, bf16[128,1024]{1,0:T(8,128)(2,1)S(1)}, u32[]{:S(2)}, u32[]{:S(2)}) %collective-permute-start.3) | collective-permute-done | bytes 262176 | tf_op jit(solution)/shard_map/ppermute | solution.py:218
  24.4 4.4 %shard_map.80 = (f32[128,1024]{1,0:T(8,128)S(1)}, bf16[128,1024]{1,0:T(8,128)(2,1)S(1)}, bf16[32,1024]{1,0:T(8,128)(2,1)S(1)}) custom-call(s32[3]{0:T(128)S(1)} %pad_add_fusion.1.meta, bf16[128,2560]{1,0:T(8,128)(2,1)S(1)} %bitcast.23, bf16[128,2560]{1,0:T(8,128)(2,1)S(1)} %bitcast.24, bf16[32,5120]{1,0:T(8,128)(2,1)S(1)} %collective-permute-done.tail_ref, ...), custom_call_target="tpu_custom_call" | custom-call | tf_op jit(solution)/shard_map/pallas_call | solution.py:174
  28.8 10.3 %collective-permute-start.5 = (bf16[128,1024]{1,0:T(8,128)(2,1)S(1)}, bf16[128,1024]{1,0:T(8,128)(2,1)S(1)}, u32[]{:S(2)}, u32[]{:S(2)}) collective-permute-start(bf16[128,1024]{1,0:T(8,128)(2,1)S(1)} %get-tuple-element.32), channel_id=1, source_target_pairs={{0,2},{2,0},{4,6},{6,4},{1,3},{3,1},{5,7},{7,5},{8,10},{10,8},{12,... | collective-permute-start | bytes 786440 | tf_op jit(solution)/shard_map/ppermute | solution.py:238
  39.0 0.7 collective-permute-start.9
  39.8 7.5 %collective-permute-done.5.next_ref = bf16[128,1024]{1,0:T(8,128)(2,1)S(1)} collective-permute-done((bf16[128,1024]{1,0:T(8,128)(2,1)S(1)}, bf16[128,1024]{1,0:T(8,128)(2,1)S(1)}, u32[]{:S(2)}, u32[]{:S(2)}) %collective-permute-start.5) | collective-permute-done | bytes 262176 | tf_op jit(solution)/shard_map/ppermute | solution.py:238
  47.2 0.2 shard_map.81.refs_4_
  47.4 0.1 collective-permute-start.13
  47.5 1.7 %collective-permute-start.10 = (bf16[128,1024]{1,0:T(8,128)(2,1)S(1)}, bf16[128,1024]{1,0:T(8,128)(2,1)S(1)}, u32[]{:S(2)}, u32[]{:S(2)}) collective-permute-start(bf16[128,1024]{1,0:T(8,128)(2,1)S(1)} %shard_map.81.refs_4_), channel_id=1, source_target_pairs={{0,32},{8,40},{16,48},{24,56},{32,64},{40,72},{48,80},{56,88},{64,... | collective-permute-start | bytes 786440 | tf_op jit(solution)/shard_map/ppermute | solution.py:246
  49.3 2.7 %collective-permute-start.11 = (bf16[128,1024]{1,0:T(8,128)(2,1)S(1)}, bf16[128,1024]{1,0:T(8,128)(2,1)S(1)}, u32[]{:S(2)}, u32[]{:S(2)}) collective-permute-start(bf16[128,1024]{1,0:T(8,128)(2,1)S(1)} %shard_map.81.refs_4_), channel_id=1, source_target_pairs={{0,64},{8,72},{16,80},{24,88},{32,96},{40,104},{48,112},{56,120},{... | collective-permute-start | bytes 786440 | tf_op jit(solution)/shard_map/ppermute | solution.py:246
  52.0 1.4 %collective-permute-start.12 = (bf16[128,1024]{1,0:T(8,128)(2,1)S(1)}, bf16[128,1024]{1,0:T(8,128)(2,1)S(1)}, u32[]{:S(2)}, u32[]{:S(2)}) collective-permute-start(bf16[128,1024]{1,0:T(8,128)(2,1)S(1)} %shard_map.81.refs_4_), channel_id=1, source_target_pairs={{0,96},{8,104},{16,112},{24,120},{32,0},{40,8},{48,16},{56,24},{64... | collective-permute-start | bytes 786440 | tf_op jit(solution)/shard_map/ppermute | solution.py:246
  53.4 2.7 %convolution_convert_fusion = bf16[128,2560]{1,0:T(8,128)(2,1)} fusion(bf16[128,1024]{1,0:T(8,128)(2,1)S(1)} %collective-permute-done.13.refs_8_, bf16[2560,1024]{1,0:T(8,128)(2,1)S(1)} %bitcast.19), kind=kOutput, calls=%fused_computation | convolution fusion | flops 671416320 | bytes 6160384 | tf_op jit(solution)/shard_map/dot_general | solution.py:48
  56.1 1.3 %collective-permute-done.10.refs_5_ = bf16[128,1024]{1,0:T(8,128)(2,1)S(1)} collective-permute-done((bf16[128,1024]{1,0:T(8,128)(2,1)S(1)}, bf16[128,1024]{1,0:T(8,128)(2,1)S(1)}, u32[]{:S(2)}, u32[]{:S(2)}) %collective-permute-start.10) | collective-permute-done | bytes 262176 | tf_op jit(solution)/shard_map/ppermute | solution.py:246
  57.4 6.6 %collective-permute-done.11.refs_6_ = bf16[128,1024]{1,0:T(8,128)(2,1)S(1)} collective-permute-done((bf16[128,1024]{1,0:T(8,128)(2,1)S(1)}, bf16[128,1024]{1,0:T(8,128)(2,1)S(1)}, u32[]{:S(2)}, u32[]{:S(2)}) %collective-permute-start.11) | collective-permute-done | bytes 262176 | tf_op jit(solution)/shard_map/ppermute | solution.py:246
  64.0 0.5 collective-permute-start.16
  64.6 0.9 collective-permute-done.15.refs_10_
  65.6 0.4 collective-permute-done.16.refs_11_
  65.9 2.3 %shard_map.82 = (bf16[160,1024]{1,0:T(8,128)(2,1)S(1)}, bf16[160,1024]{1,0:T(8,128)(2,1)S(1)}, bf16[160,1024]{1,0:T(8,128)(2,1)S(1)}, bf16[160,1024]{1,0:T(8,128)(2,1)S(1)}) custom-call(s32[2]{0:T(128)S(1)} %pad_add_fusion.meta, bf16[256,640]{1,0:T(8,128)(2,1)S(1)} %pad_maximum_fusion.2.refs_0_, bf16[256,640]{1,0:T(8,128)(2,1)S(1)} %collective-permute-done.6.refs_1_, ...), custom_call_target="tpu_custom_call" | custom-call | tf_op jit(solution)/shard_map/pallas_call | solution.py:174
  68.2 2.4 %collective-permute-start.17 = (bf16[160,1024]{1,0:T(8,128)(2,1)S(1)}, bf16[160,1024]{1,0:T(8,128)(2,1)S(1)}, u32[]{:S(2)}, u32[]{:S(2)}) collective-permute-start(bf16[160,1024]{1,0:T(8,128)(2,1)S(1)} %get-tuple-element.41), channel_id=1, source_target_pairs={{0,16},{1,144},{8,24},{9,152},{16,0},{17,128},{24,8},{25,136},{32,... | collective-permute-start | bytes 983048 | tf_op jit(solution)/shard_map/ppermute | solution.py:254
  70.6 0.7 collective-permute-start.19
  71.4 2.0 %collective-permute-start.21 = (bf16[160,1024]{1,0:T(8,128)(2,1)S(1)}, bf16[160,1024]{1,0:T(8,128)(2,1)S(1)}, u32[]{:S(2)}, u32[]{:S(2)}) collective-permute-start(bf16[160,1024]{1,0:T(8,128)(2,1)S(1)} %get-tuple-element.47), channel_id=1, source_target_pairs={{0,24},{1,152},{8,0},{9,128},{16,8},{17,136},{24,16},{25,144},{32,... | collective-permute-start | bytes 983048 | tf_op jit(solution)/shard_map/ppermute | solution.py:254
  73.4 4.3 %convolution_convert_fusion.1 = bf16[128,2560]{1,0:T(8,128)(2,1)S(1)} fusion(bf16[128,1024]{1,0:T(8,128)(2,1)S(1)} %shard_map.81.refs_4_, bf16[2560,1024]{1,0:T(8,128)(2,1)} %w_ref.3), kind=kOutput, calls=%fused_computation.1 | convolution fusion | flops 671416320 | bytes 6160384 | tf_op jit(solution)/shard_map/dot_general | solution.py:48
  77.7 2.8 %collective-permute-done.17.c_ref = bf16[160,1024]{1,0:T(8,128)(2,1)S(1)} collective-permute-done((bf16[160,1024]{1,0:T(8,128)(2,1)S(1)}, bf16[160,1024]{1,0:T(8,128)(2,1)S(1)}, u32[]{:S(2)}, u32[]{:S(2)}) %collective-permute-start.17) | collective-permute-done | bytes 327712 | tf_op jit(solution)/shard_map/ppermute | solution.py:254
  80.5 7.1 %collective-permute-done.20.b_ref = bf16[160,1024]{1,0:T(8,128)(2,1)S(1)} collective-permute-done((bf16[160,1024]{1,0:T(8,128)(2,1)S(1)}, bf16[160,1024]{1,0:T(8,128)(2,1)S(1)}, u32[]{:S(2)}, u32[]{:S(2)}) %collective-permute-start.20) | collective-permute-done | bytes 327712 | tf_op jit(solution)/shard_map/ppermute | solution.py:254
  87.6 0.7 shard_map.83
  88.3 0.1 collective-permute-start.22
  88.5 1.4 %collective-permute-done.22 = bf16[80,1024]{1,0:T(8,128)(2,1)S(1)} collective-permute-done((bf16[80,1024]{1,0:T(8,128)(2,1)S(1)}, bf16[80,1024]{1,0:T(8,128)(2,1)S(1)}, u32[]{:S(2)}, u32[]{:S(2)}) %collective-permute-start.22) | collective-permute-done | bytes 163872 | tf_op jit(solution)/shard_map/ppermute | solution.py:265
  89.9 0.1 collective-permute-start.23
  90.0 4.4 %collective-permute-start.24 = (bf16[80,256]{1,0:T(8,128)(2,1)S(1)}, bf16[80,256]{1,0:T(8,128)(2,1)S(1)}, u32[]{:S(2)}, u32[]{:S(2)}) collective-permute-start(bf16[80,256]{1,0:T(8,128)(2,1)S(1)} %get-tuple-element.60), channel_id=1, source_target_pairs={{0,4},{2,6},{4,0},{6,2},{1,5},{3,7},{5,1},{7,3},{8,12},{10,14},{12... | collective-permute-start | bytes 122888 | tf_op jit(solution)/shard_map/ppermute | solution.py:274
  94.4 2.1 %collective-permute-start.25 = (bf16[80,256]{1,0:T(8,128)(2,1)S(1)}, bf16[80,256]{1,0:T(8,128)(2,1)S(1)}, u32[]{:S(2)}, u32[]{:S(2)}) collective-permute-start(bf16[80,256]{1,0:T(8,128)(2,1)S(1)} %get-tuple-element.59), channel_id=1, source_target_pairs={{0,6},{2,4},{4,2},{6,0},{1,7},{3,5},{5,3},{7,1},{8,14},{10,12},{12... | collective-permute-start | bytes 122888 | tf_op jit(solution)/shard_map/ppermute | solution.py:274
  96.5 2.7 %maximum_select_fusion = bf16[1,128,5120]{2,1,0:T(8,128)(2,1)} fusion(bf16[1,128,2560]{2,1,0:T(8,128)(2,1)} %bitcast.11, bf16[1,128,2560]{2,1,0:T(8,128)(2,1)S(1)} %bitcast.25, pred[]{:T(512)S(6)} %eq.10), kind=kLoop, calls=%fused_computation.2 | loop fusion | flops 5898240 | bytes 2621441 | tf_op jit(solution)/shard_map/jit(_where)/select_n | solution.py:277
  99.2 1.4 %collective-permute-done.25 = bf16[80,256]{1,0:T(8,128)(2,1)S(1)} collective-permute-done((bf16[80,256]{1,0:T(8,128)(2,1)S(1)}, bf16[80,256]{1,0:T(8,128)(2,1)S(1)}, u32[]{:S(2)}, u32[]{:S(2)}) %collective-permute-start.25) | collective-permute-done | bytes 40992 | tf_op jit(solution)/shard_map/ppermute | solution.py:274
  100.5 0.7 add_multiply_fusion
  (44 shorter events, 0.7 us)
Async XLA Ops:
  0.6 3.3 %copy-start.1 = (bf16[1,128,5120]{2,1,0:T(8,128)(2,1)S(1)}, bf16[1,128,5120]{2,1,0:T(8,128)(2,1)}, u32[]{:S(2)}) copy-start(bf16[1,128,5120]{2,1,0:T(8,128)(2,1)} %param.6) | copy-start | bytes 3932164
  0.6 6.7 %collective-permute-start.1 = (bf16[128,5120]{1,0:T(8,128)(2,1)}, bf16[128,5120]{1,0:T(8,128)(2,1)S(1)}, u32[]{:S(2)}, u32[]{:S(2)}) collective-permute-start(bf16[128,5120]{1,0:T(8,128)(2,1)} %bitcast.20), channel_id=1, source_target_pairs={{0,1},{1,0},{2,3},{3,2},{4,5},{5,4},{6,7},{7,6},{8,9},{9,8},{10,11... | collective-permute-start | bytes 3932168 | tf_op jit(solution)/shard_map/ppermute | solution.py:206
  1.9 15.8 %collective-permute-start = (bf16[32,5120]{1,0:T(8,128)(2,1)S(1)}, bf16[32,5120]{1,0:T(8,128)(2,1)S(1)}, u32[]{:S(2)}, u32[]{:S(2)}) collective-permute-start(bf16[32,5120]{1,0:T(8,128)(2,1)S(1)} %pad_maximum_fusion), channel_id=1, source_target_pairs={{4,2},{6,6},{5,3},{7,7},{12,10},{14,14},{13,11},{15,15},{20,18},{2... | collective-permute-start | bytes 983048 | tf_op jit(solution)/shard_map/ppermute | solution.py:214
  4.0 2.5 %copy-start = (bf16[2560,1024]{1,0:T(8,128)(2,1)S(1)}, bf16[2560,1024]{1,0:T(8,128)(2,1)}, u32[]{:S(2)}) copy-start(bf16[2560,1024]{1,0:T(8,128)(2,1)} %w_ref.3) | copy-start | bytes 15728644
  7.3 46.1 %slice-start = ((s8[5242880]{0:T(1024)(128)(4,1)}), s8[1048576]{0:T(1024)(128)(4,1)S(1)}, s32[]{:S(2)}) async-start(s8[5242880]{0:T(1024)(128)(4,1)} %bitcast.18), calls=%async_computation | async-start | bytes 2097152
  8.2 2.1 %collective-permute-start.2 = (f32[128,1024]{1,0:T(8,128)S(1)}, f32[128,1024]{1,0:T(8,128)S(1)}, u32[]{:S(2)}, u32[]{:S(2)}) collective-permute-start(f32[128,1024]{1,0:T(8,128)S(1)} %shard_map.78), channel_id=1, source_target_pairs={{0,1},{1,0},{2,3},{3,2},{4,5},{5,4},{6,7},{7,6},{8,9},{9,8},{10,11... | collective-permute-start | bytes 1572872 | tf_op jit(solution)/shard_map/ppermute | solution.py:213
  10.3 43.1 %slice-start.1 = ((s8[5242880]{0:T(1024)(128)(4,1)}), s8[4194304]{0:T(1024)(128)(4,1)S(1)}, s32[]{:S(2)}) async-start(s8[5242880]{0:T(1024)(128)(4,1)} %bitcast.18), calls=%async_computation.1 | async-start | bytes 8388608
  10.5 13.9 %collective-permute-start.3 = (bf16[128,1024]{1,0:T(8,128)(2,1)S(1)}, bf16[128,1024]{1,0:T(8,128)(2,1)S(1)}, u32[]{:S(2)}, u32[]{:S(2)}) collective-permute-start(bf16[128,1024]{1,0:T(8,128)(2,1)S(1)} %get-tuple-element.30.kv_ref), channel_id=1, source_target_pairs={{0,2},{2,0},{4,6},{6,4},{1,3},{3,1},{5,7},{7,5},{8,10},{10,8},{12,... | collective-permute-start | bytes 786440 | tf_op jit(solution)/shard_map/ppermute | solution.py:218
  14.7 9.8 %copy-start.2 = (bf16[1,128,2560]{2,1,0:T(8,128)(2,1)S(1)}, bf16[1,128,2560]{2,1,0:T(8,128)(2,1)}, u32[]{:S(2)}) copy-start(bf16[1,128,2560]{2,1,0:T(8,128)(2,1)} %param.7) | copy-start | bytes 1966084
  14.7 9.7 %copy-start.3 = (bf16[1,128,2560]{2,1,0:T(8,128)(2,1)S(1)}, bf16[1,128,2560]{2,1,0:T(8,128)(2,1)}, u32[]{:S(2)}) copy-start(bf16[1,128,2560]{2,1,0:T(8,128)(2,1)} %param.8) | copy-start | bytes 1966084
  14.7 25.0 %collective-permute-start.8 = (bf16[256,640]{1,0:T(8,128)(2,1)S(1)}, bf16[256,640]{1,0:T(8,128)(2,1)S(1)}, u32[]{:S(2)}, u32[]{:S(2)}) collective-permute-start(bf16[256,640]{1,0:T(8,128)(2,1)S(1)} %pad_maximum_fusion.4), channel_id=1, source_target_pairs={{0,96},{8,104},{16,112},{24,120},{32,0},{40,8},{48,16},{56,24},{64... | collective-permute-start | bytes 983048 | tf_op jit(solution)/shard_map/ppermute | solution.py:231
  17.6 22.2 %collective-permute-start.6 = (bf16[256,640]{1,0:T(8,128)(2,1)S(1)}, bf16[256,640]{1,0:T(8,128)(2,1)S(1)}, u32[]{:S(2)}, u32[]{:S(2)}) collective-permute-start(bf16[256,640]{1,0:T(8,128)(2,1)S(1)} %pad_maximum_fusion.3), channel_id=1, source_target_pairs={{0,32},{8,40},{16,48},{24,56},{32,64},{40,72},{48,80},{56,88},{64,... | collective-permute-start | bytes 983048 | tf_op jit(solution)/shard_map/ppermute | solution.py:231
  17.7 3.1 %collective-permute-start.4 = (bf16[32,1024]{1,0:T(8,128)(2,1)S(1)}, bf16[32,1024]{1,0:T(8,128)(2,1)S(1)}, u32[]{:S(2)}, u32[]{:S(2)}) collective-permute-start(bf16[32,1024]{1,0:T(8,128)(2,1)S(1)} %get-tuple-element.31), channel_id=1, source_target_pairs={{4,2},{5,3},{12,10},{13,11},{20,18},{21,19},{28,26},{29,27},{36,34... | collective-permute-start | bytes 196616 | tf_op jit(solution)/shard_map/ppermute | solution.py:219
  18.4 21.4 %collective-permute-start.7 = (bf16[256,640]{1,0:T(8,128)(2,1)S(1)}, bf16[256,640]{1,0:T(8,128)(2,1)S(1)}, u32[]{:S(2)}, u32[]{:S(2)}) collective-permute-start(bf16[256,640]{1,0:T(8,128)(2,1)S(1)} %pad_maximum_fusion.1), channel_id=1, source_target_pairs={{0,64},{8,72},{16,80},{24,88},{32,96},{40,104},{48,112},{56,120},{... | collective-permute-start | bytes 983048 | tf_op jit(solution)/shard_map/ppermute | solution.py:231
  28.8 18.5 %collective-permute-start.5 = (bf16[128,1024]{1,0:T(8,128)(2,1)S(1)}, bf16[128,1024]{1,0:T(8,128)(2,1)S(1)}, u32[]{:S(2)}, u32[]{:S(2)}) collective-permute-start(bf16[128,1024]{1,0:T(8,128)(2,1)S(1)} %get-tuple-element.32), channel_id=1, source_target_pairs={{0,2},{2,0},{4,6},{6,4},{1,3},{3,1},{5,7},{7,5},{8,10},{10,8},{12,... | collective-permute-start | bytes 786440 | tf_op jit(solution)/shard_map/ppermute | solution.py:238
  39.0 8.2 %collective-permute-start.9 = (bf16[32,1024]{1,0:T(8,128)(2,1)S(1)}, bf16[32,1024]{1,0:T(8,128)(2,1)S(1)}, u32[]{:S(2)}, u32[]{:S(2)}) collective-permute-start(bf16[32,1024]{1,0:T(8,128)(2,1)S(1)} %get-tuple-element.40), channel_id=1, source_target_pairs={{2,4},{3,5},{10,12},{11,13},{18,20},{19,21},{26,28},{27,29},{34,36... | collective-permute-start | bytes 196616 | tf_op jit(solution)/shard_map/ppermute | solution.py:239
  47.4 6.0 %collective-permute-start.13 = (bf16[128,1024]{1,0:T(8,128)(2,1)S(1)}, bf16[128,1024]{1,0:T(8,128)(2,1)S(1)}, u32[]{:S(2)}, u32[]{:S(2)}) collective-permute-start(bf16[128,1024]{1,0:T(8,128)(2,1)S(1)} %shard_map.81.refs_4_), channel_id=1, source_target_pairs={{0,1},{1,0},{2,3},{3,2},{4,5},{5,4},{6,7},{7,6},{8,9},{9,8},{10,11... | collective-permute-start | bytes 786440 | tf_op jit(solution)/shard_map/ppermute | solution.py:247
  47.5 9.9 %collective-permute-start.10 = (bf16[128,1024]{1,0:T(8,128)(2,1)S(1)}, bf16[128,1024]{1,0:T(8,128)(2,1)S(1)}, u32[]{:S(2)}, u32[]{:S(2)}) collective-permute-start(bf16[128,1024]{1,0:T(8,128)(2,1)S(1)} %shard_map.81.refs_4_), channel_id=1, source_target_pairs={{0,32},{8,40},{16,48},{24,56},{32,64},{40,72},{48,80},{56,88},{64,... | collective-permute-start | bytes 786440 | tf_op jit(solution)/shard_map/ppermute | solution.py:246
  49.3 14.8 %collective-permute-start.11 = (bf16[128,1024]{1,0:T(8,128)(2,1)S(1)}, bf16[128,1024]{1,0:T(8,128)(2,1)S(1)}, u32[]{:S(2)}, u32[]{:S(2)}) collective-permute-start(bf16[128,1024]{1,0:T(8,128)(2,1)S(1)} %shard_map.81.refs_4_), channel_id=1, source_target_pairs={{0,64},{8,72},{16,80},{24,88},{32,96},{40,104},{48,112},{56,120},{... | collective-permute-start | bytes 786440 | tf_op jit(solution)/shard_map/ppermute | solution.py:246
  52.0 12.0 %collective-permute-start.12 = (bf16[128,1024]{1,0:T(8,128)(2,1)S(1)}, bf16[128,1024]{1,0:T(8,128)(2,1)S(1)}, u32[]{:S(2)}, u32[]{:S(2)}) collective-permute-start(bf16[128,1024]{1,0:T(8,128)(2,1)S(1)} %shard_map.81.refs_4_), channel_id=1, source_target_pairs={{0,96},{8,104},{16,112},{24,120},{32,0},{40,8},{48,16},{56,24},{64... | collective-permute-start | bytes 786440 | tf_op jit(solution)/shard_map/ppermute | solution.py:246
  56.1 24.4 %collective-permute-start.18 = (bf16[128,2560]{1,0:T(8,128)(2,1)}, bf16[128,2560]{1,0:T(8,128)(2,1)}, u32[]{:S(2)}, u32[]{:S(2)}) collective-permute-start(bf16[128,2560]{1,0:T(8,128)(2,1)} %convolution_convert_fusion), channel_id=1, source_target_pairs={{0,1},{1,0},{2,3},{3,2},{4,5},{5,4},{6,7},{7,6},{8,9},{9,8},{10,11... | collective-permute-start | bytes 1966088 | tf_op jit(solution)/shard_map/ppermute | solution.py:259
  57.4 7.2 %collective-permute-start.14 = (bf16[128,1024]{1,0:T(8,128)(2,1)S(1)}, bf16[128,1024]{1,0:T(8,128)(2,1)S(1)}, u32[]{:S(2)}, u32[]{:S(2)}) collective-permute-start(bf16[128,1024]{1,0:T(8,128)(2,1)S(1)} %collective-permute-done.10.refs_5_), channel_id=1, source_target_pairs={{0,1},{1,0},{2,3},{3,2},{4,5},{5,4},{6,7},{7,6},{8,9},{9,8},{10,11... | collective-permute-start | bytes 786440 | tf_op jit(solution)/shard_map/ppermute | solution.py:247
  64.0 1.5 %collective-permute-start.15 = (bf16[128,1024]{1,0:T(8,128)(2,1)S(1)}, bf16[128,1024]{1,0:T(8,128)(2,1)S(1)}, u32[]{:S(2)}, u32[]{:S(2)}) collective-permute-start(bf16[128,1024]{1,0:T(8,128)(2,1)S(1)} %collective-permute-done.11.refs_6_), channel_id=1, source_target_pairs={{0,1},{1,0},{2,3},{3,2},{4,5},{5,4},{6,7},{7,6},{8,9},{9,8},{10,11... | collective-permute-start | bytes 786440 | tf_op jit(solution)/shard_map/ppermute | solution.py:247
  64.0 1.9 %collective-permute-start.16 = (bf16[128,1024]{1,0:T(8,128)(2,1)S(1)}, bf16[128,1024]{1,0:T(8,128)(2,1)S(1)}, u32[]{:S(2)}, u32[]{:S(2)}) collective-permute-start(bf16[128,1024]{1,0:T(8,128)(2,1)S(1)} %collective-permute-done.12.refs_7_), channel_id=1, source_target_pairs={{0,1},{1,0},{2,3},{3,2},{4,5},{5,4},{6,7},{7,6},{8,9},{9,8},{10,11... | collective-permute-start | bytes 786440 | tf_op jit(solution)/shard_map/ppermute | solution.py:247
  68.2 12.3 %collective-permute-start.17 = (bf16[160,1024]{1,0:T(8,128)(2,1)S(1)}, bf16[160,1024]{1,0:T(8,128)(2,1)S(1)}, u32[]{:S(2)}, u32[]{:S(2)}) collective-permute-start(bf16[160,1024]{1,0:T(8,128)(2,1)S(1)} %get-tuple-element.41), channel_id=1, source_target_pairs={{0,16},{1,144},{8,24},{9,152},{16,0},{17,128},{24,8},{25,136},{32,... | collective-permute-start | bytes 983048 | tf_op jit(solution)/shard_map/ppermute | solution.py:254
  70.6 9.9 %collective-permute-start.19 = (bf16[160,1024]{1,0:T(8,128)(2,1)S(1)}, bf16[160,1024]{1,0:T(8,128)(2,1)S(1)}, u32[]{:S(2)}, u32[]{:S(2)}) collective-permute-start(bf16[160,1024]{1,0:T(8,128)(2,1)S(1)} %get-tuple-element.44), channel_id=1, source_target_pairs={{0,0},{1,128},{8,8},{9,136},{16,16},{17,144},{24,24},{25,152},{32,... | collective-permute-start | bytes 983048 | tf_op jit(solution)/shard_map/ppermute | solution.py:254
  71.3 16.3 %collective-permute-start.20 = (bf16[160,1024]{1,0:T(8,128)(2,1)S(1)}, bf16[160,1024]{1,0:T(8,128)(2,1)S(1)}, u32[]{:S(2)}, u32[]{:S(2)}) collective-permute-start(bf16[160,1024]{1,0:T(8,128)(2,1)S(1)} %get-tuple-element.45), channel_id=1, source_target_pairs={{0,8},{1,136},{8,16},{9,144},{16,24},{17,152},{24,0},{25,128},{32,... | collective-permute-start | bytes 983048 | tf_op jit(solution)/shard_map/ppermute | solution.py:254
  71.4 16.2 %collective-permute-start.21 = (bf16[160,1024]{1,0:T(8,128)(2,1)S(1)}, bf16[160,1024]{1,0:T(8,128)(2,1)S(1)}, u32[]{:S(2)}, u32[]{:S(2)}) collective-permute-start(bf16[160,1024]{1,0:T(8,128)(2,1)S(1)} %get-tuple-element.47), channel_id=1, source_target_pairs={{0,24},{1,152},{8,0},{9,128},{16,8},{17,136},{24,16},{25,144},{32,... | collective-permute-start | bytes 983048 | tf_op jit(solution)/shard_map/ppermute | solution.py:254
  88.3 1.5 %collective-permute-start.22 = (bf16[80,1024]{1,0:T(8,128)(2,1)S(1)}, bf16[80,1024]{1,0:T(8,128)(2,1)S(1)}, u32[]{:S(2)}, u32[]{:S(2)}) collective-permute-start(bf16[80,1024]{1,0:T(8,128)(2,1)S(1)} %get-tuple-element.49), channel_id=1, source_target_pairs={{0,1},{1,0},{2,3},{3,2},{4,5},{5,4},{6,7},{7,6},{8,9},{9,8},{10,11... | collective-permute-start | bytes 491528 | tf_op jit(solution)/shard_map/ppermute | solution.py:265
  89.9 9.3 %collective-permute-start.23 = (bf16[80,256]{1,0:T(8,128)(2,1)S(1)}, bf16[80,256]{1,0:T(8,128)(2,1)S(1)}, u32[]{:S(2)}, u32[]{:S(2)}) collective-permute-start(bf16[80,256]{1,0:T(8,128)(2,1)S(1)} %get-tuple-element.58), channel_id=1, source_target_pairs={{0,2},{2,0},{4,6},{6,4},{1,3},{3,1},{5,7},{7,5},{8,10},{10,8},{12,... | collective-permute-start | bytes 122888 | tf_op jit(solution)/shard_map/ppermute | solution.py:274
  90.0 9.2 %collective-permute-start.24 = (bf16[80,256]{1,0:T(8,128)(2,1)S(1)}, bf16[80,256]{1,0:T(8,128)(2,1)S(1)}, u32[]{:S(2)}, u32[]{:S(2)}) collective-permute-start(bf16[80,256]{1,0:T(8,128)(2,1)S(1)} %get-tuple-element.60), channel_id=1, source_target_pairs={{0,4},{2,6},{4,0},{6,2},{1,5},{3,7},{5,1},{7,3},{8,12},{10,14},{12... | collective-permute-start | bytes 122888 | tf_op jit(solution)/shard_map/ppermute | solution.py:274
  94.4 6.1 %collective-permute-start.25 = (bf16[80,256]{1,0:T(8,128)(2,1)S(1)}, bf16[80,256]{1,0:T(8,128)(2,1)S(1)}, u32[]{:S(2)}, u32[]{:S(2)}) collective-permute-start(bf16[80,256]{1,0:T(8,128)(2,1)S(1)} %get-tuple-element.59), channel_id=1, source_target_pairs={{0,6},{2,4},{4,2},{6,0},{1,7},{3,5},{5,3},{7,1},{8,14},{10,12},{12... | collective-permute-start | bytes 122888 | tf_op jit(solution)/shard_map/ppermute | solution.py:274

commit v5 on v4

--- a/solution.py
+++ b/solution.py
@@ -226,7 +226,6 @@
         mains.append(
             jnp.concatenate([lax.dynamic_slice_in_dim(r, at, span, 1) for r in (tokens, theirs)], axis=0)
         )
-    tails, mains[2] = lax.optimization_barrier((tails, mains[2]))
     for k in (1, 2, 3):
         mains[k] = lax.ppermute(mains[k], "dp", dp_shift(dx=k))
     own, to_next, to_end = call(

time: 103 us -> 102 us (level)
  no operation moved by 1% of the time
where the time goes in v5:
time: 102 us; the launch traced here: 101 us
  starting transfers between devices  39.9 us (39%)
  waiting for transfers between devices  34.6 us (34%)
  Pallas kernels  9.39 us (9%)
  matrix products  7.01 us (7%)
  other arithmetic  4.11 us (4%)
  local copies, waits for them, and re-layouts  3.82 us (4%)
  between operations  2.37 us (2%)
    ppermute x1, starting transfers between devices, on_device(): from_next = lax.ppermute(to_next, 'seq', NEXT)  10.3 us
    ppermute x4, waiting for transfers between devices, on_device(): lax.ppermute(p, ('dp', 'fsdp'), y_perm(k))  9.86 us
    pallas_call x7, Pallas kernels, call(): pl.pallas_call(kernel, grid=grid, out_shape=outs, in_specs=specs, out_spe...  9.39 us
    ppermute x3, waiting for transfers between devices, on_device(): direct = [kg] + [lax.ppermute(kg, 'dp', dp_shift(dx=k)) for k in (1, 2, 3)]  7.9 us
    ppermute x1, waiting for transfers between devices, on_device(): from_next = lax.ppermute(to_next, 'seq', NEXT)  7.47 us
    dot_general x2, matrix products, dot(): lax.dot_general(a, b, (((ca,), (cb,)), ((), ())), preferred_element_type=...  7.01 us
    ppermute x3, starting transfers between devices, on_device(): lax.ppermute(parts[k], 'seq', [(i, i ^ k) for i in range(4)]).astype(F32)  6.58 us
    ppermute x3, starting transfers between devices, on_device(): direct = [kg] + [lax.ppermute(kg, 'dp', dp_shift(dx=k)) for k in (1, 2, 3)]  5.9 us
  transfers between devices with their start and end apart: 26, of which 11 were waited for; matrix products, arithmetic and copies ran while one was open for 12% of the time, Pallas kernels for 8%

profile of v5, /device:TPU:8, one launch (start us, length us, event | category | flops | bytes accessed | tf_op | source)
XLA Modules:
  0.0 101.2 jit_solution(12305991779470473212)
XLA Ops:
  0.7 1.1 %slice_bitcast_fusion = (bf16[32,2560]{1,0:T(8,128)(2,1)S(1)}, bf16[32,2560]{1,0:T(8,128)(2,1)S(1)}) fusion(bf16[1,128,2560]{2,1,0:T(8,128)(2,1)} %param.8, bf16[1,128,2560]{2,1,0:T(8,128)(2,1)} %param.7), kind=kLoop, calls=%fused_computation.9 | loop fusion | bytes 655360 | tf_op jit(solution)/shard_map/slice | solution.py:212
  1.9 0.7 collective-permute-start
  4.0 2.5 %copy-done = bf16[2560,1024]{1,0:T(8,128)(2,1)S(1)} copy-done((bf16[2560,1024]{1,0:T(8,128)(2,1)S(1)}, bf16[2560,1024]{1,0:T(8,128)(2,1)}, u32[]{:S(2)}) %copy-start) | copy-done | bytes 5242904
  6.5 0.8 shard_map.77.own_ref
  7.4 0.9 shard_map.78
  8.2 0.6 collective-permute-start.2
  8.8 0.3 fusion
  9.1 0.1 pad_maximum_fusion.5
  9.2 1.1 %collective-permute-done.2.recv_ref = f32[128,1024]{1,0:T(8,128)S(1)} collective-permute-done((f32[128,1024]{1,0:T(8,128)S(1)}, f32[128,1024]{1,0:T(8,128)S(1)}, u32[]{:S(2)}, u32[]{:S(2)}) %collective-permute-start.2) | collective-permute-done | bytes 524320 | tf_op jit(solution)/shard_map/ppermute | solution.py:213
  10.3 0.2 shard_map.79
  10.5 4.0 %collective-permute-start.3 = (bf16[128,1024]{1,0:T(8,128)(2,1)S(1)}, bf16[128,1024]{1,0:T(8,128)(2,1)S(1)}, u32[]{:S(2)}, u32[]{:S(2)}) collective-permute-start(bf16[128,1024]{1,0:T(8,128)(2,1)S(1)} %get-tuple-element.25.kv_ref), channel_id=1, source_target_pairs={{0,2},{2,0},{4,6},{6,4},{1,3},{3,1},{5,7},{7,5},{8,10},{10,8},{12,... | collective-permute-start | bytes 786440 | tf_op jit(solution)/shard_map/ppermute | solution.py:218
  14.6 0.1 constant_dynamic-slice_fusion
  14.7 2.8 %collective-permute-start.8 = (bf16[256,640]{1,0:T(8,128)(2,1)S(1)}, bf16[256,640]{1,0:T(8,128)(2,1)S(1)}, u32[]{:S(2)}, u32[]{:S(2)}) collective-permute-start(bf16[256,640]{1,0:T(8,128)(2,1)S(1)} %pad_maximum_fusion.4), channel_id=1, source_target_pairs={{0,96},{8,104},{16,112},{24,120},{32,0},{40,8},{48,16},{56,24},{64... | collective-permute-start | bytes 983048 | tf_op jit(solution)/shard_map/ppermute | solution.py:230
  17.6 0.9 collective-permute-start.7
  18.5 1.0 collective-permute-start.6
  19.5 0.7 collective-permute-start.4
  20.2 4.2 %collective-permute-done.3.next_ref = bf16[128,1024]{1,0:T(8,128)(2,1)S(1)} collective-permute-done((bf16[128,1024]{1,0:T(8,128)(2,1)S(1)}, bf16[128,1024]{1,0:T(8,128)(2,1)S(1)}, u32[]{:S(2)}, u32[]{:S(2)}) %collective-permute-start.3) | collective-permute-done | bytes 262176 | tf_op jit(solution)/shard_map/ppermute | solution.py:218
  24.4 4.4 %shard_map.80 = (f32[128,1024]{1,0:T(8,128)S(1)}, bf16[128,1024]{1,0:T(8,128)(2,1)S(1)}, bf16[32,1024]{1,0:T(8,128)(2,1)S(1)}) custom-call(s32[3]{0:T(128)S(1)} %pad_add_fusion.1.meta, bf16[128,2560]{1,0:T(8,128)(2,1)S(1)} %bitcast.23, bf16[128,2560]{1,0:T(8,128)(2,1)S(1)} %bitcast.24, bf16[32,5120]{1,0:T(8,128)(2,1)S(1)} %collective-permute-done.tail_ref, ...), custom_call_target="tpu_custom_call" | custom-call | tf_op jit(solution)/shard_map/pallas_call | solution.py:174
  28.8 10.3 %collective-permute-start.5 = (bf16[128,1024]{1,0:T(8,128)(2,1)S(1)}, bf16[128,1024]{1,0:T(8,128)(2,1)S(1)}, u32[]{:S(2)}, u32[]{:S(2)}) collective-permute-start(bf16[128,1024]{1,0:T(8,128)(2,1)S(1)} %get-tuple-element.27), channel_id=1, source_target_pairs={{0,2},{2,0},{4,6},{6,4},{1,3},{3,1},{5,7},{7,5},{8,10},{10,8},{12,... | collective-permute-start | bytes 786440 | tf_op jit(solution)/shard_map/ppermute | solution.py:237
  39.0 0.7 collective-permute-start.9
  39.8 7.5 %collective-permute-done.5.next_ref = bf16[128,1024]{1,0:T(8,128)(2,1)S(1)} collective-permute-done((bf16[128,1024]{1,0:T(8,128)(2,1)S(1)}, bf16[128,1024]{1,0:T(8,128)(2,1)S(1)}, u32[]{:S(2)}, u32[]{:S(2)}) %collective-permute-start.5) | collective-permute-done | bytes 262176 | tf_op jit(solution)/shard_map/ppermute | solution.py:237
  47.2 0.2 shard_map.81.refs_4_
  47.4 0.1 collective-permute-start.13
  47.5 1.7 %collective-permute-start.10 = (bf16[128,1024]{1,0:T(8,128)(2,1)S(1)}, bf16[128,1024]{1,0:T(8,128)(2,1)S(1)}, u32[]{:S(2)}, u32[]{:S(2)}) collective-permute-start(bf16[128,1024]{1,0:T(8,128)(2,1)S(1)} %shard_map.81.refs_4_), channel_id=1, source_target_pairs={{0,32},{8,40},{16,48},{24,56},{32,64},{40,72},{48,80},{56,88},{64,... | collective-permute-start | bytes 786440 | tf_op jit(solution)/shard_map/ppermute | solution.py:245
  49.3 2.7 %collective-permute-start.11 = (bf16[128,1024]{1,0:T(8,128)(2,1)S(1)}, bf16[128,1024]{1,0:T(8,128)(2,1)S(1)}, u32[]{:S(2)}, u32[]{:S(2)}) collective-permute-start(bf16[128,1024]{1,0:T(8,128)(2,1)S(1)} %shard_map.81.refs_4_), channel_id=1, source_target_pairs={{0,64},{8,72},{16,80},{24,88},{32,96},{40,104},{48,112},{56,120},{... | collective-permute-start | bytes 786440 | tf_op jit(solution)/shard_map/ppermute | solution.py:245
  52.0 1.4 %collective-permute-start.12 = (bf16[128,1024]{1,0:T(8,128)(2,1)S(1)}, bf16[128,1024]{1,0:T(8,128)(2,1)S(1)}, u32[]{:S(2)}, u32[]{:S(2)}) collective-permute-start(bf16[128,1024]{1,0:T(8,128)(2,1)S(1)} %shard_map.81.refs_4_), channel_id=1, source_target_pairs={{0,96},{8,104},{16,112},{24,120},{32,0},{40,8},{48,16},{56,24},{64... | collective-permute-start | bytes 786440 | tf_op jit(solution)/shard_map/ppermute | solution.py:245
  53.4 2.7 %convolution_convert_fusion = bf16[128,2560]{1,0:T(8,128)(2,1)} fusion(bf16[128,1024]{1,0:T(8,128)(2,1)S(1)} %collective-permute-done.13.refs_8_, bf16[2560,1024]{1,0:T(8,128)(2,1)S(1)} %bitcast.19), kind=kOutput, calls=%fused_computation | convolution fusion | flops 671416320 | bytes 6160384 | tf_op jit(solution)/shard_map/dot_general | solution.py:48
  56.1 1.3 %collective-permute-done.10.refs_5_ = bf16[128,1024]{1,0:T(8,128)(2,1)S(1)} collective-permute-done((bf16[128,1024]{1,0:T(8,128)(2,1)S(1)}, bf16[128,1024]{1,0:T(8,128)(2,1)S(1)}, u32[]{:S(2)}, u32[]{:S(2)}) %collective-permute-start.10) | collective-permute-done | bytes 262176 | tf_op jit(solution)/shard_map/ppermute | solution.py:245
  57.4 6.6 %collective-permute-done.11.refs_6_ = bf16[128,1024]{1,0:T(8,128)(2,1)S(1)} collective-permute-done((bf16[128,1024]{1,0:T(8,128)(2,1)S(1)}, bf16[128,1024]{1,0:T(8,128)(2,1)S(1)}, u32[]{:S(2)}, u32[]{:S(2)}) %collective-permute-start.11) | collective-permute-done | bytes 262176 | tf_op jit(solution)/shard_map/ppermute | solution.py:245
  64.0 0.5 collective-permute-start.16
  64.6 0.9 collective-permute-done.15.refs_10_
  65.6 0.4 collective-permute-done.16.refs_11_
  65.9 2.3 %shard_map.82 = (bf16[160,1024]{1,0:T(8,128)(2,1)S(1)}, bf16[160,1024]{1,0:T(8,128)(2,1)S(1)}, bf16[160,1024]{1,0:T(8,128)(2,1)S(1)}, bf16[160,1024]{1,0:T(8,128)(2,1)S(1)}) custom-call(s32[2]{0:T(128)S(1)} %pad_add_fusion.meta, bf16[256,640]{1,0:T(8,128)(2,1)S(1)} %pad_maximum_fusion.1.refs_0_, bf16[256,640]{1,0:T(8,128)(2,1)S(1)} %collective-permute-done.6.refs_1_, ...), custom_call_target="tpu_custom_call" | custom-call | tf_op jit(solution)/shard_map/pallas_call | solution.py:174
  68.2 2.4 %collective-permute-start.17 = (bf16[160,1024]{1,0:T(8,128)(2,1)S(1)}, bf16[160,1024]{1,0:T(8,128)(2,1)S(1)}, u32[]{:S(2)}, u32[]{:S(2)}) collective-permute-start(bf16[160,1024]{1,0:T(8,128)(2,1)S(1)} %get-tuple-element.37), channel_id=1, source_target_pairs={{0,16},{1,144},{8,24},{9,152},{16,0},{17,128},{24,8},{25,136},{32,... | collective-permute-start | bytes 983048 | tf_op jit(solution)/shard_map/ppermute | solution.py:253
  70.6 0.7 collective-permute-start.19
  71.4 2.0 %collective-permute-start.21 = (bf16[160,1024]{1,0:T(8,128)(2,1)S(1)}, bf16[160,1024]{1,0:T(8,128)(2,1)S(1)}, u32[]{:S(2)}, u32[]{:S(2)}) collective-permute-start(bf16[160,1024]{1,0:T(8,128)(2,1)S(1)} %get-tuple-element.43), channel_id=1, source_target_pairs={{0,24},{1,152},{8,0},{9,128},{16,8},{17,136},{24,16},{25,144},{32,... | collective-permute-start | bytes 983048 | tf_op jit(solution)/shard_map/ppermute | solution.py:253
  73.4 4.3 %convolution_convert_fusion.1 = bf16[128,2560]{1,0:T(8,128)(2,1)S(1)} fusion(bf16[128,1024]{1,0:T(8,128)(2,1)S(1)} %shard_map.81.refs_4_, bf16[2560,1024]{1,0:T(8,128)(2,1)} %w_ref.3), kind=kOutput, calls=%fused_computation.1 | convolution fusion | flops 671416320 | bytes 6160384 | tf_op jit(solution)/shard_map/dot_general | solution.py:48
  77.7 2.8 %collective-permute-done.17.c_ref = bf16[160,1024]{1,0:T(8,128)(2,1)S(1)} collective-permute-done((bf16[160,1024]{1,0:T(8,128)(2,1)S(1)}, bf16[160,1024]{1,0:T(8,128)(2,1)S(1)}, u32[]{:S(2)}, u32[]{:S(2)}) %collective-permute-start.17) | collective-permute-done | bytes 327712 | tf_op jit(solution)/shard_map/ppermute | solution.py:253
  80.5 7.1 %collective-permute-done.20.b_ref = bf16[160,1024]{1,0:T(8,128)(2,1)S(1)} collective-permute-done((bf16[160,1024]{1,0:T(8,128)(2,1)S(1)}, bf16[160,1024]{1,0:T(8,128)(2,1)S(1)}, u32[]{:S(2)}, u32[]{:S(2)}) %collective-permute-start.20) | collective-permute-done | bytes 327712 | tf_op jit(solution)/shard_map/ppermute | solution.py:253
  87.6 0.7 shard_map.83
  88.3 0.1 collective-permute-start.22
  88.5 1.4 %collective-permute-done.22 = bf16[80,1024]{1,0:T(8,128)(2,1)S(1)} collective-permute-done((bf16[80,1024]{1,0:T(8,128)(2,1)S(1)}, bf16[80,1024]{1,0:T(8,128)(2,1)S(1)}, u32[]{:S(2)}, u32[]{:S(2)}) %collective-permute-start.22) | collective-permute-done | bytes 163872 | tf_op jit(solution)/shard_map/ppermute | solution.py:264
  89.9 0.1 collective-permute-start.23
  90.0 4.4 %collective-permute-start.24 = (bf16[80,256]{1,0:T(8,128)(2,1)S(1)}, bf16[80,256]{1,0:T(8,128)(2,1)S(1)}, u32[]{:S(2)}, u32[]{:S(2)}) collective-permute-start(bf16[80,256]{1,0:T(8,128)(2,1)S(1)} %get-tuple-element.56), channel_id=1, source_target_pairs={{0,4},{2,6},{4,0},{6,2},{1,5},{3,7},{5,1},{7,3},{8,12},{10,14},{12... | collective-permute-start | bytes 122888 | tf_op jit(solution)/shard_map/ppermute | solution.py:273
  94.4 2.1 %collective-permute-start.25 = (bf16[80,256]{1,0:T(8,128)(2,1)S(1)}, bf16[80,256]{1,0:T(8,128)(2,1)S(1)}, u32[]{:S(2)}, u32[]{:S(2)}) collective-permute-start(bf16[80,256]{1,0:T(8,128)(2,1)S(1)} %get-tuple-element.55), channel_id=1, source_target_pairs={{0,6},{2,4},{4,2},{6,0},{1,7},{3,5},{5,3},{7,1},{8,14},{10,12},{12... | collective-permute-start | bytes 122888 | tf_op jit(solution)/shard_map/ppermute | solution.py:273
  96.5 2.7 %maximum_select_fusion = bf16[1,128,5120]{2,1,0:T(8,128)(2,1)} fusion(bf16[1,128,2560]{2,1,0:T(8,128)(2,1)} %bitcast.11, bf16[1,128,2560]{2,1,0:T(8,128)(2,1)S(1)} %bitcast.25, pred[]{:T(512)S(6)} %eq.10), kind=kLoop, calls=%fused_computation.2 | loop fusion | flops 5898240 | bytes 2621441 | tf_op jit(solution)/shard_map/jit(_where)/select_n | solution.py:276
  99.2 1.4 %collective-permute-done.25 = bf16[80,256]{1,0:T(8,128)(2,1)S(1)} collective-permute-done((bf16[80,256]{1,0:T(8,128)(2,1)S(1)}, bf16[80,256]{1,0:T(8,128)(2,1)S(1)}, u32[]{:S(2)}, u32[]{:S(2)}) %collective-permute-start.25) | collective-permute-done | bytes 40992 | tf_op jit(solution)/shard_map/ppermute | solution.py:273
  100.5 0.7 add_multiply_fusion
  (44 shorter events, 0.7 us)
Async XLA Ops:
  0.6 3.3 %copy-start.1 = (bf16[1,128,5120]{2,1,0:T(8,128)(2,1)S(1)}, bf16[1,128,5120]{2,1,0:T(8,128)(2,1)}, u32[]{:S(2)}) copy-start(bf16[1,128,5120]{2,1,0:T(8,128)(2,1)} %param.6) | copy-start | bytes 3932164
  0.6 6.7 %collective-permute-start.1 = (bf16[128,5120]{1,0:T(8,128)(2,1)}, bf16[128,5120]{1,0:T(8,128)(2,1)S(1)}, u32[]{:S(2)}, u32[]{:S(2)}) collective-permute-start(bf16[128,5120]{1,0:T(8,128)(2,1)} %bitcast.20), channel_id=1, source_target_pairs={{0,1},{1,0},{2,3},{3,2},{4,5},{5,4},{6,7},{7,6},{8,9},{9,8},{10,11... | collective-permute-start | bytes 3932168 | tf_op jit(solution)/shard_map/ppermute | solution.py:206
  1.9 17.6 %collective-permute-start = (bf16[32,5120]{1,0:T(8,128)(2,1)S(1)}, bf16[32,5120]{1,0:T(8,128)(2,1)S(1)}, u32[]{:S(2)}, u32[]{:S(2)}) collective-permute-start(bf16[32,5120]{1,0:T(8,128)(2,1)S(1)} %pad_maximum_fusion), channel_id=1, source_target_pairs={{4,2},{6,6},{5,3},{7,7},{12,10},{14,14},{13,11},{15,15},{20,18},{2... | collective-permute-start | bytes 983048 | tf_op jit(solution)/shard_map/ppermute | solution.py:214
  4.0 2.5 %copy-start = (bf16[2560,1024]{1,0:T(8,128)(2,1)S(1)}, bf16[2560,1024]{1,0:T(8,128)(2,1)}, u32[]{:S(2)}) copy-start(bf16[2560,1024]{1,0:T(8,128)(2,1)} %w_ref.3) | copy-start | bytes 15728644
  7.3 46.1 %slice-start = ((s8[5242880]{0:T(1024)(128)(4,1)}), s8[1048576]{0:T(1024)(128)(4,1)S(1)}, s32[]{:S(2)}) async-start(s8[5242880]{0:T(1024)(128)(4,1)} %bitcast.18), calls=%async_computation | async-start | bytes 2097152
  8.2 2.1 %collective-permute-start.2 = (f32[128,1024]{1,0:T(8,128)S(1)}, f32[128,1024]{1,0:T(8,128)S(1)}, u32[]{:S(2)}, u32[]{:S(2)}) collective-permute-start(f32[128,1024]{1,0:T(8,128)S(1)} %shard_map.78), channel_id=1, source_target_pairs={{0,1},{1,0},{2,3},{3,2},{4,5},{5,4},{6,7},{7,6},{8,9},{9,8},{10,11... | collective-permute-start | bytes 1572872 | tf_op jit(solution)/shard_map/ppermute | solution.py:213
  10.3 43.1 %slice-start.1 = ((s8[5242880]{0:T(1024)(128)(4,1)}), s8[4194304]{0:T(1024)(128)(4,1)S(1)}, s32[]{:S(2)}) async-start(s8[5242880]{0:T(1024)(128)(4,1)} %bitcast.18), calls=%async_computation.1 | async-start | bytes 8388608
  10.5 13.9 %collective-permute-start.3 = (bf16[128,1024]{1,0:T(8,128)(2,1)S(1)}, bf16[128,1024]{1,0:T(8,128)(2,1)S(1)}, u32[]{:S(2)}, u32[]{:S(2)}) collective-permute-start(bf16[128,1024]{1,0:T(8,128)(2,1)S(1)} %get-tuple-element.25.kv_ref), channel_id=1, source_target_pairs={{0,2},{2,0},{4,6},{6,4},{1,3},{3,1},{5,7},{7,5},{8,10},{10,8},{12,... | collective-permute-start | bytes 786440 | tf_op jit(solution)/shard_map/ppermute | solution.py:218
  14.7 9.8 %copy-start.2 = (bf16[1,128,2560]{2,1,0:T(8,128)(2,1)S(1)}, bf16[1,128,2560]{2,1,0:T(8,128)(2,1)}, u32[]{:S(2)}) copy-start(bf16[1,128,2560]{2,1,0:T(8,128)(2,1)} %param.7) | copy-start | bytes 1966084
  14.7 9.7 %copy-start.3 = (bf16[1,128,2560]{2,1,0:T(8,128)(2,1)S(1)}, bf16[1,128,2560]{2,1,0:T(8,128)(2,1)}, u32[]{:S(2)}) copy-start(bf16[1,128,2560]{2,1,0:T(8,128)(2,1)} %param.8) | copy-start | bytes 1966084
  14.7 25.0 %collective-permute-start.8 = (bf16[256,640]{1,0:T(8,128)(2,1)S(1)}, bf16[256,640]{1,0:T(8,128)(2,1)S(1)}, u32[]{:S(2)}, u32[]{:S(2)}) collective-permute-start(bf16[256,640]{1,0:T(8,128)(2,1)S(1)} %pad_maximum_fusion.4), channel_id=1, source_target_pairs={{0,96},{8,104},{16,112},{24,120},{32,0},{40,8},{48,16},{56,24},{64... | collective-permute-start | bytes 983048 | tf_op jit(solution)/shard_map/ppermute | solution.py:230
  17.6 22.2 %collective-permute-start.7 = (bf16[256,640]{1,0:T(8,128)(2,1)S(1)}, bf16[256,640]{1,0:T(8,128)(2,1)S(1)}, u32[]{:S(2)}, u32[]{:S(2)}) collective-permute-start(bf16[256,640]{1,0:T(8,128)(2,1)S(1)} %pad_maximum_fusion.3), channel_id=1, source_target_pairs={{0,64},{8,72},{16,80},{24,88},{32,96},{40,104},{48,112},{56,120},{... | collective-permute-start | bytes 983048 | tf_op jit(solution)/shard_map/ppermute | solution.py:230
  18.5 21.3 %collective-permute-start.6 = (bf16[256,640]{1,0:T(8,128)(2,1)S(1)}, bf16[256,640]{1,0:T(8,128)(2,1)S(1)}, u32[]{:S(2)}, u32[]{:S(2)}) collective-permute-start(bf16[256,640]{1,0:T(8,128)(2,1)S(1)} %pad_maximum_fusion.2), channel_id=1, source_target_pairs={{0,32},{8,40},{16,48},{24,56},{32,64},{40,72},{48,80},{56,88},{64,... | collective-permute-start | bytes 983048 | tf_op jit(solution)/shard_map/ppermute | solution.py:230
  19.5 0.7 collective-permute-start.4
  28.8 18.5 %collective-permute-start.5 = (bf16[128,1024]{1,0:T(8,128)(2,1)S(1)}, bf16[128,1024]{1,0:T(8,128)(2,1)S(1)}, u32[]{:S(2)}, u32[]{:S(2)}) collective-permute-start(bf16[128,1024]{1,0:T(8,128)(2,1)S(1)} %get-tuple-element.27), channel_id=1, source_target_pairs={{0,2},{2,0},{4,6},{6,4},{1,3},{3,1},{5,7},{7,5},{8,10},{10,8},{12,... | collective-permute-start | bytes 786440 | tf_op jit(solution)/shard_map/ppermute | solution.py:237
  39.0 8.2 %collective-permute-start.9 = (bf16[32,1024]{1,0:T(8,128)(2,1)S(1)}, bf16[32,1024]{1,0:T(8,128)(2,1)S(1)}, u32[]{:S(2)}, u32[]{:S(2)}) collective-permute-start(bf16[32,1024]{1,0:T(8,128)(2,1)S(1)} %get-tuple-element.36), channel_id=1, source_target_pairs={{2,4},{3,5},{10,12},{11,13},{18,20},{19,21},{26,28},{27,29},{34,36... | collective-permute-start | bytes 196616 | tf_op jit(solution)/shard_map/ppermute | solution.py:238
  47.4 6.0 %collective-permute-start.13 = (bf16[128,1024]{1,0:T(8,128)(2,1)S(1)}, bf16[128,1024]{1,0:T(8,128)(2,1)S(1)}, u32[]{:S(2)}, u32[]{:S(2)}) collective-permute-start(bf16[128,1024]{1,0:T(8,128)(2,1)S(1)} %shard_map.81.refs_4_), channel_id=1, source_target_pairs={{0,1},{1,0},{2,3},{3,2},{4,5},{5,4},{6,7},{7,6},{8,9},{9,8},{10,11... | collective-permute-start | bytes 786440 | tf_op jit(solution)/shard_map/ppermute | solution.py:246
  47.5 9.9 %collective-permute-start.10 = (bf16[128,1024]{1,0:T(8,128)(2,1)S(1)}, bf16[128,1024]{1,0:T(8,128)(2,1)S(1)}, u32[]{:S(2)}, u32[]{:S(2)}) collective-permute-start(bf16[128,1024]{1,0:T(8,128)(2,1)S(1)} %shard_map.81.refs_4_), channel_id=1, source_target_pairs={{0,32},{8,40},{16,48},{24,56},{32,64},{40,72},{48,80},{56,88},{64,... | collective-permute-start | bytes 786440 | tf_op jit(solution)/shard_map/ppermute | solution.py:245
  49.3 14.8 %collective-permute-start.11 = (bf16[128,1024]{1,0:T(8,128)(2,1)S(1)}, bf16[128,1024]{1,0:T(8,128)(2,1)S(1)}, u32[]{:S(2)}, u32[]{:S(2)}) collective-permute-start(bf16[128,1024]{1,0:T(8,128)(2,1)S(1)} %shard_map.81.refs_4_), channel_id=1, source_target_pairs={{0,64},{8,72},{16,80},{24,88},{32,96},{40,104},{48,112},{56,120},{... | collective-permute-start | bytes 786440 | tf_op jit(solution)/shard_map/ppermute | solution.py:245
  52.0 12.0 %collective-permute-start.12 = (bf16[128,1024]{1,0:T(8,128)(2,1)S(1)}, bf16[128,1024]{1,0:T(8,128)(2,1)S(1)}, u32[]{:S(2)}, u32[]{:S(2)}) collective-permute-start(bf16[128,1024]{1,0:T(8,128)(2,1)S(1)} %shard_map.81.refs_4_), channel_id=1, source_target_pairs={{0,96},{8,104},{16,112},{24,120},{32,0},{40,8},{48,16},{56,24},{64... | collective-permute-start | bytes 786440 | tf_op jit(solution)/shard_map/ppermute | solution.py:245
  56.1 24.4 %collective-permute-start.18 = (bf16[128,2560]{1,0:T(8,128)(2,1)}, bf16[128,2560]{1,0:T(8,128)(2,1)}, u32[]{:S(2)}, u32[]{:S(2)}) collective-permute-start(bf16[128,2560]{1,0:T(8,128)(2,1)} %convolution_convert_fusion), channel_id=1, source_target_pairs={{0,1},{1,0},{2,3},{3,2},{4,5},{5,4},{6,7},{7,6},{8,9},{9,8},{10,11... | collective-permute-start | bytes 1966088 | tf_op jit(solution)/shard_map/ppermute | solution.py:258
  57.4 7.2 %collective-permute-start.14 = (bf16[128,1024]{1,0:T(8,128)(2,1)S(1)}, bf16[128,1024]{1,0:T(8,128)(2,1)S(1)}, u32[]{:S(2)}, u32[]{:S(2)}) collective-permute-start(bf16[128,1024]{1,0:T(8,128)(2,1)S(1)} %collective-permute-done.10.refs_5_), channel_id=1, source_target_pairs={{0,1},{1,0},{2,3},{3,2},{4,5},{5,4},{6,7},{7,6},{8,9},{9,8},{10,11... | collective-permute-start | bytes 786440 | tf_op jit(solution)/shard_map/ppermute | solution.py:246
  64.0 1.5 %collective-permute-start.15 = (bf16[128,1024]{1,0:T(8,128)(2,1)S(1)}, bf16[128,1024]{1,0:T(8,128)(2,1)S(1)}, u32[]{:S(2)}, u32[]{:S(2)}) collective-permute-start(bf16[128,1024]{1,0:T(8,128)(2,1)S(1)} %collective-permute-done.11.refs_6_), channel_id=1, source_target_pairs={{0,1},{1,0},{2,3},{3,2},{4,5},{5,4},{6,7},{7,6},{8,9},{9,8},{10,11... | collective-permute-start | bytes 786440 | tf_op jit(solution)/shard_map/ppermute | solution.py:246
  64.0 1.9 %collective-permute-start.16 = (bf16[128,1024]{1,0:T(8,128)(2,1)S(1)}, bf16[128,1024]{1,0:T(8,128)(2,1)S(1)}, u32[]{:S(2)}, u32[]{:S(2)}) collective-permute-start(bf16[128,1024]{1,0:T(8,128)(2,1)S(1)} %collective-permute-done.12.refs_7_), channel_id=1, source_target_pairs={{0,1},{1,0},{2,3},{3,2},{4,5},{5,4},{6,7},{7,6},{8,9},{9,8},{10,11... | collective-permute-start | bytes 786440 | tf_op jit(solution)/shard_map/ppermute | solution.py:246
  68.2 12.3 %collective-permute-start.17 = (bf16[160,1024]{1,0:T(8,128)(2,1)S(1)}, bf16[160,1024]{1,0:T(8,128)(2,1)S(1)}, u32[]{:S(2)}, u32[]{:S(2)}) collective-permute-start(bf16[160,1024]{1,0:T(8,128)(2,1)S(1)} %get-tuple-element.37), channel_id=1, source_target_pairs={{0,16},{1,144},{8,24},{9,152},{16,0},{17,128},{24,8},{25,136},{32,... | collective-permute-start | bytes 983048 | tf_op jit(solution)/shard_map/ppermute | solution.py:253
  70.6 9.9 %collective-permute-start.19 = (bf16[160,1024]{1,0:T(8,128)(2,1)S(1)}, bf16[160,1024]{1,0:T(8,128)(2,1)S(1)}, u32[]{:S(2)}, u32[]{:S(2)}) collective-permute-start(bf16[160,1024]{1,0:T(8,128)(2,1)S(1)} %get-tuple-element.40), channel_id=1, source_target_pairs={{0,0},{1,128},{8,8},{9,136},{16,16},{17,144},{24,24},{25,152},{32,... | collective-permute-start | bytes 983048 | tf_op jit(solution)/shard_map/ppermute | solution.py:253
  71.3 16.3 %collective-permute-start.20 = (bf16[160,1024]{1,0:T(8,128)(2,1)S(1)}, bf16[160,1024]{1,0:T(8,128)(2,1)S(1)}, u32[]{:S(2)}, u32[]{:S(2)}) collective-permute-start(bf16[160,1024]{1,0:T(8,128)(2,1)S(1)} %get-tuple-element.41), channel_id=1, source_target_pairs={{0,8},{1,136},{8,16},{9,144},{16,24},{17,152},{24,0},{25,128},{32,... | collective-permute-start | bytes 983048 | tf_op jit(solution)/shard_map/ppermute | solution.py:253
  71.4 16.2 %collective-permute-start.21 = (bf16[160,1024]{1,0:T(8,128)(2,1)S(1)}, bf16[160,1024]{1,0:T(8,128)(2,1)S(1)}, u32[]{:S(2)}, u32[]{:S(2)}) collective-permute-start(bf16[160,1024]{1,0:T(8,128)(2,1)S(1)} %get-tuple-element.43), channel_id=1, source_target_pairs={{0,24},{1,152},{8,0},{9,128},{16,8},{17,136},{24,16},{25,144},{32,... | collective-permute-start | bytes 983048 | tf_op jit(solution)/shard_map/ppermute | solution.py:253
  88.3 1.5 %collective-permute-start.22 = (bf16[80,1024]{1,0:T(8,128)(2,1)S(1)}, bf16[80,1024]{1,0:T(8,128)(2,1)S(1)}, u32[]{:S(2)}, u32[]{:S(2)}) collective-permute-start(bf16[80,1024]{1,0:T(8,128)(2,1)S(1)} %get-tuple-element.45), channel_id=1, source_target_pairs={{0,1},{1,0},{2,3},{3,2},{4,5},{5,4},{6,7},{7,6},{8,9},{9,8},{10,11... | collective-permute-start | bytes 491528 | tf_op jit(solution)/shard_map/ppermute | solution.py:264
  89.9 9.3 %collective-permute-start.23 = (bf16[80,256]{1,0:T(8,128)(2,1)S(1)}, bf16[80,256]{1,0:T(8,128)(2,1)S(1)}, u32[]{:S(2)}, u32[]{:S(2)}) collective-permute-start(bf16[80,256]{1,0:T(8,128)(2,1)S(1)} %get-tuple-element.54), channel_id=1, source_target_pairs={{0,2},{2,0},{4,6},{6,4},{1,3},{3,1},{5,7},{7,5},{8,10},{10,8},{12,... | collective-permute-start | bytes 122888 | tf_op jit(solution)/shard_map/ppermute | solution.py:273
  90.0 9.2 %collective-permute-start.24 = (bf16[80,256]{1,0:T(8,128)(2,1)S(1)}, bf16[80,256]{1,0:T(8,128)(2,1)S(1)}, u32[]{:S(2)}, u32[]{:S(2)}) collective-permute-start(bf16[80,256]{1,0:T(8,128)(2,1)S(1)} %get-tuple-element.56), channel_id=1, source_target_pairs={{0,4},{2,6},{4,0},{6,2},{1,5},{3,7},{5,1},{7,3},{8,12},{10,14},{12... | collective-permute-start | bytes 122888 | tf_op jit(solution)/shard_map/ppermute | solution.py:273
  94.4 6.1 %collective-permute-start.25 = (bf16[80,256]{1,0:T(8,128)(2,1)S(1)}, bf16[80,256]{1,0:T(8,128)(2,1)S(1)}, u32[]{:S(2)}, u32[]{:S(2)}) collective-permute-start(bf16[80,256]{1,0:T(8,128)(2,1)S(1)} %get-tuple-element.55), channel_id=1, source_target_pairs={{0,6},{2,4},{4,2},{6,0},{1,7},{3,5},{5,3},{7,1},{8,14},{10,12},{12... | collective-permute-start | bytes 122888 | tf_op jit(solution)/shard_map/ppermute | solution.py:273
